TPU v7x, 128 devices: a whole 4x4x4 slice. The times are simulated.
128 devices in a mesh: span: 8 (over y, x_hi), cross: 16 (over x_lo, z, core).
Axes of the slice: x: 4 (x_hi: 2, x_lo: 2; x = x_hi * 2 + x_lo), y: 4, z: 4, core: 2. Of those that a mesh axis runs over, the one named last changes fastest.
Arguments:
- adjoint_start: float32 [4, 128, 256, 1024], P(None, 'span', 'cross'), may hold values from -6 to 6
- base_flow: float32 [3, 128, 256, 1024], P(None, 'span', 'cross'), may hold values from -3 to 3
- wall_blocks: int32 [32768], P(('span', 'cross')), may hold values from 0 to 2047
- tile_sections: int32 [32768, 1], P(('span', 'cross')), may hold values from 0 to 255, as said below
- tile_normals: float32 [4, 32768], P(None, ('span', 'cross')), may hold values from -6 to 6
- modes: float32 [128, 128], replicated, may hold values from -0.5 to 0.5
Outputs:
- adjoint_field: float32 [4, 128, 256, 1024], P(None, 'span', 'cross')
- modal_load: float32 [256, 128], P(('span', 'cross'))
Inputs may be any that keep to these rules, and one draw needn't show every extreme that they name: `tile_sections`: section s is owned by the device at flat index s // 2, span major. A tile names only sections whose owner has the tile's span index or one next to it. Among the tiles of one device, no section is named more than ceil(4) times, and that many on the devices at both span ends; every section is named by some tile.
All inputs are finite; a program needn't handle non-finite values.
Results may differ from a plain program's by a relative error of at most 0.00012.
Values sent between devices are 32-bit elements; how exact they have to be, the bound alone decides.
No kernel may reach another device: no remote copies, remote signals or barrier semaphores. Data moves between devices by JAX's collectives and lax.ppermute only.
A program may use at most 128 MiB of HBM per device.

v0:
```python
import jax
import jax.numpy as jnp
from jax import lax
from jax.sharding import PartitionSpec as P

STEPS = 3
SEC_DEV = 2


time_step = 0.25
viscosity = 0.1


def with_halo(cells, sides, width):
    for axis, dim in sides:
        count = lax.axis_size(axis)
        ends = count - 1
        head = lax.slice_in_dim(cells, 0, width, axis=dim)
        tail = lax.slice_in_dim(cells, cells.shape[dim] - width, cells.shape[dim], axis=dim)
        cells = jnp.concatenate(
            [
                lax.ppermute(tail, axis, [(i, (i + 1) % count) for i in range(ends)]),
                cells,
                lax.ppermute(head, axis, [((i + 1) % count, i) for i in range(ends)]),
            ],
            axis=dim,
        )
    return cells


def passed_along(block, axis, distance):
    devices = range(lax.axis_size(axis))
    route = [(i - distance, i) for i in devices if i - distance in devices]
    return lax.ppermute(block, axis, route)


def derivs(padded):
    center = padded[:, 1:-1, 1:-1, :]
    along_z = (padded[:, 2:, 1:-1, :] - padded[:, :-2, 1:-1, :]) * 0.5
    along_y = (padded[:, 1:-1, 2:, :] - padded[:, 1:-1, :-2, :]) * 0.5
    xpad = jnp.pad(center, ((0, 0), (0, 0), (0, 0), (1, 1)))
    along_x = (xpad[..., 2:] - xpad[..., :-2]) * 0.5
    lapl = xpad[..., 2:] + xpad[..., :-2] + padded[:, 2:, 1:-1, :] + padded[:, :-2, 1:-1, :]
    lapl = lapl + padded[:, 1:-1, 2:, :] + padded[:, 1:-1, :-2, :] - 6.0 * center
    return (center, (along_x, along_y, along_z), lapl)


def advance(padded, base, grads):
    field, diffs, lapl = derivs(padded)
    result = []
    for comp in range(3):
        advect = base[0] * diffs[0][comp] + base[1] * diffs[1][comp] + base[2] * diffs[2][comp]
        coupled = grads[comp][0] * field[0] + grads[comp][1] * field[1] + grads[comp][2] * field[2]
        result.append(
            field[comp] + time_step * (advect - coupled - diffs[comp][3] + viscosity * lapl[comp])
        )
    diverg = diffs[0][0] + diffs[1][1] + diffs[2][2]
    result.append(field[3] - time_step * diverg)
    return jnp.stack(result)


def extend(field):
    return with_halo(field, (("span", 1), ("cross", 2)), 1)


def local(adjoint_start, base_flow, wall_blocks, tile_sections, tile_normals, modes):
    base_pad = with_halo(base_flow, (("span", 1), ("cross", 2)), 1)
    center, bdiff, blap = derivs(base_pad)
    grads = [[bdiff[i][j] for j in range(3)] for i in range(3)]
    field = adjoint_start
    rows_sum = jnp.zeros((wall_blocks.shape[0], 128), jnp.float32)
    for step in range(STEPS):
        field = advance(extend(field), base_flow, grads)
        shaped = field.reshape(4, -1, 128)
        rows = shaped[:, wall_blocks]
        trac = jnp.sum(tile_normals[:, :, None] * rows, axis=0)
        rows_sum = rows_sum + time_step * trac
    per_span = SEC_DEV * lax.axis_size("cross")
    first_owned = (lax.axis_index("span") - 1) * per_span
    relative = tile_sections[:, 0] - first_owned
    labels = jnp.arange(3 * per_span, dtype=jnp.int32)
    onehot = (relative[None, :] == labels[:, None]).astype(jnp.float32)
    table = jnp.dot(
        onehot, rows_sum, precision=lax.Precision.HIGHEST, preferred_element_type=jnp.float32
    )
    table = table.reshape(3, per_span, 128)
    reduced = lax.psum_scatter(table, "cross", scatter_dimension=1, tiled=True)
    from_above = passed_along(reduced[0], "span", -1)
    from_below = passed_along(reduced[2], "span", 1)
    section_sum = reduced[1] + from_above + from_below
    modal_load = jnp.dot(
        section_sum, modes, precision=lax.Precision.HIGHEST, preferred_element_type=jnp.float32
    )
    return (field, modal_load)


def solution(mesh):
    placed = (
        P(None, "span", "cross", None),
        P(None, "span", "cross", None),
        P(("span", "cross")),
        P(("span", "cross"), None),
        P(None, ("span", "cross")),
        P(),
    )
    return jax.shard_map(
        local,
        mesh=mesh,
        in_specs=placed,
        out_specs=(P(None, "span", "cross", None), P(("span", "cross"), None)),
        check_vma=False,
    )
```

profile of v0, /device:TPU:6, one launch (start us, length us, event | category | flops | bytes accessed | tf_op | source)
XLA Modules:
  0.0 393.4 jit_solution(14227085800769432490)
XLA Ops:
  5.8 4.9 %collective-permute-start.4 = (f32[3,1,16,1024]{3,2,1,0:T(8,128)}, f32[3,1,16,1024]{3,2,1,0:T(8,128)}, u32[]{:S(2)}, u32[]{:S(2)}) collective-permute-start(f32[3,1,16,1024]{3,2,1,0:T(8,128)} %get-tuple-element.36), channel_id=1, source_target_pairs={{0,16},{16,32},{32,48},{48,64},{64,80},{80,96},{96,112},{1,17},{17... | collective-permute-start | bytes 589832 | tf_op jit(solution)/shard_map/ppermute | solution.py:22
  16.0 4.6 %collective-permute-start.1 = (f32[4,1,16,1024]{3,2,1,0:T(8,128)}, f32[4,1,16,1024]{3,2,1,0:T(8,128)}, u32[]{:S(2)}, u32[]{:S(2)}) collective-permute-start(f32[4,1,16,1024]{3,2,1,0:T(8,128)} %get-tuple-element.29), channel_id=1, source_target_pairs={{16,0},{32,16},{48,32},{64,48},{80,64},{96,80},{112,96},{17,1},{33... | collective-permute-start | bytes 786440 | tf_op jit(solution)/shard_map/ppermute | solution.py:24
  26.0 4.4 %copy.43 = f32[4,16,16,1024]{3,1,2,0:T(8,128)} copy(f32[4,16,16,1024]{3,2,1,0:T(8,128)S(1)} %copy-done.37) | data formatting | bytes 8388608 | tf_op args[0]
  35.1 4.5 %collective-permute-start.6 = (f32[3,18,1,1024]{3,1,2,0:T(8,128)S(1)}, f32[3,18,1,1024]{3,1,2,0:T(8,128)S(1)}, u32[]{:S(2)}, u32[]{:S(2)}) collective-permute-start(f32[3,18,1,1024]{3,1,2,0:T(8,128)S(1)} %get-tuple-element.32), channel_id=1, source_target_pairs={{1,0},{2,1},{3,2},{4,3},{5,4},{6,5},{7,6},{8,7},{9,8},{10,9},{11,1... | collective-permute-start | bytes 663560 | tf_op jit(solution)/shard_map/ppermute | solution.py:24
  46.1 5.9 %collective-permute-start.2 = (f32[4,18,1,1024]{3,1,2,0:T(8,128)S(1)}, f32[4,18,1,1024]{3,1,2,0:T(8,128)S(1)}, u32[]{:S(2)}, u32[]{:S(2)}) collective-permute-start(f32[4,18,1,1024]{3,1,2,0:T(8,128)S(1)} %get-tuple-element.22), channel_id=1, source_target_pairs={{1,0},{2,1},{3,2},{4,3},{5,4},{6,5},{7,6},{8,7},{9,8},{10,9},{11,1... | collective-permute-start | bytes 884744 | tf_op jit(solution)/shard_map/ppermute | solution.py:24
  52.1 7.0 %fusion.5 = (f32[3,16,16,1024]{3,1,2,0:T(8,128)}, f32[3,16,16,1024]{3,1,2,0:T(8,128)}, f32[3,16,16,1024]{3,1,2,0:T(8,128)}) fusion(f32[3,18,1,1024]{3,1,2,0:T(8,128)S(1)} %collective-permute-done.7, f32[3,1,16,1024]{3,1,2,0:T(1,128)S(1)} %copy.61, f32[3,16,16,1024]{3,1,2,0:T(8,128)S(1)} %copy.44, f32[3,1,16,1024]{3,1,2,0:T(1,128)S(1)} %copy.59, ...), kind=kLoop, calls=%fused_computation.85 | loop fusion | flops 11010048 | bytes 13418496 | tf_op jit(solution)/shard_map/mul | solution.py:40
  63.4 21.4 %multiply_subtract_fusion.2 = (f32[4,16,16,1024]{3,1,2,0:T(8,128)}, f32[4,16,16,1024]{3,1,2,0:T(8,128)}, f32[4,16,16,1024]{3,1,2,0:T(8,128)}) fusion(f32[4,16,16,1024]{3,1,2,0:T(8,128)} %copy.43, f32[4,1,16,1024]{3,1,2,0:T(1,128)} %copy-done.38, f32[4,1,16,1024]{3,1,2,0:T(1,128)S(1)} %copy.47, f32[4,18,1,1024]{3,1,2,0:T(8,128)} %copy-done.40, ...), kind=kLoop, calls=%fused_computation.71 | loop fusion | flops 19922944 | bytes 17891328 | tf_op jit(solution)/shard_map/sub | solution.py:44
  84.8 6.3 %fusion.44 = f32[1,16,16,1024]{3,1,2,0:T(8,128)S(1)} fusion(f32[4,16,16,1024]{3,1,2,0:T(8,128)} %get-tuple-element.19, f32[4,16,16,1024]{3,1,2,0:T(8,128)} %get-tuple-element.20, f32[4,16,16,1024]{3,1,2,0:T(8,128)} %subtract_multiply_fusion.7, f32[4,16,16,1024]{3,1,2,0:T(8,128)} %get-tuple-element.27, f32[3,16,16,1024]{3,1,2,0:T(8,128)} %get-tuple-element.31, ...), kind=kLoop, calls=%fused_computation.155 | loop fusion | flops 4194304 | bytes 15728640 | tf_op jit(solution)/shard_map/add | solution.py:55
  97.6 4.1 %fusion.56 = (f32[1,16,16,1024]{3,1,2,0:T(8,128)S(1)}, f32[1,16,16,1024]{3,1,2,0:T(8,128)S(1)}) fusion(f32[4,16,16,1024]{3,1,2,0:T(8,128)} %get-tuple-element.19, f32[4,16,16,1024]{3,1,2,0:T(8,128)} %get-tuple-element.27, f32[4,16,16,1024]{3,1,2,0:T(8,128)S(1)} %copy-done.29, f32[4,16,16,1024]{3,1,2,0:T(8,128)S(1)} %copy-done.31, ...), kind=kLoop, calls=%fused_computation.175 | loop fusion | flops 5242880 | bytes 19922944 | tf_op jit(solution)/shard_map/add | solution.py:55
  130.1 6.1 %collective-permute-start.8 = (f32[4,1,16,1024]{3,2,1,0:T(8,128)S(1)}, f32[4,1,16,1024]{3,2,1,0:T(8,128)}, u32[]{:S(2)}, u32[]{:S(2)}) collective-permute-start(f32[4,1,16,1024]{3,2,1,0:T(8,128)S(1)} %copy.67), channel_id=1, source_target_pairs={{0,16},{16,32},{32,48},{48,64},{64,80},{80,96},{96,112},{1,17},{17... | collective-permute-start | bytes 786440 | tf_op jit(solution)/shard_map/ppermute | solution.py:22
  136.2 7.3 %pad_maximum_fusion.51 = f32[4,2048,128]{2,0,1:T(4,128)} fusion(f32[1,2048,128]{2,0,1:T(1,128)} %stack.57, f32[1,2048,128]{2,0,1:T(1,128)} %stack.56, f32[1,2048,128]{2,0,1:T(1,128)} %stack.55, f32[1,2048,128]{2,0,1:T(1,128)} %stack.54), kind=kLoop, calls=%fused_computation.60 | loop fusion | flops 3145728 | bytes 8388608 | tf_op jit(solution)/shard_map/stack | solution.py:59
  143.5 3.9 %gather_fusion = f32[256,4,128]{2,1,0:T(4,128)} fusion(f32[4,2048,128]{2,0,1:T(4,128)} %pad_maximum_fusion.51, s32[1024]{0:T(1024)S(1)} %pad_clamp_fusion), kind=kCustom, calls=%fused_computation | custom fusion | bytes 1049600 | tf_op jit(solution)/shard_map/gather | solution.py:75
  147.4 7.8 %subtract_multiply_fusion.5 = f32[4,16,16,1024]{3,1,2,0:T(8,128)} fusion(f32[4,16,16,1024]{3,1,2,0:T(8,128)} %pad_maximum_fusion.48), kind=kLoop, calls=%fused_computation.70 | loop fusion | flops 2097152 | bytes 8388608 | tf_op jit(solution)/shard_map/mul | solution.py:42
  159.8 5.8 %collective-permute-start.10 = (f32[4,18,1,1024]{3,1,2,0:T(8,128)S(1)}, f32[4,18,1,1024]{3,1,2,0:T(8,128)S(1)}, u32[]{:S(2)}, u32[]{:S(2)}) collective-permute-start(f32[4,18,1,1024]{3,1,2,0:T(8,128)S(1)} %get-tuple-element.18), channel_id=1, source_target_pairs={{1,0},{2,1},{3,2},{4,3},{5,4},{6,5},{7,6},{8,7},{9,8},{10,9},{11,1... | collective-permute-start | bytes 884744 | tf_op jit(solution)/shard_map/ppermute | solution.py:24
  172.5 8.4 %multiply_subtract_fusion.1 = f32[4,16,16,1024]{3,1,2,0:T(8,128)} fusion(f32[4,16,16,1024]{3,1,2,0:T(8,128)S(1)} %copy-done.27, f32[4,1,16,1024]{3,1,2,0:T(1,128)S(1)} %copy.70, f32[1,16,16,1024]{3,1,2,0:T(8,128)S(1)} %copy-done.18, f32[1,16,16,1024]{3,1,2,0:T(8,128)S(1)} %copy-done.12, f32[1,16,16,1024]{3,1,2,0:T(8,128)S(1)} %copy-done.14, ...), kind=kLoop, calls=%fused_computation.67 | loop fusion | flops 28311552 | bytes 13697024 | tf_op jit(solution)/shard_map/sub | solution.py:44
  181.0 4.1 %fusion.26 = f32[1,16,16,1024]{3,1,2,0:T(8,128)S(1)} fusion(f32[1,16,16,1024]{3,1,2,0:T(8,128)S(1)} %copy-done.12, f32[4,16,16,1024]{3,1,2,0:T(8,128)} %multiply_subtract_fusion.1, f32[4,16,16,1024]{3,1,2,0:T(8,128)} %subtract_multiply_fusion.3, f32[4,16,16,1024]{3,1,2,0:T(8,128)S(1)} %subtract_multiply_fusion.4, ...), kind=kLoop, calls=%fused_computation.124 | loop fusion | flops 4194304 | bytes 15728640 | tf_op jit(solution)/shard_map/add | solution.py:55
  185.2 4.7 %fusion.32 = f32[1,16,16,1024]{3,1,2,0:T(8,128)S(1)} fusion(f32[1,16,16,1024]{3,1,2,0:T(8,128)S(1)} %copy-done.14, f32[4,16,16,1024]{3,1,2,0:T(8,128)} %multiply_subtract_fusion.1, f32[4,16,16,1024]{3,1,2,0:T(8,128)} %copy-done.30, f32[4,16,16,1024]{3,1,2,0:T(8,128)} %subtract_multiply_fusion.3, f32[4,16,16,1024]{3,1,2,0:T(8,128)} %subtract_multiply_fusion.5, ...), kind=kLoop, calls=%fused_computation.134 | loop fusion | flops 4194304 | bytes 15728640 | tf_op jit(solution)/shard_map/add | solution.py:55
  189.9 5.7 %fusion.38 = (f32[1,16,16,1024]{3,1,2,0:T(8,128)S(1)}, f32[1,16,16,1024]{3,1,2,0:T(8,128)S(1)}) fusion(f32[1,16,16,1024]{3,1,2,0:T(8,128)S(1)} %copy-done.6, f32[4,16,16,1024]{3,1,2,0:T(8,128)} %multiply_subtract_fusion.1, f32[4,16,16,1024]{3,1,2,0:T(8,128)} %subtract_multiply_fusion.5, f32[4,16,16,1024]{3,1,2,0:T(8,128)} %subtract_multiply_fusion.3, ...), kind=kLoop, calls=%fused_computation.144 | loop fusion | flops 5242880 | bytes 19922944 | tf_op jit(solution)/shard_map/add | solution.py:55
  224.5 6.3 %collective-permute-start.12 = (f32[4,1,16,1024]{3,2,1,0:T(8,128)S(1)}, f32[4,1,16,1024]{3,2,1,0:T(8,128)}, u32[]{:S(2)}, u32[]{:S(2)}) collective-permute-start(f32[4,1,16,1024]{3,2,1,0:T(8,128)S(1)} %copy.73), channel_id=1, source_target_pairs={{0,16},{16,32},{32,48},{48,64},{64,80},{80,96},{96,112},{1,17},{17... | collective-permute-start | bytes 786440 | tf_op jit(solution)/shard_map/ppermute | solution.py:22
  230.8 6.9 %pad_maximum_fusion.52 = f32[4,2048,128]{2,0,1:T(4,128)} fusion(f32[1,2048,128]{2,0,1:T(1,128)} %stack.62, f32[1,2048,128]{2,0,1:T(1,128)} %stack.61, f32[1,2048,128]{2,0,1:T(1,128)} %stack.60, f32[1,2048,128]{2,0,1:T(1,128)} %stack.59), kind=kLoop, calls=%fused_computation.61 | loop fusion | flops 3145728 | bytes 8388608 | tf_op jit(solution)/shard_map/stack | solution.py:59
  237.7 4.0 %gather_fusion.1 = f32[256,4,128]{2,1,0:T(4,128)} fusion(f32[4,2048,128]{2,0,1:T(4,128)} %pad_maximum_fusion.52, s32[1024]{0:T(1024)S(1)} %pad_clamp_fusion), kind=kCustom, calls=%fused_computation.1 | custom fusion | bytes 1049600 | tf_op jit(solution)/shard_map/gather | solution.py:75
  241.7 7.8 %subtract_multiply_fusion.2 = f32[4,16,16,1024]{3,1,2,0:T(8,128)} fusion(f32[4,16,16,1024]{3,1,2,0:T(8,128)} %pad_maximum_fusion.49), kind=kLoop, calls=%fused_computation.66 | loop fusion | flops 2097152 | bytes 8388608 | tf_op jit(solution)/shard_map/mul | solution.py:42
  254.1 5.8 %collective-permute-start.14 = (f32[4,18,1,1024]{3,1,2,0:T(8,128)S(1)}, f32[4,18,1,1024]{3,1,2,0:T(8,128)S(1)}, u32[]{:S(2)}, u32[]{:S(2)}) collective-permute-start(f32[4,18,1,1024]{3,1,2,0:T(8,128)S(1)} %get-tuple-element.16), channel_id=1, source_target_pairs={{1,0},{2,1},{3,2},{4,3},{5,4},{6,5},{7,6},{8,7},{9,8},{10,9},{11,1... | collective-permute-start | bytes 884744 | tf_op jit(solution)/shard_map/ppermute | solution.py:24
  266.8 8.4 %multiply_subtract_fusion = f32[4,16,16,1024]{3,1,2,0:T(8,128)} fusion(f32[4,16,16,1024]{3,1,2,0:T(8,128)S(1)} %copy-done.28, f32[4,1,16,1024]{3,1,2,0:T(1,128)S(1)} %copy.76, f32[1,16,16,1024]{3,1,2,0:T(8,128)S(1)} %copy-done.16, f32[1,16,16,1024]{3,1,2,0:T(8,128)S(1)} %copy-done.8, f32[1,16,16,1024]{3,1,2,0:T(8,128)S(1)} %copy-done.10, ...), kind=kLoop, calls=%fused_computation.63 | loop fusion | flops 28311552 | bytes 13697024 | tf_op jit(solution)/shard_map/sub | solution.py:44
  275.3 5.1 %fusion.8 = f32[1,16,16,1024]{3,1,2,0:T(8,128)} fusion(f32[1,16,16,1024]{3,1,2,0:T(8,128)S(1)} %copy-done.8, f32[4,16,16,1024]{3,1,2,0:T(8,128)} %multiply_subtract_fusion, f32[4,16,16,1024]{3,1,2,0:T(8,128)} %subtract_multiply_fusion, f32[4,16,16,1024]{3,1,2,0:T(8,128)S(1)} %subtract_multiply_fusion.1, f32[4,16,16,1024]{3,1,2,0:T(8,128)} %subtract_multiply_fusion.2, ...), kind=kLoop, calls=%fused_computation.94 | loop fusion | flops 4194304 | bytes 15728640 | tf_op jit(solution)/shard_map/add | solution.py:55
  280.4 4.8 %fusion.14 = f32[1,16,16,1024]{3,1,2,0:T(8,128)} fusion(f32[1,16,16,1024]{3,1,2,0:T(8,128)S(1)} %copy-done.10, f32[4,16,16,1024]{3,1,2,0:T(8,128)} %multiply_subtract_fusion, f32[4,16,16,1024]{3,1,2,0:T(8,128)S(1)} %subtract_multiply_fusion.1, f32[4,16,16,1024]{3,1,2,0:T(8,128)} %subtract_multiply_fusion, f32[4,16,16,1024]{3,1,2,0:T(8,128)} %subtract_multiply_fusion.2, ...), kind=kLoop, calls=%fused_computation.104 | loop fusion | flops 4194304 | bytes 15728640 | tf_op jit(solution)/shard_map/add | solution.py:55
  285.2 5.7 %fusion.20 = (f32[1,16,16,1024]{3,1,2,0:T(8,128)S(1)}, f32[1,16,16,1024]{3,1,2,0:T(8,128)}) fusion(f32[1,16,16,1024]{3,1,2,0:T(8,128)S(1)} %copy-done.4, f32[4,16,16,1024]{3,1,2,0:T(8,128)} %multiply_subtract_fusion, f32[4,16,16,1024]{3,1,2,0:T(8,128)} %subtract_multiply_fusion.2, f32[4,16,16,1024]{3,1,2,0:T(8,128)} %subtract_multiply_fusion, ...), kind=kLoop, calls=%fused_computation.114 | loop fusion | flops 5242880 | bytes 19922944 | tf_op jit(solution)/shard_map/add | solution.py:55
  307.9 6.9 %pad_maximum_fusion.53 = f32[4,2048,128]{2,0,1:T(4,128)} fusion(f32[1,2048,128]{2,0,1:T(1,128)} %stack.67, f32[1,2048,128]{2,0,1:T(1,128)} %stack.66, f32[1,2048,128]{2,0,1:T(1,128)} %stack.65, f32[1,2048,128]{2,0,1:T(1,128)} %stack.64), kind=kLoop, calls=%fused_computation.62 | loop fusion | flops 3145728 | bytes 8388608 | tf_op jit(solution)/shard_map/stack | solution.py:59
  314.8 4.0 %gather_fusion.2 = f32[256,4,128]{2,1,0:T(4,128)} fusion(f32[4,2048,128]{2,0,1:T(4,128)} %pad_maximum_fusion.53, s32[1024]{0:T(1024)S(1)} %pad_clamp_fusion), kind=kCustom, calls=%fused_computation.2 | custom fusion | bytes 1049600 | tf_op jit(solution)/shard_map/gather | solution.py:75
  321.4 56.8 %all-reduce.4 = f32[3,32,128]{2,1,0:T(8,128)S(1)} all-reduce(f32[3,32,128]{2,1,0:T(8,128)S(1)} %bitcast.53), channel_id=2, replica_groups=mesh['span'=8,'cross'=16] {'cross'}, use_global_device_ids=true, to_apply=%region_3.4.clone | all-reduce | flops 12288 | bytes 98304
  380.5 6.0 %collective-permute-start.17 = (f32[2,128]{1,0:T(2,128)S(1)}, f32[2,128]{1,0:T(2,128)S(1)}, u32[]{:S(2)}, u32[]{:S(2)}) collective-permute-start(f32[2,128]{1,0:T(2,128)S(1)} %get-tuple-element.38), channel_id=1, source_target_pairs={{0,16},{16,32},{32,48},{48,64},{64,80},{80,96},{96,112},{1,17},{17... | collective-permute-start | bytes 3080 | tf_op jit(solution)/shard_map/ppermute | solution.py:34
  388.0 4.4 %copy.92 = f32[4,16,16,1024]{3,2,1,0:T(8,128)} copy(f32[4,16,16,1024]{3,1,2,0:T(8,128)S(1)} %pad_maximum_fusion.50) | data formatting | bytes 8388608
  (178 shorter events, 141.2 us)
Async XLA Ops:
  0.6 391.8 %copy-start = (f32[128,128]{1,0:T(8,128)S(1)}, f32[128,128]{1,0:T(8,128)}, u32[]{:S(2)}) copy-start(f32[128,128]{1,0:T(8,128)} %param.11) | copy-start | bytes 196612
  2.5 30.0 %collective-permute-start.5 = (f32[3,1,16,1024]{3,2,1,0:T(8,128)}, f32[3,1,16,1024]{3,2,1,0:T(8,128)}, u32[]{:S(2)}, u32[]{:S(2)}) collective-permute-start(f32[3,1,16,1024]{3,2,1,0:T(8,128)} %get-tuple-element.35), channel_id=1, source_target_pairs={{16,0},{32,16},{48,32},{64,48},{80,64},{96,80},{112,96},{17,1},{33... | collective-permute-start | bytes 589832 | tf_op jit(solution)/shard_map/ppermute | solution.py:24
  5.8 28.0 %collective-permute-start.4 = (f32[3,1,16,1024]{3,2,1,0:T(8,128)}, f32[3,1,16,1024]{3,2,1,0:T(8,128)}, u32[]{:S(2)}, u32[]{:S(2)}) collective-permute-start(f32[3,1,16,1024]{3,2,1,0:T(8,128)} %get-tuple-element.36), channel_id=1, source_target_pairs={{0,16},{16,32},{32,48},{48,64},{64,80},{80,96},{96,112},{1,17},{17... | collective-permute-start | bytes 589832 | tf_op jit(solution)/shard_map/ppermute | solution.py:22
  12.5 29.0 %collective-permute-start = (f32[4,1,16,1024]{3,2,1,0:T(8,128)S(1)}, f32[4,1,16,1024]{3,2,1,0:T(8,128)}, u32[]{:S(2)}, u32[]{:S(2)}) collective-permute-start(f32[4,1,16,1024]{3,2,1,0:T(8,128)S(1)} %get-tuple-element.28), channel_id=1, source_target_pairs={{0,16},{16,32},{32,48},{48,64},{64,80},{80,96},{96,112},{1,17},{17... | collective-permute-start | bytes 786440 | tf_op jit(solution)/shard_map/ppermute | solution.py:22
  16.0 26.9 %collective-permute-start.1 = (f32[4,1,16,1024]{3,2,1,0:T(8,128)}, f32[4,1,16,1024]{3,2,1,0:T(8,128)}, u32[]{:S(2)}, u32[]{:S(2)}) collective-permute-start(f32[4,1,16,1024]{3,2,1,0:T(8,128)} %get-tuple-element.29), channel_id=1, source_target_pairs={{16,0},{32,16},{48,32},{64,48},{80,64},{96,80},{112,96},{17,1},{33... | collective-permute-start | bytes 786440 | tf_op jit(solution)/shard_map/ppermute | solution.py:24
  32.5 11.5 %copy-start.1 = (f32[4,16,16,1024]{3,1,2,0:T(8,128)S(1)}, f32[4,16,16,1024]{3,1,2,0:T(8,128)}, u32[]{:S(2)}) copy-start(f32[4,16,16,1024]{3,1,2,0:T(8,128)} %copy.43) | copy-start | bytes 12582916
  35.1 17.0 %collective-permute-start.6 = (f32[3,18,1,1024]{3,1,2,0:T(8,128)S(1)}, f32[3,18,1,1024]{3,1,2,0:T(8,128)S(1)}, u32[]{:S(2)}, u32[]{:S(2)}) collective-permute-start(f32[3,18,1,1024]{3,1,2,0:T(8,128)S(1)} %get-tuple-element.32), channel_id=1, source_target_pairs={{1,0},{2,1},{3,2},{4,3},{5,4},{6,5},{7,6},{8,7},{9,8},{10,9},{11,1... | collective-permute-start | bytes 663560 | tf_op jit(solution)/shard_map/ppermute | solution.py:24
  39.6 12.4 %collective-permute-start.7 = (f32[3,18,1,1024]{3,1,2,0:T(8,128)S(1)}, f32[3,18,1,1024]{3,1,2,0:T(8,128)S(1)}, u32[]{:S(2)}, u32[]{:S(2)}) collective-permute-start(f32[3,18,1,1024]{3,1,2,0:T(8,128)S(1)} %get-tuple-element.33), channel_id=1, source_target_pairs={{0,1},{1,2},{2,3},{3,4},{4,5},{5,6},{6,7},{7,8},{8,9},{9,10},{10,1... | collective-permute-start | bytes 663560 | tf_op jit(solution)/shard_map/ppermute | solution.py:22
  44.0 15.1 %copy-start.38 = (f32[4,1,16,1024]{3,1,2,0:T(1,128)}, f32[4,1,16,1024]{3,1,2,0:T(1,128)S(1)}, u32[]{:S(2)}) copy-start(f32[4,1,16,1024]{3,1,2,0:T(1,128)S(1)} %copy.49) | copy-start | bytes 786436
  44.2 14.9 %collective-permute-start.3 = (f32[4,18,1,1024]{3,1,2,0:T(8,128)S(1)}, f32[4,18,1,1024]{3,1,2,0:T(8,128)S(1)}, u32[]{:S(2)}, u32[]{:S(2)}) collective-permute-start(f32[4,18,1,1024]{3,1,2,0:T(8,128)S(1)} %get-tuple-element.21), channel_id=1, source_target_pairs={{0,1},{1,2},{2,3},{3,4},{4,5},{5,6},{6,7},{7,8},{8,9},{9,10},{10,1... | collective-permute-start | bytes 884744 | tf_op jit(solution)/shard_map/ppermute | solution.py:22
  46.1 13.0 %collective-permute-start.2 = (f32[4,18,1,1024]{3,1,2,0:T(8,128)S(1)}, f32[4,18,1,1024]{3,1,2,0:T(8,128)S(1)}, u32[]{:S(2)}, u32[]{:S(2)}) collective-permute-start(f32[4,18,1,1024]{3,1,2,0:T(8,128)S(1)} %get-tuple-element.22), channel_id=1, source_target_pairs={{1,0},{2,1},{3,2},{4,3},{5,4},{6,5},{7,6},{8,7},{9,8},{10,9},{11,1... | collective-permute-start | bytes 884744 | tf_op jit(solution)/shard_map/ppermute | solution.py:24
  91.1 17.0 %copy-start.11 = (f32[1,16,16,1024]{3,1,2,0:T(8,128)}, f32[1,16,16,1024]{3,1,2,0:T(8,128)S(1)}, u32[]{:S(2)}) copy-start(f32[1,16,16,1024]{3,1,2,0:T(8,128)S(1)} %fusion.44) | copy-start | bytes 3145732
  97.6 10.6 %copy-start.13 = (f32[1,16,16,1024]{3,1,2,0:T(8,128)}, f32[1,16,16,1024]{3,1,2,0:T(8,128)S(1)}, u32[]{:S(2)}) copy-start(f32[1,16,16,1024]{3,1,2,0:T(8,128)S(1)} %fusion.50) | copy-start | bytes 3145732
  127.9 27.3 %collective-permute-start.9 = (f32[4,1,16,1024]{3,2,1,0:T(8,128)}, f32[4,1,16,1024]{3,2,1,0:T(8,128)}, u32[]{:S(2)}, u32[]{:S(2)}) collective-permute-start(f32[4,1,16,1024]{3,2,1,0:T(8,128)} %copy.68), channel_id=1, source_target_pairs={{16,0},{32,16},{48,32},{64,48},{80,64},{96,80},{112,96},{17,1},{33... | collective-permute-start | bytes 786440 | tf_op jit(solution)/shard_map/ppermute | solution.py:24
  130.1 26.4 %collective-permute-start.8 = (f32[4,1,16,1024]{3,2,1,0:T(8,128)S(1)}, f32[4,1,16,1024]{3,2,1,0:T(8,128)}, u32[]{:S(2)}, u32[]{:S(2)}) collective-permute-start(f32[4,1,16,1024]{3,2,1,0:T(8,128)S(1)} %copy.67), channel_id=1, source_target_pairs={{0,16},{16,32},{32,48},{48,64},{64,80},{80,96},{96,112},{1,17},{17... | collective-permute-start | bytes 786440 | tf_op jit(solution)/shard_map/ppermute | solution.py:22
  147.4 10.3 %copy-start.12 = (f32[1,16,16,1024]{3,1,2,0:T(8,128)S(1)}, f32[1,16,16,1024]{3,1,2,0:T(8,128)}, u32[]{:S(2)}) copy-start(f32[1,16,16,1024]{3,1,2,0:T(8,128)} %copy-done.11) | copy-start | bytes 3145732
  147.4 10.3 %copy-start.14 = (f32[1,16,16,1024]{3,1,2,0:T(8,128)S(1)}, f32[1,16,16,1024]{3,1,2,0:T(8,128)}, u32[]{:S(2)}) copy-start(f32[1,16,16,1024]{3,1,2,0:T(8,128)} %copy-done.13) | copy-start | bytes 3145732
  147.4 10.3 %copy-start.18 = (f32[1,16,16,1024]{3,1,2,0:T(8,128)S(1)}, f32[1,16,16,1024]{3,1,2,0:T(8,128)}, u32[]{:S(2)}) copy-start(f32[1,16,16,1024]{3,1,2,0:T(8,128)} %copy-done.17) | copy-start | bytes 3145732
  157.9 11.2 %collective-permute-start.11 = (f32[4,18,1,1024]{3,1,2,0:T(8,128)S(1)}, f32[4,18,1,1024]{3,1,2,0:T(8,128)S(1)}, u32[]{:S(2)}, u32[]{:S(2)}) collective-permute-start(f32[4,18,1,1024]{3,1,2,0:T(8,128)S(1)} %get-tuple-element.17), channel_id=1, source_target_pairs={{0,1},{1,2},{2,3},{3,4},{4,5},{5,6},{6,7},{7,8},{8,9},{9,10},{10,1... | collective-permute-start | bytes 884744 | tf_op jit(solution)/shard_map/ppermute | solution.py:22
  159.8 11.0 %collective-permute-start.10 = (f32[4,18,1,1024]{3,1,2,0:T(8,128)S(1)}, f32[4,18,1,1024]{3,1,2,0:T(8,128)S(1)}, u32[]{:S(2)}, u32[]{:S(2)}) collective-permute-start(f32[4,18,1,1024]{3,1,2,0:T(8,128)S(1)} %get-tuple-element.18), channel_id=1, source_target_pairs={{1,0},{2,1},{3,2},{4,3},{5,4},{6,5},{7,6},{8,7},{9,8},{10,9},{11,1... | collective-permute-start | bytes 884744 | tf_op jit(solution)/shard_map/ppermute | solution.py:24
  185.2 17.0 %copy-start.7 = (f32[1,16,16,1024]{3,1,2,0:T(8,128)}, f32[1,16,16,1024]{3,1,2,0:T(8,128)S(1)}, u32[]{:S(2)}) copy-start(f32[1,16,16,1024]{3,1,2,0:T(8,128)S(1)} %fusion.26) | copy-start | bytes 3145732
  189.9 12.2 %copy-start.9 = (f32[1,16,16,1024]{3,1,2,0:T(8,128)}, f32[1,16,16,1024]{3,1,2,0:T(8,128)S(1)}, u32[]{:S(2)}) copy-start(f32[1,16,16,1024]{3,1,2,0:T(8,128)S(1)} %fusion.32) | copy-start | bytes 3145732
  222.6 26.9 %collective-permute-start.13 = (f32[4,1,16,1024]{3,2,1,0:T(8,128)}, f32[4,1,16,1024]{3,2,1,0:T(8,128)}, u32[]{:S(2)}, u32[]{:S(2)}) collective-permute-start(f32[4,1,16,1024]{3,2,1,0:T(8,128)} %copy.74), channel_id=1, source_target_pairs={{16,0},{32,16},{48,32},{64,48},{80,64},{96,80},{112,96},{17,1},{33... | collective-permute-start | bytes 786440 | tf_op jit(solution)/shard_map/ppermute | solution.py:24
  224.5 26.2 %collective-permute-start.12 = (f32[4,1,16,1024]{3,2,1,0:T(8,128)S(1)}, f32[4,1,16,1024]{3,2,1,0:T(8,128)}, u32[]{:S(2)}, u32[]{:S(2)}) collective-permute-start(f32[4,1,16,1024]{3,2,1,0:T(8,128)S(1)} %copy.73), channel_id=1, source_target_pairs={{0,16},{16,32},{32,48},{48,64},{64,80},{80,96},{96,112},{1,17},{17... | collective-permute-start | bytes 786440 | tf_op jit(solution)/shard_map/ppermute | solution.py:22
  241.7 10.3 %copy-start.10 = (f32[1,16,16,1024]{3,1,2,0:T(8,128)S(1)}, f32[1,16,16,1024]{3,1,2,0:T(8,128)}, u32[]{:S(2)}) copy-start(f32[1,16,16,1024]{3,1,2,0:T(8,128)} %copy-done.9) | copy-start | bytes 3145732
  241.7 10.3 %copy-start.16 = (f32[1,16,16,1024]{3,1,2,0:T(8,128)S(1)}, f32[1,16,16,1024]{3,1,2,0:T(8,128)}, u32[]{:S(2)}) copy-start(f32[1,16,16,1024]{3,1,2,0:T(8,128)} %copy-done.15) | copy-start | bytes 3145732
  252.1 11.2 %collective-permute-start.15 = (f32[4,18,1,1024]{3,1,2,0:T(8,128)S(1)}, f32[4,18,1,1024]{3,1,2,0:T(8,128)S(1)}, u32[]{:S(2)}, u32[]{:S(2)}) collective-permute-start(f32[4,18,1,1024]{3,1,2,0:T(8,128)S(1)} %get-tuple-element.15), channel_id=1, source_target_pairs={{0,1},{1,2},{2,3},{3,4},{4,5},{5,6},{6,7},{7,8},{8,9},{9,10},{10,1... | collective-permute-start | bytes 884744 | tf_op jit(solution)/shard_map/ppermute | solution.py:22
  254.1 11.0 %collective-permute-start.14 = (f32[4,18,1,1024]{3,1,2,0:T(8,128)S(1)}, f32[4,18,1,1024]{3,1,2,0:T(8,128)S(1)}, u32[]{:S(2)}, u32[]{:S(2)}) collective-permute-start(f32[4,18,1,1024]{3,1,2,0:T(8,128)S(1)} %get-tuple-element.16), channel_id=1, source_target_pairs={{1,0},{2,1},{3,2},{4,3},{5,4},{6,5},{7,6},{8,7},{9,8},{10,9},{11,1... | collective-permute-start | bytes 884744 | tf_op jit(solution)/shard_map/ppermute | solution.py:24
  307.9 10.9 %copy-start.41 = (f32[4,256]{0,1:T(8,128)S(1)}, f32[4,256]{0,1:T(8,128)}, u32[]{:S(2)}) copy-start(f32[4,256]{0,1:T(8,128)} %copy.79) | copy-start | bytes 12292
  307.9 78.6 %copy-start.33 = (f32[1,16,16,1024]{3,1,2,0:T(8,128)S(1)}, f32[1,16,16,1024]{3,1,2,0:T(8,128)}, u32[]{:S(2)}) copy-start(f32[1,16,16,1024]{3,1,2,0:T(8,128)} %copy-done.32) | copy-start | bytes 3145732
  378.2 14.3 %collective-permute-start.16 = (f32[2,128]{1,0:T(2,128)S(1)}, f32[2,128]{1,0:T(2,128)S(1)}, u32[]{:S(2)}, u32[]{:S(2)}) collective-permute-start(f32[2,128]{1,0:T(2,128)S(1)} %get-tuple-element.37), channel_id=1, source_target_pairs={{16,0},{32,16},{48,32},{64,48},{80,64},{96,80},{112,96},{17,1},{33... | collective-permute-start | bytes 3080 | tf_op jit(solution)/shard_map/ppermute | solution.py:34
  380.5 12.0 %collective-permute-start.17 = (f32[2,128]{1,0:T(2,128)S(1)}, f32[2,128]{1,0:T(2,128)S(1)}, u32[]{:S(2)}, u32[]{:S(2)}) collective-permute-start(f32[2,128]{1,0:T(2,128)S(1)} %get-tuple-element.38), channel_id=1, source_target_pairs={{0,16},{16,32},{32,48},{48,64},{64,80},{80,96},{96,112},{1,17},{17... | collective-permute-start | bytes 3080 | tf_op jit(solution)/shard_map/ppermute | solution.py:34
  (30 other events, 181.3 us)
where the time goes:
time: 400 us; the launch traced here: 393 us
  other arithmetic  149 us (37%)
  local copies, waits for them, and re-layouts  109 us (27%)
  starting transfers between devices  70.6 us (18%)
  blocking collectives  56.8 us (14%)
  waiting for transfers between devices  4.12 us (1%)
    unnamed x1, blocking collectives  56.8 us
    add x9, other arithmetic, advance(): field[comp]  44 us
    another operation x12, local copies, waits for them, and re-layouts, advance(): return jnp.stack(result)  39.8 us
    sub x3, other arithmetic, derivs(): lapl + padded[:, 1:-1, 2:, :] + padded[:, 1:-1, :-2, :] - 6.0 * center  38.2 us
    ppermute x8, starting transfers between devices, with_halo(): lax.ppermute(head, axis, [((i + 1) % count, i) for i in range(ends)])  34 us
    ppermute x8, starting transfers between devices, with_halo(): lax.ppermute(tail, axis, [(i, (i + 1) % count) for i in range(ends)])  28.4 us
    another operation x6, other arithmetic, advance(): return jnp.stack(result)  27.5 us
    unnamed x93, local copies, waits for them, and re-layouts  19.8 us
  transfers between devices with their start and end apart: 18, of which 4 were waited for; matrix products, arithmetic and copies ran while one was open for 20% of the time, Pallas kernels for 0%

commit v1 on v0

v1 whole, which is shorter than its diff:
```python
import functools

import jax
import jax.numpy as jnp
from jax import lax
from jax.experimental import pallas as pl
from jax.experimental.pallas import tpu as pltpu
from jax.sharding import PartitionSpec as P

STEPS = 3
SEC_DEV = 2
TIME_STEP = 0.25
VISCOSITY = 0.1
LANES = 128
ROWS = 8
HALF = 0.5 * TIME_STEP
DIFF = TIME_STEP * VISCOSITY
KEEP = 1.0 - 6.0 * DIFF

VMEM = pltpu.VMEM
SMEM = pltpu.SMEM


def lane_shifts(get, k, last, lane):
    here = get(k)
    plus = pltpu.roll(here, LANES - 1, 1)
    minus = pltpu.roll(here, 1, 1)
    next_one = pltpu.roll(get(k + 1), LANES - 1, 1) if k < last else 0.0
    prev_one = pltpu.roll(get(k - 1), 1, 1) if k > 0 else 0.0
    return jnp.where(lane == LANES - 1, next_one, plus), jnp.where(lane == 0, prev_one, minus)


def row_shifts(tiles, yt, halo_lo, halo_hi, sub):
    here = tiles[yt]
    plus = pltpu.roll(here, ROWS - 1, 0)
    minus = pltpu.roll(here, 1, 0)
    if yt + 1 < len(tiles):
        over = pltpu.roll(tiles[yt + 1], ROWS - 1, 0)
    else:
        over = jnp.broadcast_to(halo_hi, here.shape)
    if yt > 0:
        under = pltpu.roll(tiles[yt - 1], 1, 0)
    else:
        under = jnp.broadcast_to(halo_lo, here.shape)
    return jnp.where(sub == ROWS - 1, over, plus), jnp.where(sub == 0, under, minus)


def plane(field, field_lo, field_hi, base, base_lo, base_hi, y_lo, y_hi, put, ny, nx):
    lane = lax.broadcasted_iota(jnp.int32, (ROWS, LANES), 1)
    sub = lax.broadcasted_iota(jnp.int32, (ROWS, LANES), 0)
    last = nx // LANES - 1
    tiles = ny // ROWS
    for k in range(nx // LANES):
        for yt in range(tiles):
            def around(get, off, c):
                xs = lane_shifts(lambda kk: get(c, yt, kk), k, last, lane)
                ys = row_shifts([get(c, j, k) for j in range(tiles)], yt, y_lo(off + c, k), y_hi(off + c, k), sub)
                return xs, ys
            f = [field(c, yt, k) for c in range(4)]
            u = [base(c, yt, k) for c in range(3)]
            fs, us = [], []
            for c in range(4):
                xs, ys = around(field, 0, c)
                fs.append((xs, ys, (field_hi(c, yt, k), field_lo(c, yt, k))))
            for c in range(3):
                xs, ys = around(base, 4, c)
                us.append((xs, ys, (base_hi(c, yt, k), base_lo(c, yt, k))))
            scaled = [HALF * u[d] for d in range(3)]
            up = [scaled[d] + DIFF for d in range(3)]
            down = [DIFF - scaled[d] for d in range(3)]
            out = []
            for i in range(3):
                acc = KEEP * f[i]
                for d in range(3):
                    acc = acc + up[d] * fs[i][d][0] + down[d] * fs[i][d][1]
                pull = fs[3][i][0] - fs[3][i][1]
                for j in range(3):
                    pull = pull + (us[j][i][0] - us[j][i][1]) * f[j]
                out.append(acc - HALF * pull)
            div = fs[0][0][0] - fs[0][0][1]
            for d in (1, 2):
                div = div + (fs[d][d][0] - fs[d][d][1])
            out.append(f[3] - HALF * div)
            for c in range(4):
                put(c, yt, k, out[c])


def tile_of(ref, index):
    def get(c, yt, k):
        return ref[(c, *index, pl.ds(yt * ROWS, ROWS), pl.ds(k * LANES, LANES))]
    return get


def pack_kernel(field, base, z_lo, z_hi, y_lo, y_hi, sems):
    nz, ny, nx = field.shape[1:]
    copies = []
    for src, lo, hi in ((field, 0, 4), (base, 4, 7)):
        copies += [(src.at[:, 0], z_lo.at[lo:hi]), (src.at[:, nz - 1], z_hi.at[lo:hi])]
        for k in range(nx // LANES):
            col = pl.ds(k * LANES, LANES)
            copies += [
                (src.at[:, :, 0, col], y_lo.at[lo:hi, :, k]),
                (src.at[:, :, ny - 1, col], y_hi.at[lo:hi, :, k]),
            ]
    started = [pltpu.make_async_copy(a, b, sems.at[i]) for i, (a, b) in enumerate(copies)]
    for one in started:
        one.start()
    for one in started:
        one.wait()


def pack(field, base):
    _, nz, ny, nx = field.shape
    per_row = nx // LANES
    shapes = [(7, ny, nx), (7, ny, nx), (7, nz, per_row, LANES), (7, nz, per_row, LANES)]
    return pl.pallas_call(
        pack_kernel,
        out_shape=[jax.ShapeDtypeStruct(s, jnp.float32) for s in shapes],
        in_specs=[pl.BlockSpec(memory_space=pl.ANY)] * 2,
        out_specs=[pl.BlockSpec(memory_space=pl.ANY)] * 4,
        scratch_shapes=[pltpu.SemaphoreType.DMA((4 + 4 * per_row,))],
        name="pack_faces",
    )(field, base)


def step_kernel(first, field, base, zf_lo, zf_hi, yf_lo, yf_hi, zb_lo, zb_hi, yb_lo, yb_hi, blocks, normals, rows_in,
                new, z_lo, z_hi, y_lo, y_hi, rows):
    _, nz, ny, nx = field.shape
    boff = zb_lo.shape[0] - 3

    def do(z, f_lo, f_hi, b_lo, b_hi):
        def halo(fref, bref):
            def get(c, k):
                if c < 4:
                    return fref[c, z, pl.ds(k, 1), :]
                return bref[boff + c - 4, z, pl.ds(k, 1), :]
            return get

        def put(c, yt, k, value):
            col = pl.ds(k * LANES, LANES)
            new[c, z, pl.ds(yt * ROWS, ROWS), col] = value
            if yt == 0:
                y_lo[c, z, pl.ds(k, 1), :] = value[:1]
            if yt == ny // ROWS - 1:
                y_hi[c, z, pl.ds(k, 1), :] = value[ROWS - 1:]

        plane(tile_of(field, (z,)), f_lo, f_hi, tile_of(base, (z,)), b_lo, b_hi, halo(yf_lo, yb_lo), halo(yf_hi, yb_hi), put, ny, nx)

    def shifted(ref, off):
        inner = tile_of(ref, ())
        return lambda c, yt, k: inner(c + off, yt, k)

    do(0, shifted(zf_lo, 0), tile_of(field, (1,)), shifted(zb_lo, boff), tile_of(base, (1,)))

    def body(z, carry):
        do(z, tile_of(field, (z - 1,)), tile_of(field, (z + 1,)), tile_of(base, (z - 1,)), tile_of(base, (z + 1,)))
        return carry

    lax.fori_loop(1, nz - 1, body, 0)
    do(nz - 1, tile_of(field, (nz - 2,)), shifted(zf_hi, 0), tile_of(base, (nz - 2,)), shifted(zb_hi, boff))
    z_lo[...] = new[:, 0]
    z_hi[...] = new[:, nz - 1]

    per_row = nx // LANES

    row_bits, y_bits = per_row.bit_length() - 1, ny.bit_length() - 1
    sub = lax.broadcasted_iota(jnp.int32, (ROWS, LANES), 0)

    def gather(group, carry):
        kept = jnp.zeros((ROWS, LANES), jnp.float32)
        for j in range(ROWS):
            t = group * ROWS + j
            b = blocks[t]
            z = lax.shift_right_logical(b, row_bits + y_bits)
            y = lax.shift_right_logical(b, row_bits) & (ny - 1)
            near = pl.ds(pl.multiple_of(y & (ny - ROWS), ROWS), ROWS)
            col = pl.ds(pl.multiple_of((b & (per_row - 1)) * LANES, LANES), LANES)
            total = normals[0, t] * new[0, z, near, col]
            for c in range(1, 4):
                total = total + normals[c, t] * new[c, z, near, col]
            total = pltpu.roll(total, (j + ROWS - (y & (ROWS - 1))) & (ROWS - 1), 0)
            kept = jnp.where(sub == j, total, kept)
        kept = TIME_STEP * kept
        here = pl.ds(pl.multiple_of(group * ROWS, ROWS), ROWS)
        if not first:
            kept = kept + rows_in[here, :]
        rows[here, :] = kept
        return carry

    lax.fori_loop(0, rows.shape[0] // ROWS, gather, 0)


def advance(first, field, base, halos, base_halos, blocks, normals, rows):
    _, nz, ny, nx = field.shape
    per_row = nx // LANES
    shapes = [field.shape, (4, ny, nx), (4, ny, nx), (4, nz, per_row, LANES), (4, nz, per_row, LANES), rows.shape]
    vm = pl.BlockSpec(memory_space=VMEM)
    sm = pl.BlockSpec(memory_space=SMEM)
    return pl.pallas_call(
        functools.partial(step_kernel, first),
        out_shape=[jax.ShapeDtypeStruct(s, jnp.float32) for s in shapes],
        in_specs=[vm] * 10 + [sm, sm, vm],
        out_specs=[vm] * 6,
        compiler_params=pltpu.CompilerParams(vmem_limit_bytes=48 * 2**20),
        name="adjoint_step",
    )(field, base, *halos, *base_halos, blocks, normals, rows)


def shift_along(block, axis, distance):
    count = lax.axis_size(axis)
    route = [(i, i + distance) for i in range(count) if 0 <= i + distance < count]
    return lax.ppermute(block, axis, route)


def exchange(z_lo, z_hi, y_lo, y_hi):
    return (shift_along(z_hi, "span", 1), shift_along(z_lo, "span", -1),
            shift_along(y_hi, "cross", 1), shift_along(y_lo, "cross", -1))


def local(adjoint_start, base_flow, wall_blocks, tile_sections, tile_normals, modes):
    halos = exchange(*pack(adjoint_start, base_flow))
    base_halos = halos
    field = adjoint_start
    rows = jnp.zeros((wall_blocks.shape[0], LANES), jnp.float32)
    for step in range(STEPS):
        field, *faces, rows = advance(step == 0, field, base_flow, halos, base_halos, wall_blocks, tile_normals, rows)
        if step < STEPS - 1:
            halos = exchange(*faces)
    crosses = lax.axis_size("cross")
    per_span = SEC_DEV * crosses
    relative = tile_sections[:, 0] - (lax.axis_index("span") - 1) * per_span
    span_off, inside = relative // per_span, relative % per_span
    spot = (inside // SEC_DEV) * (3 * SEC_DEV) + span_off * SEC_DEV + inside % SEC_DEV
    labels = jnp.arange(3 * per_span, dtype=jnp.int32)
    onehot = (spot[None, :] == labels[:, None]).astype(jnp.float32)
    table = jnp.dot(onehot, rows, precision=lax.Precision.HIGHEST, preferred_element_type=jnp.float32)
    parts = lax.all_to_all(table.reshape(crosses, 3 * SEC_DEV, LANES), "cross", 0, 0, tiled=True)
    reduced = jnp.sum(parts, axis=0)
    above = shift_along(reduced[:SEC_DEV], "span", -1)
    below = shift_along(reduced[2 * SEC_DEV:], "span", 1)
    section_sum = reduced[SEC_DEV:2 * SEC_DEV] + above + below
    modal_load = jnp.dot(section_sum, modes, precision=lax.Precision.HIGHEST, preferred_element_type=jnp.float32)
    return field, modal_load


def solution(mesh):
    placed = (
        P(None, "span", "cross", None),
        P(None, "span", "cross", None),
        P(("span", "cross")),
        P(("span", "cross"), None),
        P(None, ("span", "cross")),
        P(),
    )
    return jax.shard_map(
        local,
        mesh=mesh,
        in_specs=placed,
        out_specs=(P(None, "span", "cross", None), P(("span", "cross"), None)),
        check_vma=False,
    )
```

time: 400 us -> 208 us (0.52)
  the two profiles are of different devices: /device:TPU:6 before, /device:TPU:1 now
where the time goes in v1:
time: 208 us; the launch traced here: 205 us
  Pallas kernels  107 us (51%)
  starting transfers between devices  44.4 us (21%)
  waiting for transfers between devices  32.9 us (16%)
  blocking collectives  19.4 us (9%)
    pallas_call x1, Pallas kernels, pack(): pl.pallas_call(pack_kernel, out_shape=[jax.ShapeDtypeStruct(s, jnp.float3...  57 us
    pallas_call x3, Pallas kernels, advance(): pl.pallas_call(functools.partial(step_kernel, first), out_shape=[jax.Shap...  49.8 us
    ppermute x14, starting transfers between devices, shift_along(): return lax.ppermute(block, axis, route)  44.4 us
    ppermute x14, waiting for transfers between devices, shift_along(): return lax.ppermute(block, axis, route)  32.9 us
    all_to_all x1, blocking collectives, local(): lax.all_to_all(table.reshape(crosses, 3 * SEC_DEV, LANES), 'cross', 0, 0,...  19.4 us
  transfers between devices with their start and end apart: 14, of which 7 were waited for; matrix products, arithmetic and copies ran while one was open for 0% of the time, Pallas kernels for 0%

profile of v1, /device:TPU:1, one launch (start us, length us, event | category | flops | bytes accessed | tf_op | source)
XLA Modules:
  0.0 205.3 jit_solution(1377693741305961945)
XLA Ops:
  0.6 0.0 copy-start
  0.7 57.0 %pack_faces.1 = (f32[7,16,1024]{2,1,0:T(8,128)}, f32[7,16,1024]{2,1,0:T(8,128)}, f32[7,16,8,128]{3,2,1,0:T(8,128)}, f32[7,16,8,128]{3,2,1,0:T(8,128)}) custom-call(f32[4,16,16,1024]{3,2,1,0:T(8,128)} %field.3, f32[3,16,16,1024]{3,2,1,0:T(8,128)} %base.7), custom_call_target="tpu_custom_call" | custom-call | tf_op jit(solution)/shard_map/pack_faces/pallas_call | solution.py:116
  57.7 5.5 %collective-permute-start = (f32[7,16,1024]{2,1,0:T(8,128)}, f32[7,16,1024]{2,1,0:T(8,128)S(1)}, u32[]{:S(2)}, u32[]{:S(2)}) collective-permute-start(f32[7,16,1024]{2,1,0:T(8,128)} %get-tuple-element.20), channel_id=1, source_target_pairs={{0,16},{16,32},{32,48},{48,64},{64,80},{80,96},{96,112},{1,17},{17... | collective-permute-start | bytes 1376264 | tf_op jit(solution)/shard_map/ppermute | solution.py:212
  63.2 1.3 collective-permute-start.1
  64.5 4.4 %collective-permute-start.2 = (f32[7,16,8,128]{3,2,1,0:T(8,128)}, f32[7,16,8,128]{3,2,1,0:T(8,128)S(1)}, u32[]{:S(2)}, u32[]{:S(2)}) collective-permute-start(f32[7,16,8,128]{3,2,1,0:T(8,128)} %get-tuple-element.22), channel_id=1, source_target_pairs={{0,1},{1,2},{2,3},{3,4},{4,5},{5,6},{6,7},{7,8},{8,9},{9,10},{10,1... | collective-permute-start | bytes 1376264 | tf_op jit(solution)/shard_map/ppermute | solution.py:212
  68.9 1.9 collective-permute-start.3
  70.8 1.8 collective-permute-done.zf_lo.zb_lo
  72.7 11.7 %collective-permute-done.1.zf_hi.zb_hi = f32[7,16,1024]{2,1,0:T(8,128)S(1)} collective-permute-done((f32[7,16,1024]{2,1,0:T(8,128)}, f32[7,16,1024]{2,1,0:T(8,128)S(1)}, u32[]{:S(2)}, u32[]{:S(2)}) %collective-permute-start.1) | collective-permute-done | bytes 458784 | tf_op jit(solution)/shard_map/ppermute | solution.py:212
  84.4 0.0 collective-permute-done.2.yf_lo.yb_lo
  84.4 0.0 collective-permute-done.3.yf_hi.yb_hi
  84.4 16.7 %adjoint_step.3 = (f32[4,16,16,1024]{3,2,1,0:T(8,128)}, f32[4,16,1024]{2,1,0:T(8,128)}, f32[4,16,1024]{2,1,0:T(8,128)}, f32[4,16,8,128]{3,2,1,0:T(8,128)S(1)}, f...) custom-call(f32[4,16,16,1024]{3,2,1,0:T(8,128)} %field.3, f32[3,16,16,1024]{3,2,1,0:T(8,128)} %base.7, ...), custom_call_target="tpu_custom_call" | custom-call | tf_op jit(solution)/shard_map/adjoint_step/pallas_call | solution.py:199
  101.1 4.7 %collective-permute-start.4 = (f32[4,16,1024]{2,1,0:T(8,128)}, f32[4,16,1024]{2,1,0:T(8,128)S(1)}, u32[]{:S(2)}, u32[]{:S(2)}) collective-permute-start(f32[4,16,1024]{2,1,0:T(8,128)} %get-tuple-element.25), channel_id=1, source_target_pairs={{0,16},{16,32},{32,48},{48,64},{64,80},{80,96},{96,112},{1,17},{17... | collective-permute-start | bytes 786440 | tf_op jit(solution)/shard_map/ppermute | solution.py:212
  105.7 1.3 collective-permute-start.5
  107.0 5.3 %collective-permute-start.6 = (f32[4,16,8,128]{3,2,1,0:T(8,128)}, f32[4,16,8,128]{3,2,1,0:T(8,128)S(1)}, u32[]{:S(2)}, u32[]{:S(2)}) collective-permute-start(f32[4,16,8,128]{3,2,1,0:T(8,128)} %get-tuple-element.27), channel_id=1, source_target_pairs={{0,1},{1,2},{2,3},{3,4},{4,5},{5,6},{6,7},{7,8},{8,9},{9,10},{10,1... | collective-permute-start | bytes 786440 | tf_op jit(solution)/shard_map/ppermute | solution.py:212
  112.3 1.9 collective-permute-start.7
  114.2 0.0 collective-permute-done.4.zf_lo
  114.2 3.5 %collective-permute-done.5.zf_hi = f32[4,16,1024]{2,1,0:T(8,128)S(1)} collective-permute-done((f32[4,16,1024]{2,1,0:T(8,128)}, f32[4,16,1024]{2,1,0:T(8,128)S(1)}, u32[]{:S(2)}, u32[]{:S(2)}) %collective-permute-start.5) | collective-permute-done | bytes 262176 | tf_op jit(solution)/shard_map/ppermute | solution.py:212
  117.7 2.3 %collective-permute-done.7.yf_hi = f32[4,16,8,128]{3,2,1,0:T(8,128)S(1)} collective-permute-done((f32[4,16,8,128]{3,2,1,0:T(8,128)S(1)}, f32[4,16,8,128]{3,2,1,0:T(8,128)S(1)}, u32[]{:S(2)}, u32[]{:S(2)}) %collective-permute-start.7) | collective-permute-done | bytes 262176 | tf_op jit(solution)/shard_map/ppermute | solution.py:212
  120.0 16.4 %adjoint_step.4 = (f32[4,16,16,1024]{3,2,1,0:T(8,128)}, f32[4,16,1024]{2,1,0:T(8,128)S(1)}, f32[4,16,1024]{2,1,0:T(8,128)S(1)}, f32[4,16,8,128]{3,2,1,0:T(8,128)...) custom-call(f32[4,16,16,1024]{3,2,1,0:T(8,128)} %get-tuple-element.24.field, f32[3,16,16,1024]{3,2,1,0:T(8,128)} %base.7, ...), custom_call_target="tpu_custom_call" | custom-call | tf_op jit(solution)/shard_map/adjoint_step/pallas_call | solution.py:199
  136.3 3.5 %collective-permute-start.10 = (f32[4,16,8,128]{3,2,1,0:T(8,128)S(1)}, f32[4,16,8,128]{3,2,1,0:T(8,128)S(1)}, u32[]{:S(2)}, u32[]{:S(2)}) collective-permute-start(f32[4,16,8,128]{3,2,1,0:T(8,128)S(1)} %get-tuple-element.33), channel_id=1, source_target_pairs={{0,1},{1,2},{2,3},{3,4},{4,5},{5,6},{6,7},{7,8},{8,9},{9,10},{10,1... | collective-permute-start | bytes 786440 | tf_op jit(solution)/shard_map/ppermute | solution.py:212
  139.8 1.9 collective-permute-start.11
  141.7 4.7 %collective-permute-start.8 = (f32[4,16,1024]{2,1,0:T(8,128)S(1)}, f32[4,16,1024]{2,1,0:T(8,128)S(1)}, u32[]{:S(2)}, u32[]{:S(2)}) collective-permute-start(f32[4,16,1024]{2,1,0:T(8,128)S(1)} %get-tuple-element.31), channel_id=1, source_target_pairs={{0,16},{16,32},{32,48},{48,64},{64,80},{80,96},{96,112},{1,17},{17... | collective-permute-start | bytes 786440 | tf_op jit(solution)/shard_map/ppermute | solution.py:212
  146.5 1.3 collective-permute-start.9
  147.8 4.6 %collective-permute-done.8.zf_lo = f32[4,16,1024]{2,1,0:T(8,128)S(1)} collective-permute-done((f32[4,16,1024]{2,1,0:T(8,128)S(1)}, f32[4,16,1024]{2,1,0:T(8,128)S(1)}, u32[]{:S(2)}, u32[]{:S(2)}) %collective-permute-start.8) | collective-permute-done | bytes 262176 | tf_op jit(solution)/shard_map/ppermute | solution.py:212
  152.5 8.2 %collective-permute-done.9.zf_hi = f32[4,16,1024]{2,1,0:T(8,128)S(1)} collective-permute-done((f32[4,16,1024]{2,1,0:T(8,128)S(1)}, f32[4,16,1024]{2,1,0:T(8,128)S(1)}, u32[]{:S(2)}, u32[]{:S(2)}) %collective-permute-start.9) | collective-permute-done | bytes 262176 | tf_op jit(solution)/shard_map/ppermute | solution.py:212
  160.7 16.7 %adjoint_step.5 = (f32[4,16,16,1024]{3,2,1,0:T(8,128)}, f32[4,16,1024]{2,1,0:T(8,128)}, f32[4,16,1024]{2,1,0:T(8,128)}, f32[4,16,8,128]{3,2,1,0:T(8,128)}, f32[4...) custom-call(f32[4,16,16,1024]{3,2,1,0:T(8,128)} %get-tuple-element.30.field, f32[3,16,16,1024]{3,2,1,0:T(8,128)} %base.7, ...), custom_call_target="tpu_custom_call" | custom-call | tf_op jit(solution)/shard_map/adjoint_step/pallas_call | solution.py:199
  177.5 0.2 fusion
  177.7 19.4 %all_to_all.5 = f32[16,6,128]{2,1,0:T(8,128)S(1)} all-to-all(f32[16,6,128]{2,1,0:T(8,128)S(1)} %reshape.70), channel_id=1, replica_groups=mesh['span'=8,'cross'=16] {'cross'}, dimensions={0} | all-to-all | bytes 98304 | tf_op jit(solution)/shard_map/all_to_all | solution.py:237
  197.1 1.3 collective-permute-start.12
  198.4 5.5 %collective-permute-start.13 = (f32[2,128]{1,0:T(2,128)S(1)}, f32[2,128]{1,0:T(2,128)S(1)}, u32[]{:S(2)}, u32[]{:S(2)}) collective-permute-start(f32[2,128]{1,0:T(2,128)S(1)} %get-tuple-element.39), channel_id=1, source_target_pairs={{0,16},{16,32},{32,48},{48,64},{64,80},{80,96},{96,112},{1,17},{17... | collective-permute-start | bytes 3080 | tf_op jit(solution)/shard_map/ppermute | solution.py:212
  203.9 0.7 collective-permute-done.13
  204.6 0.7 fusion.3
  (17 shorter events, 0.1 us)
Async XLA Ops:
  0.6 204.0 %copy-start = (f32[128,128]{1,0:T(8,128)S(1)}, f32[128,128]{1,0:T(8,128)}, u32[]{:S(2)}) copy-start(f32[128,128]{1,0:T(8,128)} %param.11) | copy-start | bytes 196612
  0.6 83.7 %copy-start.1 = (f32[4,256]{1,0:T(4,128)S(1)}, f32[4,256]{1,0:T(4,128)}, u32[]{:S(2)}) copy-start(f32[4,256]{1,0:T(4,128)} %normals.5) | copy-start | bytes 12292
  0.7 83.7 %copy-start.2 = (s32[256]{0:T(256)S(1)}, s32[256]{0:T(256)}, u32[]{:S(2)}) copy-start(s32[256]{0:T(256)} %blocks.5) | copy-start | bytes 3076
  57.7 15.0 %collective-permute-start = (f32[7,16,1024]{2,1,0:T(8,128)}, f32[7,16,1024]{2,1,0:T(8,128)S(1)}, u32[]{:S(2)}, u32[]{:S(2)}) collective-permute-start(f32[7,16,1024]{2,1,0:T(8,128)} %get-tuple-element.20), channel_id=1, source_target_pairs={{0,16},{16,32},{32,48},{48,64},{64,80},{80,96},{96,112},{1,17},{17... | collective-permute-start | bytes 1376264 | tf_op jit(solution)/shard_map/ppermute | solution.py:212
  63.2 21.2 %collective-permute-start.1 = (f32[7,16,1024]{2,1,0:T(8,128)}, f32[7,16,1024]{2,1,0:T(8,128)S(1)}, u32[]{:S(2)}, u32[]{:S(2)}) collective-permute-start(f32[7,16,1024]{2,1,0:T(8,128)} %get-tuple-element.21), channel_id=1, source_target_pairs={{16,0},{32,16},{48,32},{64,48},{80,64},{96,80},{112,96},{17,1},{33... | collective-permute-start | bytes 1376264 | tf_op jit(solution)/shard_map/ppermute | solution.py:212
  64.5 19.9 %collective-permute-start.2 = (f32[7,16,8,128]{3,2,1,0:T(8,128)}, f32[7,16,8,128]{3,2,1,0:T(8,128)S(1)}, u32[]{:S(2)}, u32[]{:S(2)}) collective-permute-start(f32[7,16,8,128]{3,2,1,0:T(8,128)} %get-tuple-element.22), channel_id=1, source_target_pairs={{0,1},{1,2},{2,3},{3,4},{4,5},{5,6},{6,7},{7,8},{8,9},{9,10},{10,1... | collective-permute-start | bytes 1376264 | tf_op jit(solution)/shard_map/ppermute | solution.py:212
  68.9 15.5 %collective-permute-start.3 = (f32[7,16,8,128]{3,2,1,0:T(8,128)}, f32[7,16,8,128]{3,2,1,0:T(8,128)S(1)}, u32[]{:S(2)}, u32[]{:S(2)}) collective-permute-start(f32[7,16,8,128]{3,2,1,0:T(8,128)} %get-tuple-element.23), channel_id=1, source_target_pairs={{1,0},{2,1},{3,2},{4,3},{5,4},{6,5},{7,6},{8,7},{9,8},{10,9},{11,1... | collective-permute-start | bytes 1376264 | tf_op jit(solution)/shard_map/ppermute | solution.py:212
  101.1 13.2 %collective-permute-start.4 = (f32[4,16,1024]{2,1,0:T(8,128)}, f32[4,16,1024]{2,1,0:T(8,128)S(1)}, u32[]{:S(2)}, u32[]{:S(2)}) collective-permute-start(f32[4,16,1024]{2,1,0:T(8,128)} %get-tuple-element.25), channel_id=1, source_target_pairs={{0,16},{16,32},{32,48},{48,64},{64,80},{80,96},{96,112},{1,17},{17... | collective-permute-start | bytes 786440 | tf_op jit(solution)/shard_map/ppermute | solution.py:212
  105.7 12.0 %collective-permute-start.5 = (f32[4,16,1024]{2,1,0:T(8,128)}, f32[4,16,1024]{2,1,0:T(8,128)S(1)}, u32[]{:S(2)}, u32[]{:S(2)}) collective-permute-start(f32[4,16,1024]{2,1,0:T(8,128)} %get-tuple-element.26), channel_id=1, source_target_pairs={{16,0},{32,16},{48,32},{64,48},{80,64},{96,80},{112,96},{17,1},{33... | collective-permute-start | bytes 786440 | tf_op jit(solution)/shard_map/ppermute | solution.py:212
  107.0 10.7 %collective-permute-start.6 = (f32[4,16,8,128]{3,2,1,0:T(8,128)}, f32[4,16,8,128]{3,2,1,0:T(8,128)S(1)}, u32[]{:S(2)}, u32[]{:S(2)}) collective-permute-start(f32[4,16,8,128]{3,2,1,0:T(8,128)} %get-tuple-element.27), channel_id=1, source_target_pairs={{0,1},{1,2},{2,3},{3,4},{4,5},{5,6},{6,7},{7,8},{8,9},{9,10},{10,1... | collective-permute-start | bytes 786440 | tf_op jit(solution)/shard_map/ppermute | solution.py:212
  112.3 7.7 %collective-permute-start.7 = (f32[4,16,8,128]{3,2,1,0:T(8,128)S(1)}, f32[4,16,8,128]{3,2,1,0:T(8,128)S(1)}, u32[]{:S(2)}, u32[]{:S(2)}) collective-permute-start(f32[4,16,8,128]{3,2,1,0:T(8,128)S(1)} %get-tuple-element.28), channel_id=1, source_target_pairs={{1,0},{2,1},{3,2},{4,3},{5,4},{6,5},{7,6},{8,7},{9,8},{10,9},{11,1... | collective-permute-start | bytes 786440 | tf_op jit(solution)/shard_map/ppermute | solution.py:212
  120.0 27.8 %copy-start.3 = (s32[256,1]{0,1:T(1,128)S(1)}, s32[256,1]{0,1:T(1,128)}, u32[]{:S(2)}) copy-start(s32[256,1]{0,1:T(1,128)} %param.9) | copy-start | bytes 3076
  136.3 11.5 %collective-permute-start.10 = (f32[4,16,8,128]{3,2,1,0:T(8,128)S(1)}, f32[4,16,8,128]{3,2,1,0:T(8,128)S(1)}, u32[]{:S(2)}, u32[]{:S(2)}) collective-permute-start(f32[4,16,8,128]{3,2,1,0:T(8,128)S(1)} %get-tuple-element.33), channel_id=1, source_target_pairs={{0,1},{1,2},{2,3},{3,4},{4,5},{5,6},{6,7},{7,8},{8,9},{9,10},{10,1... | collective-permute-start | bytes 786440 | tf_op jit(solution)/shard_map/ppermute | solution.py:212
  139.8 8.0 %collective-permute-start.11 = (f32[4,16,8,128]{3,2,1,0:T(8,128)S(1)}, f32[4,16,8,128]{3,2,1,0:T(8,128)S(1)}, u32[]{:S(2)}, u32[]{:S(2)}) collective-permute-start(f32[4,16,8,128]{3,2,1,0:T(8,128)S(1)} %get-tuple-element.34), channel_id=1, source_target_pairs={{1,0},{2,1},{3,2},{4,3},{5,4},{6,5},{7,6},{8,7},{9,8},{10,9},{11,1... | collective-permute-start | bytes 786440 | tf_op jit(solution)/shard_map/ppermute | solution.py:212
  141.7 10.7 %collective-permute-start.8 = (f32[4,16,1024]{2,1,0:T(8,128)S(1)}, f32[4,16,1024]{2,1,0:T(8,128)S(1)}, u32[]{:S(2)}, u32[]{:S(2)}) collective-permute-start(f32[4,16,1024]{2,1,0:T(8,128)S(1)} %get-tuple-element.31), channel_id=1, source_target_pairs={{0,16},{16,32},{32,48},{48,64},{64,80},{80,96},{96,112},{1,17},{17... | collective-permute-start | bytes 786440 | tf_op jit(solution)/shard_map/ppermute | solution.py:212
  146.5 14.3 %collective-permute-start.9 = (f32[4,16,1024]{2,1,0:T(8,128)S(1)}, f32[4,16,1024]{2,1,0:T(8,128)S(1)}, u32[]{:S(2)}, u32[]{:S(2)}) collective-permute-start(f32[4,16,1024]{2,1,0:T(8,128)S(1)} %get-tuple-element.32), channel_id=1, source_target_pairs={{16,0},{32,16},{48,32},{64,48},{80,64},{96,80},{112,96},{17,1},{33... | collective-permute-start | bytes 786440 | tf_op jit(solution)/shard_map/ppermute | solution.py:212
  197.1 6.8 %collective-permute-start.12 = (f32[2,128]{1,0:T(2,128)S(1)}, f32[2,128]{1,0:T(2,128)S(1)}, u32[]{:S(2)}, u32[]{:S(2)}) collective-permute-start(f32[2,128]{1,0:T(2,128)S(1)} %get-tuple-element.38), channel_id=1, source_target_pairs={{16,0},{32,16},{48,32},{64,48},{80,64},{96,80},{112,96},{17,1},{33... | collective-permute-start | bytes 3080 | tf_op jit(solution)/shard_map/ppermute | solution.py:212
  198.4 6.2 %collective-permute-start.13 = (f32[2,128]{1,0:T(2,128)S(1)}, f32[2,128]{1,0:T(2,128)S(1)}, u32[]{:S(2)}, u32[]{:S(2)}) collective-permute-start(f32[2,128]{1,0:T(2,128)S(1)} %get-tuple-element.39), channel_id=1, source_target_pairs={{0,16},{16,32},{32,48},{48,64},{64,80},{80,96},{96,112},{1,17},{17... | collective-permute-start | bytes 3080 | tf_op jit(solution)/shard_map/ppermute | solution.py:212

commit v2 on v1

v2 whole, which is shorter than its diff:
```python
import functools

import jax
import jax.numpy as jnp
from jax import lax
from jax.experimental import pallas as pl
from jax.experimental.pallas import tpu as pltpu
from jax.sharding import PartitionSpec as P

STEPS = 3
SEC_DEV = 2
TIME_STEP = 0.25
VISCOSITY = 0.1
LANES = 128
ROWS = 8
HALF = 0.5 * TIME_STEP
DIFF = TIME_STEP * VISCOSITY
KEEP = 1.0 - 6.0 * DIFF

VMEM = pltpu.VMEM
SMEM = pltpu.SMEM


def lane_shifts(get, k, last, lane):
    here = get(k)
    plus = pltpu.roll(here, LANES - 1, 1)
    minus = pltpu.roll(here, 1, 1)
    next_one = pltpu.roll(get(k + 1), LANES - 1, 1) if k < last else 0.0
    prev_one = pltpu.roll(get(k - 1), 1, 1) if k > 0 else 0.0
    return jnp.where(lane == LANES - 1, next_one, plus), jnp.where(lane == 0, prev_one, minus)


def row_shifts(tiles, yt, sub):
    here = tiles[yt]
    plus = pltpu.roll(here, ROWS - 1, 0)
    minus = pltpu.roll(here, 1, 0)
    over = pltpu.roll(tiles[yt + 1], ROWS - 1, 0) if yt + 1 < len(tiles) else 0.0
    under = pltpu.roll(tiles[yt - 1], 1, 0) if yt > 0 else 0.0
    return jnp.where(sub == ROWS - 1, over, plus), jnp.where(sub == 0, under, minus)


def plane(field, field_lo, field_hi, base, base_lo, base_hi, put, ny, nx):
    lane = lax.broadcasted_iota(jnp.int32, (ROWS, LANES), 1)
    sub = lax.broadcasted_iota(jnp.int32, (ROWS, LANES), 0)
    last = nx // LANES - 1
    tiles = ny // ROWS
    for k in range(nx // LANES):
        for yt in range(tiles):
            def around(get, get_lo, get_hi, c):
                xs = lane_shifts(lambda kk: get(c, yt, kk), k, last, lane)
                ys = row_shifts([get(c, j, k) for j in range(tiles)], yt, sub)
                return xs, ys, (get_hi(c, yt, k), get_lo(c, yt, k))
            f = [field(c, yt, k) for c in range(4)]
            u = [base(c, yt, k) for c in range(3)]
            fs = [around(field, field_lo, field_hi, c) for c in range(4)]
            us = [around(base, base_lo, base_hi, c) for c in range(3)]
            scaled = [HALF * u[d] for d in range(3)]
            up = [scaled[d] + DIFF for d in range(3)]
            down = [DIFF - scaled[d] for d in range(3)]
            out = []
            for i in range(3):
                acc = KEEP * f[i]
                for d in range(3):
                    acc = acc + up[d] * fs[i][d][0] + down[d] * fs[i][d][1]
                pull = fs[3][i][0] - fs[3][i][1]
                for j in range(3):
                    pull = pull + (us[j][i][0] - us[j][i][1]) * f[j]
                out.append(acc - HALF * pull)
            div = fs[0][0][0] - fs[0][0][1]
            for d in (1, 2):
                div = div + (fs[d][d][0] - fs[d][d][1])
            out.append(f[3] - HALF * div)
            for c in range(4):
                put(c, yt, k, out[c])


def fix(sign, d, f, u, beyond_f, beyond_u):
    coef = DIFF + (sign * HALF) * u[d]
    out = [coef * beyond_f[i] for i in range(3)]
    pull = beyond_f[3]
    for j in range(3):
        pull = pull + beyond_u[j] * f[j]
    out[d] = out[d] - (sign * HALF) * pull
    return out + [(-sign * HALF) * beyond_f[d]]


def tile_of(ref, index):
    def get(c, yt, k):
        return ref[(c, *index, pl.ds(yt * ROWS, ROWS), pl.ds(k * LANES, LANES))]
    return get


def pack_kernel(field, base, z_lo, z_hi, y_lo, y_hi):
    nz, ny, nx = field.shape[1:]

    def body(z, carry):
        for src, off, n in ((field, 0, 4), (base, 4, 3)):
            for c in range(n):
                for k in range(nx // LANES):
                    col = pl.ds(k * LANES, LANES)
                    y_lo[c + off, z, pl.ds(k, 1), :] = src[c, z, pl.ds(0, 1), col]
                    y_hi[c + off, z, pl.ds(k, 1), :] = src[c, z, pl.ds(ny - 1, 1), col]
        return carry

    lax.fori_loop(0, nz, body, 0)
    z_lo[0:4] = field[:, 0]
    z_lo[4:7] = base[:, 0]
    z_hi[0:4] = field[:, nz - 1]
    z_hi[4:7] = base[:, nz - 1]


def f32(*shape):
    return jax.ShapeDtypeStruct(shape, jnp.float32)


def call(kernel, name, out_shape, in_specs, out_specs, scratch=(), mib=20, cost=None):
    return pl.pallas_call(
        kernel,
        out_shape=out_shape,
        in_specs=in_specs,
        out_specs=out_specs,
        scratch_shapes=list(scratch),
        compiler_params=pltpu.CompilerParams(vmem_limit_bytes=mib * 2**20),
        cost_estimate=cost,
        name=name,
    )


IN_VMEM = pl.BlockSpec(memory_space=VMEM)
IN_SMEM = pl.BlockSpec(memory_space=SMEM)
ANYWHERE = pl.BlockSpec(memory_space=pl.ANY)


def pack(field, base):
    _, nz, ny, nx = field.shape
    shapes = [f32(7, ny, nx)] * 2 + [f32(7, nz, nx // LANES, LANES)] * 2
    return call(pack_kernel, "pack_faces", shapes, [IN_VMEM] * 2, [IN_VMEM] * 4)(field, base)


def gather_tiles(cells, z_off, blocks, normals, rows, rows_in):
    ny, nx = cells.shape[2:]
    per_row = nx // LANES
    row_bits, y_bits = per_row.bit_length() - 1, ny.bit_length() - 1
    sub = lax.broadcasted_iota(jnp.int32, (ROWS, LANES), 0)

    def gather(group, carry):
        kept = jnp.zeros((ROWS, LANES), jnp.float32)
        for j in range(ROWS):
            t = group * ROWS + j
            b = blocks[t]
            z = lax.shift_right_logical(b, row_bits + y_bits) + z_off
            y = lax.shift_right_logical(b, row_bits) & (ny - 1)
            near = pl.ds(pl.multiple_of(y & (ny - ROWS), ROWS), ROWS)
            col = pl.ds(pl.multiple_of((b & (per_row - 1)) * LANES, LANES), LANES)
            total = normals[0, t] * cells[0, z, near, col]
            for c in range(1, 4):
                total = total + normals[c, t] * cells[c, z, near, col]
            total = pltpu.roll(total, (j + ROWS - (y & (ROWS - 1))) & (ROWS - 1), 0)
            kept = jnp.where(sub == j, total, kept)
        kept = TIME_STEP * kept
        here = pl.ds(pl.multiple_of(group * ROWS, ROWS), ROWS)
        if rows_in is not None:
            kept = kept + rows_in[here, :]
        rows[here, :] = kept
        return carry

    lax.fori_loop(0, rows.shape[0] // ROWS, gather, 0)


def put_rows(cells, at, rows_lo, rows_hi, z):
    ny, nx = cells.shape[2:]
    for c in range(4):
        for k in range(nx // LANES):
            col = pl.ds(k * LANES, LANES)
            cells[c, at, pl.ds(0, 1), col] = rows_lo[c, z, pl.ds(k, 1), :]
            cells[c, at, pl.ds(ny - 1, 1), col] = rows_hi[c, z, pl.ds(k, 1), :]


def stencil_kernel(step, *refs):
    if step == 0:
        (field, base, new, p_lo, p_hi, r_lo, r_hi, cells, flow, fresh, fsem, usem, osem) = refs
    else:
        (field, base, own_lo, own_hi, row_lo, row_hi, blocks, normals, *rest) = refs
        if step > 1:
            rows_in, *rest = rest
        else:
            rows_in = None
        (new, p_lo, p_hi, r_lo, r_hi, rows, cells, flow, fresh, fsem, usem, osem) = rest
    nz, ny, nx = fresh.shape[1:]

    def load(z):
        return (pltpu.make_async_copy(field.at[:, z], cells.at[:, z + 1], fsem.at[z]),
                pltpu.make_async_copy(base.at[:, z], flow.at[:, z + 1], usem.at[z]))

    def store(z):
        return pltpu.make_async_copy(fresh.at[:, z], new.at[:, z], osem.at[z])

    def start(z, carry):
        for one in load(z):
            one.start()
        return carry

    lax.fori_loop(0, nz, start, 0)
    for at in (0, nz + 1):
        cells[:, at] = jnp.zeros((4, ny, nx), jnp.float32)
        flow[:, at] = jnp.zeros((3, ny, nx), jnp.float32)

    def ready(z):
        for one in load(z):
            one.wait()
        if step > 0:
            put_rows(cells, z + 1, row_lo, row_hi, z)

    ready(0)
    if step > 0:
        cells[:, 1] = own_lo[...]

    def body(z, carry):
        @pl.when(z + 1 < nz)
        def _():
            ready(z + 1)

        if step > 0:
            @pl.when(z + 1 == nz - 1)
            def _():
                cells[:, nz] = own_hi[...]

        def put(c, yt, k, value):
            fresh[c, z, pl.ds(yt * ROWS, ROWS), pl.ds(k * LANES, LANES)] = value
            if yt == 0:
                r_lo[c, z, pl.ds(k, 1), :] = value[:1]
            if yt == ny // ROWS - 1:
                r_hi[c, z, pl.ds(k, 1), :] = value[ROWS - 1:]

        plane(tile_of(cells, (z + 1,)), tile_of(cells, (z,)), tile_of(cells, (z + 2,)),
              tile_of(flow, (z + 1,)), tile_of(flow, (z,)), tile_of(flow, (z + 2,)), put, ny, nx)
        store(z).start()
        return carry

    lax.fori_loop(0, nz, body, 0)
    p_lo[...] = fresh[:, 0]
    p_hi[...] = fresh[:, nz - 1]
    if step > 0:
        gather_tiles(cells, 1, blocks, normals, rows, rows_in)

    def finish(z, carry):
        store(z).wait()
        return carry

    lax.fori_loop(0, nz, finish, 0)


def stencil(step, field, base, own=(), rows=(), blocks=None, normals=None, rows_in=()):
    _, nz, ny, nx = field.shape
    per_row = nx // LANES
    outs = [f32(*field.shape)] + [f32(4, ny, nx)] * 2 + [f32(4, nz, per_row, LANES)] * 2
    specs = [ANYWHERE] + [IN_VMEM] * 4
    ins, args = [ANYWHERE] * 2, [field, base]
    if step > 0:
        ins += [IN_VMEM] * 4 + [IN_SMEM] * 2 + [IN_VMEM] * len(rows_in)
        args += [*own, *rows, blocks, normals, *rows_in]
        outs.append(f32(blocks.shape[0], LANES))
        specs.append(IN_VMEM)
    scratch = [VMEM((4, nz + 2, ny, nx), jnp.float32), VMEM((3, nz + 2, ny, nx), jnp.float32), VMEM((4, nz, ny, nx), jnp.float32)]
    scratch += [pltpu.SemaphoreType.DMA((nz,))] * 3
    cost = pl.CostEstimate(flops=130 * field.size // 4, bytes_accessed=11 * 2**20, transcendentals=0)
    return call(functools.partial(stencil_kernel, step), "stencil", outs, ins, specs, scratch, 32, cost)(*args)


def row_fix_kernel(p_lo, p_hi, r_lo, r_hi, own_lo, own_hi, base_lo, base_hi, far_lo, far_hi, fbase_lo, fbase_hi,
                   q_lo, q_hi, s_lo, s_hi):
    _, ny, nx = p_lo.shape
    nz = r_lo.shape[1]

    def body(z, carry):
        for sign, r, own, base, far, fbase, s in ((-1, r_lo, own_lo, base_lo, far_lo, fbase_lo, s_lo),
                                                  (1, r_hi, own_hi, base_hi, far_hi, fbase_hi, s_hi)):
            add = fix(sign, 1, [own[c, z] for c in range(3)], [base[4 + c, z] for c in range(3)],
                      [far[c, z] for c in range(4)], [fbase[4 + c, z] for c in range(3)])
            for c in range(4):
                s[c, z] = r[c, z] + add[c]
        return carry

    lax.fori_loop(0, nz, body, 0)
    for z, p, q in ((0, p_lo, q_lo), (nz - 1, p_hi, q_hi)):
        q[...] = p[...]
        for c in range(4):
            for k in range(nx // LANES):
                col = pl.ds(k * LANES, LANES)
                q[c, pl.ds(0, 1), col] = s_lo[c, z, pl.ds(k, 1), :]
                q[c, pl.ds(ny - 1, 1), col] = s_hi[c, z, pl.ds(k, 1), :]


def row_fix(planes, rows, own_rows, base_rows, far_rows, far_base_rows):
    outs = [f32(*planes[0].shape)] * 2 + [f32(*rows[0].shape)] * 2
    cost = pl.CostEstimate(flops=10**6, bytes_accessed=2**18, transcendentals=0)
    return call(row_fix_kernel, "row_fix", outs, [IN_VMEM] * 12, [IN_VMEM] * 4, cost=cost)(
        *planes, *rows, *own_rows, *base_rows, *far_rows, *far_base_rows)


def plane_fix_kernel(first, *refs):
    (q_lo, q_hi, s_lo, s_hi, own_lo, own_hi, base_lo, base_hi, fbase_lo, fbase_hi, far_lo, far_hi, *rest) = refs
    if first:
        out_lo, out_hi, row_lo, row_hi = rest
    else:
        old_lo, old_hi, got_lo, got_hi, out_lo, out_hi, row_lo, row_hi, next_lo, next_hi = rest
    _, ny, nx = q_lo.shape
    nz = s_lo.shape[1]
    span = lax.axis_index("span")
    sides = (
        (-1, q_lo, own_lo, base_lo, fbase_lo, far_lo, out_lo, span > 0),
        (1, q_hi, own_hi, base_hi, fbase_hi, far_hi, out_hi, span < lax.axis_size("span") - 1),
    )
    for side, (sign, q, own, base, fbase, far, out, there) in enumerate(sides):
        for yt in range(ny // ROWS):
            for k in range(nx // LANES):
                tile = (pl.ds(yt * ROWS, ROWS), pl.ds(k * LANES, LANES))
                u = [base[(4 + c, *tile)] for c in range(3)]
                fu = [fbase[(4 + c, *tile)] for c in range(3)]
                beyond = [far[(c, *tile)] for c in range(4)]
                if not first:
                    old, got, nxt = ((old_lo, got_lo, next_lo), (old_hi, got_hi, next_hi))[side]
                    back = fix(-sign, 2, beyond, fu, [old[(c, *tile)] for c in range(4)], u)
                    beyond = [jnp.where(there, got[(c, *tile)] + back[c], 0.0) for c in range(4)]
                    for c in range(4):
                        nxt[(c, *tile)] = beyond[c]
                add = fix(sign, 2, [own[(c, *tile)] for c in range(3)], u, beyond, fu)
                for c in range(4):
                    out[(c, *tile)] = q[(c, *tile)] + add[c]
    row_lo[...] = s_lo[...]
    row_hi[...] = s_hi[...]
    for z, out in ((0, out_lo), (nz - 1, out_hi)):
        for c in range(4):
            for k in range(nx // LANES):
                col = pl.ds(k * LANES, LANES)
                row_lo[c, z, pl.ds(k, 1), :] = out[c, pl.ds(0, 1), col]
                row_hi[c, z, pl.ds(k, 1), :] = out[c, pl.ds(ny - 1, 1), col]


def plane_fix(planes, rows, own, base, far_base, far, old=(), got=()):
    first = not got
    outs = [f32(*planes[0].shape)] * 2 + [f32(*rows[0].shape)] * 2
    if not first:
        outs += [f32(*planes[0].shape)] * 2
    cost = pl.CostEstimate(flops=10**6, bytes_accessed=2**18, transcendentals=0)
    args = [*planes, *rows, *own, *base, *far_base, *far, *old, *got]
    return call(functools.partial(plane_fix_kernel, first), "plane_fix", outs, [IN_VMEM] * len(args), [IN_VMEM] * len(outs),
                cost=cost)(*args)


def finish_kernel(field, own_lo, own_hi, row_lo, row_hi, blocks, normals, sections, rows_in, new, table, cells, rows, fsem, osem):
    nz, ny, nx = cells.shape[1:]

    def load(z):
        return pltpu.make_async_copy(field.at[:, z], cells.at[:, z], fsem.at[z])

    def store(z):
        return pltpu.make_async_copy(cells.at[:, z], new.at[:, z], osem.at[z])

    def start(z, carry):
        load(z).start()
        return carry

    def patch(z, carry):
        load(z).wait()
        put_rows(cells, z, row_lo, row_hi, z)

        @pl.when(z == 0)
        def _():
            cells[:, 0] = own_lo[...]

        @pl.when(z == nz - 1)
        def _():
            cells[:, nz - 1] = own_hi[...]

        store(z).start()
        return carry

    def done(z, carry):
        store(z).wait()
        return carry

    lax.fori_loop(0, nz, start, 0)
    lax.fori_loop(0, nz, patch, 0)
    gather_tiles(cells, 0, blocks, normals, rows, rows_in)
    labels = lax.broadcasted_iota(jnp.int32, (table.shape[0], rows.shape[0]), 0)
    onehot = (labels == sections[...]).astype(jnp.float32)
    table[...] = jnp.dot(onehot, rows[...], precision=lax.Precision.HIGHEST, preferred_element_type=jnp.float32)
    lax.fori_loop(0, nz, done, 0)


def finish(field, own, rows, blocks, normals, sections, rows_in, total):
    nz = field.shape[1]
    tiles = blocks.shape[0]
    scratch = [VMEM(field.shape, jnp.float32), VMEM((tiles, LANES), jnp.float32)] + [pltpu.SemaphoreType.DMA((nz,))] * 2
    return call(finish_kernel, "finish", [f32(*field.shape), f32(total, LANES)],
                [ANYWHERE] + [IN_VMEM] * 4 + [IN_SMEM] * 2 + [IN_VMEM] * 2, [ANYWHERE, IN_VMEM], scratch, 24)(
        field, *own, *rows, blocks, normals, sections, rows_in)


def shift_along(block, axis, distance):
    count = lax.axis_size(axis)
    route = [(i, i + distance) for i in range(count) if 0 <= i + distance < count]
    return lax.ppermute(block, axis, route)


def swap(faces, axis):
    lo, hi = faces
    return [shift_along(hi, axis, 1), shift_along(lo, axis, -1)]


def local(adjoint_start, base_flow, wall_blocks, tile_sections, tile_normals, modes):
    z_lo, z_hi, y_lo, y_hi = pack(adjoint_start, base_flow)
    base_planes, base_rows = [z_lo, z_hi], [y_lo, y_hi]
    own, own_rows = base_planes, base_rows
    far = far_base = swap(base_planes, "span")
    far_rows = far_base_rows = swap(base_rows, "cross")
    field, rows_sum = adjoint_start, ()
    old, got = (), ()
    for step in range(STEPS):
        if step == 0:
            field, *edge = stencil(step, field, base_flow)
        else:
            field, *edge, rows_sum = stencil(step, field, base_flow, own, own_rows, wall_blocks, tile_normals, rows_sum)
            rows_sum = (rows_sum,)
        planes, rows = edge[:2], edge[2:]
        *planes, row_lo, row_hi = row_fix(planes, rows, own_rows, base_rows, far_rows, far_base_rows)
        coming = swap(planes, "span") if step < STEPS - 1 else ()
        out = plane_fix(planes, (row_lo, row_hi), own, base_planes, far_base, far, old, got)
        old, own, own_rows, got = own, out[:2], out[2:4], coming
        if step > 0:
            far = out[4:]
        if step < STEPS - 1:
            far_rows = swap(own_rows, "cross")
    sections = tile_sections.reshape(1, -1)
    crosses, spans = lax.axis_size("cross"), lax.axis_size("span")
    field, table = finish(field, own, own_rows, wall_blocks, tile_normals, sections, rows_sum[0], spans * crosses * SEC_DEV)
    parts = lax.all_to_all(table.reshape(spans * crosses, SEC_DEV, LANES), ("span", "cross"), 0, 0, tiled=True)
    section_sum = jnp.sum(parts, axis=0)
    modal_load = jnp.dot(section_sum, modes, precision=lax.Precision.HIGHEST, preferred_element_type=jnp.float32)
    return field, modal_load


def solution(mesh):
    placed = (
        P(None, "span", "cross", None),
        P(None, "span", "cross", None),
        P(("span", "cross")),
        P(("span", "cross"), None),
        P(None, ("span", "cross")),
        P(),
    )
    return jax.shard_map(
        local,
        mesh=mesh,
        in_specs=placed,
        out_specs=(P(None, "span", "cross", None), P(("span", "cross"), None)),
        check_vma=False,
    )
```

time: 208 us -> 129 us (0.62); the launches traced: 205 us -> 129 us
  Pallas kernels: 107 us -> 50.1 us
  waiting for transfers between devices: 32.9 us -> 7.23 us
  blocking collectives: 19.4 us -> 25.7 us
  starting transfers between devices: 44.4 us -> 39.8 us
  local copies, waits for them, and re-layouts: 0.05 us -> 4.14 us
    pallas_call x4 -> x11, Pallas kernels: 107 us -> 50.1 us  [the longest x3 41.1 us: stencil(): call(functools.partial(stencil_kernel, step), 'stencil', outs, ins, specs...]
    ppermute x14 -> x12, waiting for transfers between devices: 32.9 us -> 7.23 us  [shift_along(): return lax.ppermute(block, axis, route)]
    all_to_all x1, blocking collectives: 19.4 us -> 25.7 us  [local(): lax.all_to_all(table.reshape(spans * crosses, SEC_DEV, LANES), ('span', '...]
    ppermute x14 -> x12, starting transfers between devices: 44.4 us -> 39.8 us  [shift_along(): return lax.ppermute(block, axis, route)]
    unnamed x8 -> x16, local copies, waits for them, and re-layouts: 0.02 us -> 4.14 us
  transfers between devices with their start and end apart: 14 -> 12, of which waited for: 7 -> 1; matrix products, arithmetic and copies ran while one was open for 0% -> 0% of each run, Pallas kernels for 0% -> 33%
where the time goes in v2:
time: 129 us
  Pallas kernels  50.1 us (39%)
  starting transfers between devices  39.8 us (31%)
  blocking collectives  25.7 us (20%)
  waiting for transfers between devices  7.23 us (6%)
  local copies, waits for them, and re-layouts  4.14 us (3%)
    pallas_call x3, Pallas kernels, stencil(): call(functools.partial(stencil_kernel, step), 'stencil', outs, ins, specs...  41.1 us
    ppermute x12, starting transfers between devices, shift_along(): return lax.ppermute(block, axis, route)  39.8 us
    all_to_all x1, blocking collectives, local(): lax.all_to_all(table.reshape(spans * crosses, SEC_DEV, LANES), ('span', '...  25.7 us
    ppermute x12, waiting for transfers between devices, shift_along(): return lax.ppermute(block, axis, route)  7.23 us
    pallas_call x1, Pallas kernels, finish(): call(finish_kernel, 'finish', [f32(*field.shape), f32(total, LANES)], [AN...  5.39 us
    unnamed x16, local copies, waits for them, and re-layouts  4.14 us
  transfers between devices with their start and end apart: 12, of which 1 were waited for; matrix products, arithmetic and copies ran while one was open for 0% of the time, Pallas kernels for 33%

profile of v2, /device:TPU:1, one launch (start us, length us, event | category | flops | bytes accessed | tf_op | source)
XLA Modules:
  0.0 128.8 jit_solution(6889559116517904567)
XLA Ops:
  0.6 0.0 copy-start
  0.7 1.9 %copy-done.1 = f32[3,16,16,1024]{3,2,1,0:T(8,128)S(1)} copy-done((f32[3,16,16,1024]{3,2,1,0:T(8,128)S(1)}, f32[3,16,16,1024]{3,2,1,0:T(8,128)}, u32[]{:S(2)}) %copy-start.1) | copy-done | bytes 3145752
  2.6 2.2 %copy-done.3 = f32[4,16,16,1024]{3,2,1,0:T(8,128)S(1)} copy-done((f32[4,16,16,1024]{3,2,1,0:T(8,128)S(1)}, f32[4,16,16,1024]{3,2,1,0:T(8,128)}, u32[]{:S(2)}) %copy-start.3) | copy-done | bytes 4194328
  4.8 0.8 pack_faces.1
  5.5 5.2 %collective-permute-start = (f32[7,16,8,128]{3,2,1,0:T(8,128)S(1)}, f32[7,16,8,128]{3,2,1,0:T(8,128)S(1)}, u32[]{:S(2)}, u32[]{:S(2)}) collective-permute-start(f32[7,16,8,128]{3,2,1,0:T(8,128)S(1)} %get-tuple-element.57.own_hi.base_hi), channel_id=1, source_target_pairs={{0,1},{1,2},{2,3},{3,4},{4,5},{5,6},{6,7},{7,8},{8,9},{9,10},{10,1... | collective-permute-start | bytes 1376264 | tf_op jit(solution)/shard_map/ppermute | solution.py:404
  10.7 1.9 %collective-permute-start.1 = (f32[7,16,8,128]{3,2,1,0:T(8,128)S(1)}, f32[7,16,8,128]{3,2,1,0:T(8,128)S(1)}, u32[]{:S(2)}, u32[]{:S(2)}) collective-permute-start(f32[7,16,8,128]{3,2,1,0:T(8,128)S(1)} %get-tuple-element.56.own_lo.base_lo), channel_id=1, source_target_pairs={{1,0},{2,1},{3,2},{4,3},{5,4},{6,5},{7,6},{8,7},{9,8},{10,9},{11,1... | collective-permute-start | bytes 1376264 | tf_op jit(solution)/shard_map/ppermute | solution.py:404
  12.7 4.7 %collective-permute-start.2 = (f32[7,16,1024]{2,1,0:T(8,128)S(1)}, f32[7,16,1024]{2,1,0:T(8,128)S(1)}, u32[]{:S(2)}, u32[]{:S(2)}) collective-permute-start(f32[7,16,1024]{2,1,0:T(8,128)S(1)} %get-tuple-element.63.refs_5_.refs_7_.refs_13_), channel_id=1, source_target_pairs={{0,16},{16,32},{32,48},{48,64},{64,80},{80,96},{96,112},{1,17},{17... | collective-permute-start | bytes 1376264 | tf_op jit(solution)/shard_map/ppermute | solution.py:404
  17.4 1.3 %collective-permute-start.3 = (f32[7,16,1024]{2,1,0:T(8,128)S(1)}, f32[7,16,1024]{2,1,0:T(8,128)S(1)}, u32[]{:S(2)}, u32[]{:S(2)}) collective-permute-start(f32[7,16,1024]{2,1,0:T(8,128)S(1)} %get-tuple-element.62.refs_4_.refs_6_.refs_12_), channel_id=1, source_target_pairs={{16,0},{32,16},{48,32},{64,48},{80,64},{96,80},{112,96},{17,1},{33... | collective-permute-start | bytes 1376264 | tf_op jit(solution)/shard_map/ppermute | solution.py:404
  18.7 11.0 %stencil.3 = (f32[4,16,16,1024]{3,2,1,0:T(8,128)S(1)}, f32[4,16,1024]{2,1,0:T(8,128)S(1)}, f32[4,16,1024]{2,1,0:T(8,128)S(1)}, f32[4,16,8,128]{3,2,1,0:T(8,128)S(1)}, f32[4,16,8,128]{3,2,1,0:T(8,128)S(1)}) custom-call(f32[4,16,16,1024]{3,2,1,0:T(8,128)S(1)} %copy-done.4, f32[3,16,16,1024]{3,2,1,0:T(8,128)S(1)} %copy-done.2), custom_call_target="tpu_custom_call" | custom-call | flops 34078720 | bytes 11534336 | tf_op jit(solution)/shard_map/stencil/pallas_call | solution.py:267
  29.7 0.0 copy-start.5
  29.7 0.4 row_fix.3
  30.1 7.2 %collective-permute-done.3.refs_9_.refs_11_ = f32[7,16,1024]{2,1,0:T(8,128)S(1)} collective-permute-done((f32[7,16,1024]{2,1,0:T(8,128)S(1)}, f32[7,16,1024]{2,1,0:T(8,128)S(1)}, u32[]{:S(2)}, u32[]{:S(2)}) %collective-permute-start.3) | collective-permute-done | bytes 458784 | tf_op jit(solution)/shard_map/ppermute | solution.py:404
  37.3 0.2 plane_fix.3
  37.5 6.0 %collective-permute-start.4 = (f32[4,16,8,128]{3,2,1,0:T(8,128)S(1)}, f32[4,16,8,128]{3,2,1,0:T(8,128)S(1)}, u32[]{:S(2)}, u32[]{:S(2)}) collective-permute-start(f32[4,16,8,128]{3,2,1,0:T(8,128)S(1)} %get-tuple-element.67.refs_5_.own_hi), channel_id=1, source_target_pairs={{0,1},{1,2},{2,3},{3,4},{4,5},{5,6},{6,7},{7,8},{8,9},{9,10},{10,1... | collective-permute-start | bytes 786440 | tf_op jit(solution)/shard_map/ppermute | solution.py:404
  43.5 1.9 %collective-permute-start.5 = (f32[4,16,8,128]{3,2,1,0:T(8,128)S(1)}, f32[4,16,8,128]{3,2,1,0:T(8,128)S(1)}, u32[]{:S(2)}, u32[]{:S(2)}) collective-permute-start(f32[4,16,8,128]{3,2,1,0:T(8,128)S(1)} %get-tuple-element.66.refs_4_.own_lo), channel_id=1, source_target_pairs={{1,0},{2,1},{3,2},{4,3},{5,4},{6,5},{7,6},{8,7},{9,8},{10,9},{11,1... | collective-permute-start | bytes 786440 | tf_op jit(solution)/shard_map/ppermute | solution.py:404
  45.4 4.7 %collective-permute-start.6 = (f32[4,16,1024]{2,1,0:T(8,128)S(1)}, f32[4,16,1024]{2,1,0:T(8,128)S(1)}, u32[]{:S(2)}, u32[]{:S(2)}) collective-permute-start(f32[4,16,1024]{2,1,0:T(8,128)S(1)} %get-tuple-element.59.refs_1_), channel_id=1, source_target_pairs={{0,16},{16,32},{32,48},{48,64},{64,80},{80,96},{96,112},{1,17},{17... | collective-permute-start | bytes 786440 | tf_op jit(solution)/shard_map/ppermute | solution.py:404
  50.1 1.3 %collective-permute-start.7 = (f32[4,16,1024]{2,1,0:T(8,128)S(1)}, f32[4,16,1024]{2,1,0:T(8,128)S(1)}, u32[]{:S(2)}, u32[]{:S(2)}) collective-permute-start(f32[4,16,1024]{2,1,0:T(8,128)S(1)} %get-tuple-element.58.refs_0_), channel_id=1, source_target_pairs={{16,0},{32,16},{48,32},{64,48},{80,64},{96,80},{112,96},{17,1},{33... | collective-permute-start | bytes 786440 | tf_op jit(solution)/shard_map/ppermute | solution.py:404
  51.4 15.0 %stencil.4 = (f32[4,16,16,1024]{3,2,1,0:T(8,128)S(1)}, f32[4,16,1024]{2,1,0:T(8,128)S(1)}, f32[4,16,1024]{2,1,0:T(8,128)S(1)}, f32[4,16,8,128]{3,2,1,0:T(8,128)S...) custom-call(f32[4,16,16,1024]{3,2,1,0:T(8,128)S(1)} %get-tuple-element.51.refs_0_, ...), custom_call_target="tpu_custom_call" | custom-call | flops 34078720 | bytes 11534336 | tf_op jit(solution)/shard_map/stencil/pallas_call | solution.py:267
  66.5 0.4 row_fix.4
  66.9 0.3 plane_fix.4
  67.2 3.9 %collective-permute-start.8 = (f32[4,16,8,128]{3,2,1,0:T(8,128)S(1)}, f32[4,16,8,128]{3,2,1,0:T(8,128)S(1)}, u32[]{:S(2)}, u32[]{:S(2)}) collective-permute-start(f32[4,16,8,128]{3,2,1,0:T(8,128)S(1)} %get-tuple-element.80.refs_5_.own_hi), channel_id=1, source_target_pairs={{0,1},{1,2},{2,3},{3,4},{4,5},{5,6},{6,7},{7,8},{8,9},{9,10},{10,1... | collective-permute-start | bytes 786440 | tf_op jit(solution)/shard_map/ppermute | solution.py:404
  71.2 1.9 %collective-permute-start.9 = (f32[4,16,8,128]{3,2,1,0:T(8,128)S(1)}, f32[4,16,8,128]{3,2,1,0:T(8,128)S(1)}, u32[]{:S(2)}, u32[]{:S(2)}) collective-permute-start(f32[4,16,8,128]{3,2,1,0:T(8,128)S(1)} %get-tuple-element.79.refs_4_.own_lo), channel_id=1, source_target_pairs={{1,0},{2,1},{3,2},{4,3},{5,4},{6,5},{7,6},{8,7},{9,8},{10,9},{11,1... | collective-permute-start | bytes 786440 | tf_op jit(solution)/shard_map/ppermute | solution.py:404
  73.1 5.8 %collective-permute-start.10 = (f32[4,16,1024]{2,1,0:T(8,128)S(1)}, f32[4,16,1024]{2,1,0:T(8,128)S(1)}, u32[]{:S(2)}, u32[]{:S(2)}) collective-permute-start(f32[4,16,1024]{2,1,0:T(8,128)S(1)} %get-tuple-element.74.refs_1_), channel_id=1, source_target_pairs={{0,16},{16,32},{32,48},{48,64},{64,80},{80,96},{96,112},{1,17},{17... | collective-permute-start | bytes 786440 | tf_op jit(solution)/shard_map/ppermute | solution.py:404
  78.9 1.3 %collective-permute-start.11 = (f32[4,16,1024]{2,1,0:T(8,128)S(1)}, f32[4,16,1024]{2,1,0:T(8,128)S(1)}, u32[]{:S(2)}, u32[]{:S(2)}) collective-permute-start(f32[4,16,1024]{2,1,0:T(8,128)S(1)} %get-tuple-element.73.refs_0_), channel_id=1, source_target_pairs={{16,0},{32,16},{48,32},{64,48},{80,64},{96,80},{112,96},{17,1},{33... | collective-permute-start | bytes 786440 | tf_op jit(solution)/shard_map/ppermute | solution.py:404
  80.2 15.1 %stencil.5 = (f32[4,16,16,1024]{3,2,1,0:T(8,128)S(1)}, f32[4,16,1024]{2,1,0:T(8,128)S(1)}, f32[4,16,1024]{2,1,0:T(8,128)S(1)}, f32[4,16,8,128]{3,2,1,0:T(8,128)S...) custom-call(f32[4,16,16,1024]{3,2,1,0:T(8,128)S(1)} %get-tuple-element.68.refs_0_, ...), custom_call_target="tpu_custom_call" | custom-call | flops 34078720 | bytes 11534336 | tf_op jit(solution)/shard_map/stencil/pallas_call | solution.py:267
  95.3 0.0 copy-start.7
  95.3 0.4 row_fix.5
  95.7 1.1 plane_fix.5
  96.8 5.4 %finish.1 = (f32[4,16,16,1024]{3,2,1,0:T(8,128)}, f32[256,128]{1,0:T(8,128)S(1)}) custom-call(f32[4,16,16,1024]{3,2,1,0:T(8,128)S(1)} %get-tuple-element.82.field, f32[4,16,1024]{2,1,0:T(8,128)S(1)} %get-tuple-element.93.own_lo, f32[4,16,1024]{2,1,0:T(8,128)S(1)} %get-tuple-element.94.own_hi, f32[4,16,8,128]{3,2,1,0:T(8,128)S(1)} %get-tuple-element.95.row_lo, ...), custom_call_target="tpu_custom_call" | custom-call | tf_op jit(solution)/shard_map/finish/pallas_call | solution.py:396
  102.2 25.7 %all_to_all.5 = f32[128,2,128]{2,1,0:T(2,128)S(1)} all-to-all(f32[128,2,128]{2,1,0:T(2,128)S(1)} %bitcast.4), channel_id=1, replica_groups=mesh['span'=8,'cross'=16] {'span','cross'}, dimensions={0} | all-to-all | bytes 262144 | tf_op jit(solution)/shard_map/all_to_all | solution.py:438
  127.9 0.1 reduce_sum.9
  128.1 0.7 fusion
  (22 shorter events, 0.1 us)
Async XLA Ops:
  0.6 127.5 %copy-start = (f32[128,128]{1,0:T(8,128)S(1)}, f32[128,128]{1,0:T(8,128)}, u32[]{:S(2)}) copy-start(f32[128,128]{1,0:T(8,128)} %param.11) | copy-start | bytes 196612
  0.6 1.9 %copy-start.1 = (f32[3,16,16,1024]{3,2,1,0:T(8,128)S(1)}, f32[3,16,16,1024]{3,2,1,0:T(8,128)}, u32[]{:S(2)}) copy-start(f32[3,16,16,1024]{3,2,1,0:T(8,128)} %refs_1_.5) | copy-start | bytes 9437188
  2.6 2.2 %copy-start.3 = (f32[4,16,16,1024]{3,2,1,0:T(8,128)S(1)}, f32[4,16,16,1024]{3,2,1,0:T(8,128)}, u32[]{:S(2)}) copy-start(f32[4,16,16,1024]{3,2,1,0:T(8,128)} %field.1) | copy-start | bytes 12582916
  4.8 13.9 %copy-start.2 = (f32[3,16,16,1024]{3,2,1,0:T(8,128)S(1)}, f32[3,16,16,1024]{3,2,1,0:T(8,128)}, u32[]{:S(2)}) copy-start(f32[3,16,16,1024]{3,2,1,0:T(8,128)} %refs_1_.5) | copy-start | bytes 9437188
  4.8 13.9 %copy-start.4 = (f32[4,16,16,1024]{3,2,1,0:T(8,128)S(1)}, f32[4,16,16,1024]{3,2,1,0:T(8,128)}, u32[]{:S(2)}) copy-start(f32[4,16,16,1024]{3,2,1,0:T(8,128)} %field.1) | copy-start | bytes 12582916
  5.5 24.1 %collective-permute-start = (f32[7,16,8,128]{3,2,1,0:T(8,128)S(1)}, f32[7,16,8,128]{3,2,1,0:T(8,128)S(1)}, u32[]{:S(2)}, u32[]{:S(2)}) collective-permute-start(f32[7,16,8,128]{3,2,1,0:T(8,128)S(1)} %get-tuple-element.57.own_hi.base_hi), channel_id=1, source_target_pairs={{0,1},{1,2},{2,3},{3,4},{4,5},{5,6},{6,7},{7,8},{8,9},{9,10},{10,1... | collective-permute-start | bytes 1376264 | tf_op jit(solution)/shard_map/ppermute | solution.py:404
  10.7 18.9 %collective-permute-start.1 = (f32[7,16,8,128]{3,2,1,0:T(8,128)S(1)}, f32[7,16,8,128]{3,2,1,0:T(8,128)S(1)}, u32[]{:S(2)}, u32[]{:S(2)}) collective-permute-start(f32[7,16,8,128]{3,2,1,0:T(8,128)S(1)} %get-tuple-element.56.own_lo.base_lo), channel_id=1, source_target_pairs={{1,0},{2,1},{3,2},{4,3},{5,4},{6,5},{7,6},{8,7},{9,8},{10,9},{11,1... | collective-permute-start | bytes 1376264 | tf_op jit(solution)/shard_map/ppermute | solution.py:404
  12.7 17.4 %collective-permute-start.2 = (f32[7,16,1024]{2,1,0:T(8,128)S(1)}, f32[7,16,1024]{2,1,0:T(8,128)S(1)}, u32[]{:S(2)}, u32[]{:S(2)}) collective-permute-start(f32[7,16,1024]{2,1,0:T(8,128)S(1)} %get-tuple-element.63.refs_5_.refs_7_.refs_13_), channel_id=1, source_target_pairs={{0,16},{16,32},{32,48},{48,64},{64,80},{80,96},{96,112},{1,17},{17... | collective-permute-start | bytes 1376264 | tf_op jit(solution)/shard_map/ppermute | solution.py:404
  17.4 20.0 %collective-permute-start.3 = (f32[7,16,1024]{2,1,0:T(8,128)S(1)}, f32[7,16,1024]{2,1,0:T(8,128)S(1)}, u32[]{:S(2)}, u32[]{:S(2)}) collective-permute-start(f32[7,16,1024]{2,1,0:T(8,128)S(1)} %get-tuple-element.62.refs_4_.refs_6_.refs_12_), channel_id=1, source_target_pairs={{16,0},{32,16},{48,32},{64,48},{80,64},{96,80},{112,96},{17,1},{33... | collective-permute-start | bytes 1376264 | tf_op jit(solution)/shard_map/ppermute | solution.py:404
  29.7 21.7 %copy-start.5 = (f32[4,256]{1,0:T(4,128)S(1)}, f32[4,256]{1,0:T(4,128)}, u32[]{:S(2)}) copy-start(f32[4,256]{1,0:T(4,128)} %normals.1) | copy-start | bytes 12292
  29.7 21.7 %copy-start.6 = (s32[256]{0:T(256)S(1)}, s32[256]{0:T(256)}, u32[]{:S(2)}) copy-start(s32[256]{0:T(256)} %blocks.1) | copy-start | bytes 3076
  37.5 28.9 %collective-permute-start.4 = (f32[4,16,8,128]{3,2,1,0:T(8,128)S(1)}, f32[4,16,8,128]{3,2,1,0:T(8,128)S(1)}, u32[]{:S(2)}, u32[]{:S(2)}) collective-permute-start(f32[4,16,8,128]{3,2,1,0:T(8,128)S(1)} %get-tuple-element.67.refs_5_.own_hi), channel_id=1, source_target_pairs={{0,1},{1,2},{2,3},{3,4},{4,5},{5,6},{6,7},{7,8},{8,9},{9,10},{10,1... | collective-permute-start | bytes 786440 | tf_op jit(solution)/shard_map/ppermute | solution.py:404
  43.5 23.0 %collective-permute-start.5 = (f32[4,16,8,128]{3,2,1,0:T(8,128)S(1)}, f32[4,16,8,128]{3,2,1,0:T(8,128)S(1)}, u32[]{:S(2)}, u32[]{:S(2)}) collective-permute-start(f32[4,16,8,128]{3,2,1,0:T(8,128)S(1)} %get-tuple-element.66.refs_4_.own_lo), channel_id=1, source_target_pairs={{1,0},{2,1},{3,2},{4,3},{5,4},{6,5},{7,6},{8,7},{9,8},{10,9},{11,1... | collective-permute-start | bytes 786440 | tf_op jit(solution)/shard_map/ppermute | solution.py:404
  45.4 21.5 %collective-permute-start.6 = (f32[4,16,1024]{2,1,0:T(8,128)S(1)}, f32[4,16,1024]{2,1,0:T(8,128)S(1)}, u32[]{:S(2)}, u32[]{:S(2)}) collective-permute-start(f32[4,16,1024]{2,1,0:T(8,128)S(1)} %get-tuple-element.59.refs_1_), channel_id=1, source_target_pairs={{0,16},{16,32},{32,48},{48,64},{64,80},{80,96},{96,112},{1,17},{17... | collective-permute-start | bytes 786440 | tf_op jit(solution)/shard_map/ppermute | solution.py:404
  50.1 16.8 %collective-permute-start.7 = (f32[4,16,1024]{2,1,0:T(8,128)S(1)}, f32[4,16,1024]{2,1,0:T(8,128)S(1)}, u32[]{:S(2)}, u32[]{:S(2)}) collective-permute-start(f32[4,16,1024]{2,1,0:T(8,128)S(1)} %get-tuple-element.58.refs_0_), channel_id=1, source_target_pairs={{16,0},{32,16},{48,32},{64,48},{80,64},{96,80},{112,96},{17,1},{33... | collective-permute-start | bytes 786440 | tf_op jit(solution)/shard_map/ppermute | solution.py:404
  67.2 28.0 %collective-permute-start.8 = (f32[4,16,8,128]{3,2,1,0:T(8,128)S(1)}, f32[4,16,8,128]{3,2,1,0:T(8,128)S(1)}, u32[]{:S(2)}, u32[]{:S(2)}) collective-permute-start(f32[4,16,8,128]{3,2,1,0:T(8,128)S(1)} %get-tuple-element.80.refs_5_.own_hi), channel_id=1, source_target_pairs={{0,1},{1,2},{2,3},{3,4},{4,5},{5,6},{6,7},{7,8},{8,9},{9,10},{10,1... | collective-permute-start | bytes 786440 | tf_op jit(solution)/shard_map/ppermute | solution.py:404
  71.2 24.1 %collective-permute-start.9 = (f32[4,16,8,128]{3,2,1,0:T(8,128)S(1)}, f32[4,16,8,128]{3,2,1,0:T(8,128)S(1)}, u32[]{:S(2)}, u32[]{:S(2)}) collective-permute-start(f32[4,16,8,128]{3,2,1,0:T(8,128)S(1)} %get-tuple-element.79.refs_4_.own_lo), channel_id=1, source_target_pairs={{1,0},{2,1},{3,2},{4,3},{5,4},{6,5},{7,6},{8,7},{9,8},{10,9},{11,1... | collective-permute-start | bytes 786440 | tf_op jit(solution)/shard_map/ppermute | solution.py:404
  73.1 22.6 %collective-permute-start.10 = (f32[4,16,1024]{2,1,0:T(8,128)S(1)}, f32[4,16,1024]{2,1,0:T(8,128)S(1)}, u32[]{:S(2)}, u32[]{:S(2)}) collective-permute-start(f32[4,16,1024]{2,1,0:T(8,128)S(1)} %get-tuple-element.74.refs_1_), channel_id=1, source_target_pairs={{0,16},{16,32},{32,48},{48,64},{64,80},{80,96},{96,112},{1,17},{17... | collective-permute-start | bytes 786440 | tf_op jit(solution)/shard_map/ppermute | solution.py:404
  78.9 16.8 %collective-permute-start.11 = (f32[4,16,1024]{2,1,0:T(8,128)S(1)}, f32[4,16,1024]{2,1,0:T(8,128)S(1)}, u32[]{:S(2)}, u32[]{:S(2)}) collective-permute-start(f32[4,16,1024]{2,1,0:T(8,128)S(1)} %get-tuple-element.73.refs_0_), channel_id=1, source_target_pairs={{16,0},{32,16},{48,32},{64,48},{80,64},{96,80},{112,96},{17,1},{33... | collective-permute-start | bytes 786440 | tf_op jit(solution)/shard_map/ppermute | solution.py:404
  95.3 1.6 %copy-start.7 = (s32[256,1]{0,1:T(1,128)S(1)}, s32[256,1]{0,1:T(1,128)}, u32[]{:S(2)}) copy-start(s32[256,1]{0,1:T(1,128)} %param.9) | copy-start | bytes 3076

commit v3 on v0

v3 whole, which is shorter than its diff:
```python
import functools

import jax
import jax.numpy as jnp
from jax import lax
from jax.experimental import pallas as pl
from jax.experimental.pallas import tpu as pltpu
from jax.sharding import PartitionSpec as P

STEPS = 3
SEC_DEV = 2
TIME_STEP = 0.25
VISCOSITY = 0.1
LANES = 128
ROWS = 8
HALF = 0.5 * TIME_STEP
DIFF = TIME_STEP * VISCOSITY
KEEP = 1.0 - 6.0 * DIFF

VMEM = pltpu.VMEM
SMEM = pltpu.SMEM


def plane(field, f_lo, f_hi, slopes, base, put, ny, nx, put_slopes=None):
    lane = lax.broadcasted_iota(jnp.int32, (ROWS, LANES), 1)
    sub = lax.broadcasted_iota(jnp.int32, (ROWS, LANES), 0)
    last = nx // LANES - 1
    tiles = range(ny // ROWS)

    class Shifted:
        def __init__(self, get, c):
            self.get, self.c, self.kept = get, c, {}

        def once(self, key, make):
            if key not in self.kept:
                self.kept[key] = make()
            return self.kept[key]

        def tile(self, yt, k):
            return self.once((0, yt, k), lambda: self.get(self.c, yt, k))

        def left(self, yt, k):
            return self.once((1, yt, k), lambda: pltpu.roll(self.tile(yt, k), LANES - 1, 1))

        def right(self, yt, k):
            return self.once((2, yt, k), lambda: pltpu.roll(self.tile(yt, k), 1, 1))

        def up(self, yt, k):
            return self.once((3, yt, k), lambda: pltpu.roll(self.tile(yt, k), ROWS - 1, 0))

        def down(self, yt, k):
            return self.once((4, yt, k), lambda: pltpu.roll(self.tile(yt, k), 1, 0))

        def along_x(self, yt, k):
            return (jnp.where(lane == LANES - 1, self.left(yt, k + 1) if k < last else 0.0, self.left(yt, k)),
                    jnp.where(lane == 0, self.right(yt, k - 1) if k > 0 else 0.0, self.right(yt, k)))

        def along_y(self, yt, k):
            return (jnp.where(sub == ROWS - 1, self.up(yt + 1, k) if yt + 1 in tiles else 0.0, self.up(yt, k)),
                    jnp.where(sub == 0, self.down(yt - 1, k) if yt > 0 else 0.0, self.down(yt, k)))

    fields = [Shifted(field, c) for c in range(4)]
    flows = [Shifted(base, c) for c in range(3)]
    for k in range(nx // LANES):
        for yt in tiles:
            f = [fields[c].tile(yt, k) for c in range(4)]
            u = [flows[c].tile(yt, k) for c in range(3)]
            fs = [(fields[c].along_x(yt, k), fields[c].along_y(yt, k), (f_hi(c, yt, k), f_lo(c, yt, k))) for c in range(4)]
            slope = slopes(flows, yt, k)
            scaled = [HALF * u[d] for d in range(3)]
            up = [scaled[d] + DIFF for d in range(3)]
            down = [DIFF - scaled[d] for d in range(3)]
            out = []
            for i in range(3):
                acc = KEEP * f[i]
                for d in range(3):
                    acc = acc + up[d] * fs[i][d][0] + down[d] * fs[i][d][1]
                pull = fs[3][i][0] - fs[3][i][1]
                for j in range(3):
                    pull = pull + slope[i][j] * f[j]
                out.append(acc - HALF * pull)
            div = fs[0][0][0] - fs[0][0][1]
            for d in (1, 2):
                div = div + (fs[d][d][0] - fs[d][d][1])
            out.append(f[3] - HALF * div)
            for c in range(4):
                put(c, yt, k, out[c])
            if put_slopes is not None:
                put_slopes(yt, k, slope)


def fix(sign, d, f, u, beyond_f, beyond_u):
    half = sign * HALF
    coef = DIFF + half * u[d]
    out = [coef * beyond_f[i] for i in range(3)]
    pull = beyond_f[3]
    for j in range(3):
        pull = pull + beyond_u[j] * f[j]
    out[d] = out[d] - half * pull
    return out + [-half * beyond_f[d]]


def is_even(axis):
    return lax.axis_index(axis) % 2 == 0


def upper_sides(axis):
    even = is_even(axis)
    return even, jnp.logical_not(even)


def sign_of(upper):
    return jnp.where(upper, 1.0, -1.0).astype(jnp.float32)


def plane_tile(ref, c, yt, k):
    col = pl.ds(k * LANES, LANES)
    if ref.shape[1] == ROWS:
        return ref[2 * c + yt, :, col]
    return ref[c, pl.ds(yt * ROWS, ROWS), col]


def tile_of(ref, index):
    def get(c, yt, k):
        return ref[(c, *index, pl.ds(yt * ROWS, ROWS), pl.ds(k * LANES, LANES))]
    return get


def sides_kernel(field, base, z_even, z_odd, y_even, y_odd, f_all, b_all, sems):
    nz, ny, nx = field.shape[1:]
    even_y, even_z = is_even("cross"), is_even("span")

    def copies(z):
        return (pltpu.make_async_copy(field.at[:, z], f_all.at[:, z], sems.at[0, z]),
                pltpu.make_async_copy(base.at[:, z], b_all.at[:, z], sems.at[1, z]))

    def start(z, carry):
        for one in copies(z):
            one.start()
        return carry

    def rows(z, carry):
        for one in copies(z):
            one.wait()
        for src, off, n in ((f_all, 0, 4), (b_all, 4, 3)):
            for c in range(n):
                for k in range(nx // LANES):
                    col = pl.ds(k * LANES, LANES)
                    lo, hi = src[c, z, pl.ds(0, 1), col], src[c, z, pl.ds(ny - 1, 1), col]
                    y_even[c + off, z, pl.ds(k, 1), :] = jnp.where(even_y, hi, lo)
                    y_odd[c + off, z, pl.ds(k, 1), :] = jnp.where(even_y, lo, hi)
        return carry

    lax.fori_loop(0, nz, start, 0)
    lax.fori_loop(0, nz, rows, 0)
    z_up = jnp.where(even_z, nz - 1, 0)
    for out, z in ((z_even, z_up), (z_odd, nz - 1 - z_up)):
        out[0:4] = f_all[:, z]
        out[4:7] = b_all[:, z]


def f32(*shape):
    return jax.ShapeDtypeStruct(shape, jnp.float32)


def call(kernel, name, out_shape, in_specs, out_specs, scratch=(), mib=6, cost=None, aliases=None):
    return pl.pallas_call(
        kernel,
        out_shape=out_shape,
        in_specs=in_specs,
        out_specs=out_specs,
        scratch_shapes=list(scratch),
        compiler_params=pltpu.CompilerParams(vmem_limit_bytes=mib * 2**20),
        cost_estimate=cost,
        input_output_aliases=aliases or {},
        name=name,
    )


IN_VMEM = pl.BlockSpec(memory_space=VMEM)
IN_SMEM = pl.BlockSpec(memory_space=SMEM)
ANYWHERE = pl.BlockSpec(memory_space=pl.ANY)
FREE = pl.CostEstimate(flops=0, bytes_accessed=0, transcendentals=0)
IN_HBM = pl.BlockSpec(memory_space=pltpu.HBM)


def outer_sides(field, base):
    _, nz, ny, nx = field.shape
    outs = [f32(7, ny, nx)] * 2 + [f32(7, nz, nx // LANES, LANES)] * 2
    scratch = [VMEM(field.shape, jnp.float32), VMEM(base.shape, jnp.float32), pltpu.SemaphoreType.DMA((2, nz))]
    return call(sides_kernel, "outer_sides", outs, [ANYWHERE] * 2, [IN_VMEM] * 4, scratch, mib=52)(field, base)


def gather_tiles(cells, blocks, normals, rows):
    ny, nx = cells[0].shape[2:]
    per_row = nx // LANES
    row_bits, y_bits = per_row.bit_length() - 1, ny.bit_length() - 1
    sub = lax.broadcasted_iota(jnp.int32, (ROWS, LANES), 0)

    def gather(group, carry):
        kept = jnp.zeros((ROWS, LANES), jnp.float32)
        for j in range(ROWS):
            t = group * ROWS + j
            b = blocks[t]
            z = lax.shift_right_logical(b, row_bits + y_bits)
            y = lax.shift_right_logical(b, row_bits) & (ny - 1)
            near = pl.ds(pl.multiple_of(y & (ny - ROWS), ROWS), ROWS)
            col = pl.ds(pl.multiple_of((b & (per_row - 1)) * LANES, LANES), LANES)
            total = 0.0
            for c in range(4):
                run = cells[0][c, z, near, col]
                for more in cells[1:]:
                    run = run + more[c, z, near, col]
                total = total + normals[c, t] * run
            total = pltpu.roll(total, (j + ROWS - (y & (ROWS - 1))) & (ROWS - 1), 0)
            kept = jnp.where(sub == j, total, kept)
        rows[pl.ds(pl.multiple_of(group * ROWS, ROWS), ROWS), :] = TIME_STEP * kept
        return carry

    lax.fori_loop(0, rows.shape[0] // ROWS, gather, 0)


def put_rows(cells, even, rows_even, rows_odd, z, at):
    ny, nx = cells.shape[-2:]
    for c in range(4):
        for k in range(nx // LANES):
            col = pl.ds(k * LANES, LANES)
            one, two = rows_even[c, z, pl.ds(k, 1), :], rows_odd[c, z, pl.ds(k, 1), :]
            cells[(c, *at, pl.ds(0, 1), col)] = jnp.where(even, two, one)
            cells[(c, *at, pl.ds(ny - 1, 1), col)] = jnp.where(even, one, two)


def stencil_kernel(step, *refs):
    if step == 0:
        field, base, new, p_lo, p_hi, r_lo, r_hi, slope_ref = refs
    elif step < STEPS - 1:
        field, base, slope_ref, new, p_lo, p_hi, r_lo, r_hi = refs
    else:
        field, base, slope_ref, before, new, p_lo, p_hi, r_lo, r_hi, both = refs
    nz, ny, nx = field.shape[1:]

    def outside(c, yt, k):
        return jnp.zeros((ROWS, LANES), jnp.float32)

    def do(z, lower, upper):
        def at(yt, k):
            return (z, pl.ds(yt * ROWS, ROWS), pl.ds(k * LANES, LANES))

        def beside(ref, there, off):
            return tile_of(ref, (z + off,)) if there else outside

        def put(c, yt, k, value):
            new[(c, *at(yt, k))] = value
            if yt == 0:
                r_lo[c, z, pl.ds(k, 1), :] = value[:1]
            if yt == ny // ROWS - 1:
                r_hi[c, z, pl.ds(k, 1), :] = value[ROWS - 1:]
            if step == STEPS - 1:
                both[(c, *at(yt, k))] = before[(c, *at(yt, k))] + field[(c, *at(yt, k))]

        b_lo, b_hi = beside(base, lower, -1), beside(base, upper, 1)

        def slopes(flows, yt, k):
            if step > 0:
                return [[slope_ref[(3 * i + j, *at(yt, k))] for j in range(3)] for i in range(3)]
            found = []
            for along in (lambda j: flows[j].along_x(yt, k), lambda j: flows[j].along_y(yt, k), lambda j: (b_hi(j, yt, k), b_lo(j, yt, k))):
                sides = [along(j) for j in range(3)]
                found.append([hi - lo for hi, lo in sides])
            return found

        def put_slopes(yt, k, slope):
            for i in range(3):
                for j in range(3):
                    slope_ref[(3 * i + j, *at(yt, k))] = slope[i][j]

        plane(tile_of(field, (z,)), beside(field, lower, -1), beside(field, upper, 1), slopes, tile_of(base, (z,)), put, ny, nx,
              put_slopes if step == 0 else None)

    def body(z, carry):
        do(z, True, True)
        return carry

    do(0, False, True)
    p_lo[...] = new[:, 0]
    lax.fori_loop(1, nz - 1, body, 0)
    do(nz - 1, True, False)
    p_hi[...] = new[:, nz - 1]


def stencil(step, field, base, slopes=None, before=None):
    _, nz, ny, nx = field.shape
    outs = [f32(*field.shape)] + [f32(4, ny, nx)] * 2 + [f32(4, nz, nx // LANES, LANES)] * 2
    args = [field, base]
    if step == 0:
        outs.append(f32(9, nz, ny, nx))
    else:
        args.append(slopes)
    if step == STEPS - 1:
        args.append(before)
        outs.append(f32(*field.shape))
    ins = [IN_VMEM] * len(args)
    return call(functools.partial(stencil_kernel, step), "stencil", outs, ins, [IN_VMEM] * len(outs), cost=FREE)(*args)


def row_fix_kernel(after, p_lo, p_hi, r_lo, r_hi, own_e, own_o, base_e, base_o, far_e, far_o, fbase_e, fbase_o,
                   q_e, q_o, s_e, s_o):
    del after
    nz = r_lo.shape[1]
    uppers = upper_sides("cross")

    def body(z, carry):
        for upper, own, base, far, fbase, s in ((uppers[0], own_e, base_e, far_e, fbase_e, s_e),
                                                (uppers[1], own_o, base_o, far_o, fbase_o, s_o)):
            add = fix(sign_of(upper), 1, [own[c, z] for c in range(3)], [base[4 + c, z] for c in range(3)],
                      [far[c, z] for c in range(4)], [fbase[4 + c, z] for c in range(3)])
            for c in range(4):
                s[c, z] = jnp.where(upper, r_hi[c, z], r_lo[c, z]) + add[c]
        return carry

    lax.fori_loop(0, nz, body, 0)
    for upper, q in zip(upper_sides("span"), (q_e, q_o)):
        for c in range(4):
            q[c] = jnp.where(upper, p_hi[c], p_lo[c])
        put_rows(q, uppers[0], s_e, s_o, jnp.where(upper, nz - 1, 0), ())


def row_fix(after, planes, rows, own_rows, base_rows, far_rows, far_base_rows):
    outs = [f32(*planes[0].shape)] * 2 + [f32(*rows[0].shape)] * 2
    cost = FREE
    return call(row_fix_kernel, "row_fix", outs, [ANYWHERE] + [IN_VMEM] * 12, [IN_VMEM] * 4, cost=cost)(
        after, *planes, *rows, *own_rows, *base_rows, *far_rows, *far_base_rows)


def far_fix_kernel(got_e, got_o, far_e, far_o, fbase_e, fbase_o, old_e, old_o, base_e, base_o, next_e, next_o):
    _, ny, nx = got_e.shape
    span, ends = lax.axis_index("span"), lax.axis_size("span") - 1
    uppers = upper_sides("span")
    sides = (
        (uppers[0], got_e, far_e, fbase_e, old_e, base_e, next_e),
        (uppers[1], got_o, far_o, fbase_o, old_o, base_o, next_o),
    )
    for upper, got, far, fbase, old, base, nxt in sides:
        there = span != jnp.where(upper, ends, 0)
        for yt in range(ny // ROWS):
            for k in range(nx // LANES):
                tile = (pl.ds(yt * ROWS, ROWS), pl.ds(k * LANES, LANES))
                back = fix(-sign_of(upper), 2, [far[(c, *tile)] for c in range(3)], [fbase[(4 + c, *tile)] for c in range(3)],
                           [old[(c, *tile)] for c in range(4)], [base[(4 + c, *tile)] for c in range(3)])
                for c in range(4):
                    nxt[(c, *tile)] = jnp.where(there, got[(c, *tile)] + back[c], 0.0)


def far_fix(got, far, far_base, old, base):
    args = [*got, *far, *far_base, *old, *base]
    return call(far_fix_kernel, "far_fix", [f32(*got[0].shape)] * 2, [IN_VMEM] * len(args), [IN_VMEM] * 2, cost=FREE)(*args)


def plane_fix_kernel(big, q_e, q_o, s_e, s_o, own_e, own_o, base_e, base_o, fbase_e, fbase_o, far_e, far_o,
                     whole, out_e, out_o, row_e, row_o):
    del big
    _, ny, nx = q_e.shape
    nz = s_e.shape[1]
    even_y = is_even("cross")
    uppers = upper_sides("span")
    sides = (
        (uppers[0], q_e, own_e, base_e, fbase_e, far_e, out_e),
        (uppers[1], q_o, own_o, base_o, fbase_o, far_o, out_o),
    )
    row_e[...] = s_e[...]
    row_o[...] = s_o[...]
    for upper, q, own, base, fbase, far, out in sides:
        for yt in range(ny // ROWS):
            for k in range(nx // LANES):
                tile = (pl.ds(yt * ROWS, ROWS), pl.ds(k * LANES, LANES))
                add = fix(sign_of(upper), 2, [own[(c, *tile)] for c in range(3)], [base[(4 + c, *tile)] for c in range(3)],
                          [far[(c, *tile)] for c in range(4)], [fbase[(4 + c, *tile)] for c in range(3)])
                for c in range(4):
                    out[(c, *tile)] = q[(c, *tile)] + add[c]
        z = jnp.where(upper, nz - 1, 0)
        whole[:, z] = out[...]
        for c in range(4):
            for k in range(nx // LANES):
                col = pl.ds(k * LANES, LANES)
                lo, hi = out[c, pl.ds(0, 1), col], out[c, pl.ds(ny - 1, 1), col]
                row_e[c, z, pl.ds(k, 1), :] = jnp.where(even_y, hi, lo)
                row_o[c, z, pl.ds(k, 1), :] = jnp.where(even_y, lo, hi)

    def body(z, carry):
        put_rows(whole, even_y, s_e, s_o, z, (z,))
        return carry

    lax.fori_loop(1, nz - 1, body, 0)


def plane_fix(last, field, planes, rows, own, base, far_base, far):
    outs = [f32(*planes[0].shape)] * 2 + [f32(*rows[0].shape)] * 2
    scratch = []
    if last:
        outs, scratch = [], [VMEM(o.shape, o.dtype) for o in outs]
    outs = [f32(*field.shape)] + outs
    args = [field, *planes, *rows, *own, *base, *far_base, *far]
    return call(plane_fix_kernel, "plane_fix", outs, [IN_VMEM] * len(args), [IN_VMEM] * len(outs), scratch,
                cost=FREE, aliases={0: 0})(*args)


def finish_kernel(field, both, blocks, normals, sections, new, table, rows, sem):
    out = pltpu.make_async_copy(field, new, sem)
    out.start()
    gather_tiles((both, field), blocks, normals, rows)
    labels = lax.broadcasted_iota(jnp.int32, (table.shape[0], rows.shape[0]), 0)
    onehot = (labels == sections[...]).astype(jnp.float32)
    table[...] = jnp.dot(onehot, rows[...], precision=lax.Precision.HIGHEST, preferred_element_type=jnp.float32)
    out.wait()


def finish(field, both, blocks, normals, sections, total):
    scratch = [VMEM((blocks.shape[0], LANES), jnp.float32), pltpu.SemaphoreType.DMA]
    return call(finish_kernel, "finish", [f32(*field.shape), f32(total, LANES)],
                [IN_VMEM] * 2 + [IN_SMEM] * 2 + [IN_VMEM], [ANYWHERE, IN_VMEM], scratch)(
        field, both, blocks, normals, sections)


def swap(sides, axis):
    even, odd = sides
    count = lax.axis_size(axis)
    return [lax.ppermute(even, axis, [(i, i ^ 1) for i in range(count)]),
            lax.ppermute(odd, axis, [(i, ((i + 1) ^ 1) - 1) for i in range(1, count - 1)])]


def local(adjoint_start, base_flow, wall_blocks, tile_sections, tile_normals, modes):
    sides = outer_sides(adjoint_start, base_flow)
    own = base_planes = sides[:2]
    own_rows = base_rows = sides[2:]
    far_rows = far_base_rows = swap(base_rows, "cross")
    far = far_base = swap(base_planes, "span")
    field, before, slopes, both = adjoint_start, None, None, None
    old, got, after = None, None, base_planes[0]
    for step in range(STEPS):
        fresh, *edge = stencil(step, field, base_flow, slopes, before)
        if step == 0:
            slopes = edge.pop()
        else:
            far = far_fix(got, far, far_base, old, base_planes)
            after = far[0]
            if step == STEPS - 1:
                both = edge.pop()
        *planes, row_lo, row_hi = row_fix(after, edge[:2], edge[2:], own_rows, base_rows, far_rows, far_base_rows)
        if step < STEPS - 1:
            got = swap(planes, "span")
        before, old = field, own
        field, *out = plane_fix(step == STEPS - 1, fresh, planes, (row_lo, row_hi), own, base_planes, far_base, far)
        own, own_rows = out[:2], out[2:]
        if step < STEPS - 1:
            far_rows = swap(own_rows, "cross")
    sections = tile_sections.reshape(1, -1)
    devices = lax.axis_size("cross") * lax.axis_size("span")
    field, table = finish(field, both, wall_blocks, tile_normals, sections, devices * SEC_DEV)
    parts = lax.all_to_all(table.reshape(devices, SEC_DEV, LANES), ("span", "cross"), 0, 0, tiled=True)
    section_sum = jnp.sum(parts, axis=0)
    modal_load = jnp.dot(section_sum, modes, precision=lax.Precision.HIGHEST, preferred_element_type=jnp.float32)
    return field, modal_load


def solution(mesh):
    placed = (
        P(None, "span", "cross", None),
        P(None, "span", "cross", None),
        P(("span", "cross")),
        P(("span", "cross"), None),
        P(None, ("span", "cross")),
        P(),
    )
    return jax.shard_map(
        local,
        mesh=mesh,
        in_specs=placed,
        out_specs=(P(None, "span", "cross", None), P(("span", "cross"), None)),
        check_vma=False,
    )
```

time: 400 us -> 95.9 us (0.24)
  the two profiles are of different devices: /device:TPU:6 before, /device:TPU:1 now
where the time goes in v3:
time: 95.9 us; the launch traced here: 95.6 us
  blocking collectives  29.7 us (31%)
  Pallas kernels  25.6 us (27%)
  starting transfers between devices  24.2 us (25%)
  waiting for transfers between devices  11.9 us (12%)
  local copies, waits for them, and re-layouts  2.37 us (2%)
    all_to_all x1, blocking collectives, local(): lax.all_to_all(table.reshape(devices, SEC_DEV, LANES), ('span', 'cross'),...  29.7 us
    ppermute x6, starting transfers between devices, swap(): lax.ppermute(odd, axis, [(i, (i + 1 ^ 1) - 1) for i in range(1, count - 1)])  14.7 us
    pallas_call x3, Pallas kernels, stencil(): call(functools.partial(stencil_kernel, step), 'stencil', outs, ins, [IN_V...  14.5 us
    ppermute x6, waiting for transfers between devices, swap(): lax.ppermute(even, axis, [(i, i ^ 1) for i in range(count)])  11.9 us
    ppermute x6, starting transfers between devices, swap(): lax.ppermute(even, axis, [(i, i ^ 1) for i in range(count)])  9.53 us
    pallas_call x1, Pallas kernels, finish(): call(finish_kernel, 'finish', [f32(*field.shape), f32(total, LANES)], [IN...  4.19 us
    pallas_call x1, Pallas kernels, outer_sides(): call(sides_kernel, 'outer_sides', outs, [ANYWHERE] * 2, [IN_VMEM] * 4, sc...  3.63 us
    unnamed x12, local copies, waits for them, and re-layouts  2.37 us
  transfers between devices with their start and end apart: 12, of which 1 were waited for; matrix products, arithmetic and copies ran while one was open for 0% of the time, Pallas kernels for 17%

profile of v3, /device:TPU:1, one launch (start us, length us, event | category | flops | bytes accessed | tf_op | source)
XLA Modules:
  0.0 95.6 jit_solution(493865276810506274)
XLA Ops:
  0.7 3.6 %outer_sides.1 = (f32[7,16,1024]{2,1,0:T(8,128)S(1)}, f32[7,16,1024]{2,1,0:T(8,128)S(1)}, f32[7,16,8,128]{3,2,1,0:T(8,128)S(1)}, f32[7,16,8,128]{3,2,1,0:T(8,128)S(1)}) custom-call(f32[4,16,16,1024]{3,2,1,0:T(8,128)} %field.1, f32[3,16,16,1024]{3,2,1,0:T(8,128)} %refs_1_.5), custom_call_target="tpu_custom_call" | custom-call | tf_op jit(solution)/shard_map/outer_sides/pallas_call | solution.py:191
  4.3 1.5 %collective-permute-start = (f32[7,16,8,128]{3,2,1,0:T(8,128)S(1)}, f32[7,16,8,128]{3,2,1,0:T(8,128)S(1)}, u32[]{:S(2)}, u32[]{:S(2)}) collective-permute-start(f32[7,16,8,128]{3,2,1,0:T(8,128)S(1)} %get-tuple-element.57.own_e.base_e), channel_id=1, source_target_pairs={{0,1},{1,0},{2,3},{3,2},{4,5},{5,4},{6,7},{7,6},{8,9},{9,8},{10,11... | collective-permute-start | bytes 1376264 | tf_op jit(solution)/shard_map/ppermute | solution.py:427
  5.8 3.5 %collective-permute-start.1 = (f32[7,16,8,128]{3,2,1,0:T(8,128)S(1)}, f32[7,16,8,128]{3,2,1,0:T(8,128)S(1)}, u32[]{:S(2)}, u32[]{:S(2)}) collective-permute-start(f32[7,16,8,128]{3,2,1,0:T(8,128)S(1)} %get-tuple-element.58.own_o.base_o), channel_id=1, source_target_pairs={{1,2},{2,1},{3,4},{4,3},{5,6},{6,5},{7,8},{8,7},{9,10},{10,9},{11,... | collective-permute-start | bytes 1376264 | tf_op jit(solution)/shard_map/ppermute | solution.py:428
  9.3 0.7 collective-permute-start.3
  10.0 5.3 %collective-permute-start.2 = (f32[7,16,1024]{2,1,0:T(8,128)S(1)}, f32[7,16,1024]{2,1,0:T(8,128)S(1)}, u32[]{:S(2)}, u32[]{:S(2)}) collective-permute-start(f32[7,16,1024]{2,1,0:T(8,128)S(1)} %get-tuple-element.52.after.own_e.base_e.old_e), channel_id=1, source_target_pairs={{0,16},{16,0},{32,48},{48,32},{64,80},{80,64},{96,112},{112,96},{1... | collective-permute-start | bytes 1376264 | tf_op jit(solution)/shard_map/ppermute | solution.py:427
  15.3 2.2 %copy-done.2 = f32[4,16,16,1024]{3,2,1,0:T(8,128)S(1)} copy-done((f32[4,16,16,1024]{3,2,1,0:T(8,128)S(1)}, f32[4,16,16,1024]{3,2,1,0:T(8,128)}, u32[]{:S(2)}) %copy-start.2) | copy-done | bytes 4194328
  17.5 5.5 %stencil.3 = (f32[4,16,16,1024]{3,2,1,0:T(8,128)S(1)}, f32[4,16,1024]{2,1,0:T(8,128)S(1)}, f32[4,16,1024]{2,1,0:T(8,128)S(1)}, f32[4,16,8,128]{3,2,1,0:T(8,128)S...) custom-call(f32[4,16,16,1024]{3,2,1,0:T(8,128)S(1)} %copy-done.2, f32[3,16,16,1024]{3,2,1,0:T(8,128)S(1)} %copy-done.1), custom_call_target="tpu_custom_call" | custom-call | tf_op jit(solution)/shard_map/stencil/pallas_call | solution.py:303
  23.0 0.5 row_fix.3
  23.5 0.1 collective-permute-start.4
  23.6 0.7 collective-permute-start.5
  24.3 11.9 %collective-permute-done.2.fbase_e.far_e = f32[7,16,1024]{2,1,0:T(8,128)S(1)} collective-permute-done((f32[7,16,1024]{2,1,0:T(8,128)S(1)}, f32[7,16,1024]{2,1,0:T(8,128)S(1)}, u32[]{:S(2)}, u32[]{:S(2)}) %collective-permute-start.2) | collective-permute-done | bytes 458784 | tf_op jit(solution)/shard_map/ppermute | solution.py:427
  36.2 0.6 plane_fix.3
  36.7 0.1 collective-permute-start.6
  36.8 3.8 %collective-permute-start.7 = (f32[4,16,8,128]{3,2,1,0:T(8,128)S(1)}, f32[4,16,8,128]{3,2,1,0:T(8,128)S(1)}, u32[]{:S(2)}, u32[]{:S(2)}) collective-permute-start(f32[4,16,8,128]{3,2,1,0:T(8,128)S(1)} %get-tuple-element.73.own_o), channel_id=1, source_target_pairs={{1,2},{2,1},{3,4},{4,3},{5,6},{6,5},{7,8},{8,7},{9,10},{10,9},{11,... | collective-permute-start | bytes 786440 | tf_op jit(solution)/shard_map/ppermute | solution.py:428
  40.7 4.3 %stencil.4 = (f32[4,16,16,1024]{3,2,1,0:T(8,128)S(1)}, f32[4,16,1024]{2,1,0:T(8,128)S(1)}, f32[4,16,1024]{2,1,0:T(8,128)S(1)}, f32[4,16,8,128]{3,2,1,0:T(8,128)S(1)}, f32[4,16,8,128]{3,2,1,0:T(8,128)S(1)}) custom-call(f32[4,16,16,1024]{3,2,1,0:T(8,128)S(1)} %get-tuple-element.64.refs_0_.refs_3_, f32[3,16,16,1024]{3,2,1,0:T(8,128)S(1)} %copy-done.1, ...), custom_call_target="tpu_custom_call" | custom-call | tf_op jit(solution)/shard_map/stencil/pallas_call | solution.py:303
  45.0 0.1 far_fix.2
  45.1 0.5 row_fix.4
  45.6 2.5 %collective-permute-start.8 = (f32[4,16,1024]{2,1,0:T(8,128)S(1)}, f32[4,16,1024]{2,1,0:T(8,128)S(1)}, u32[]{:S(2)}, u32[]{:S(2)}) collective-permute-start(f32[4,16,1024]{2,1,0:T(8,128)S(1)} %get-tuple-element.74.q_e), channel_id=1, source_target_pairs={{0,16},{16,0},{32,48},{48,32},{64,80},{80,64},{96,112},{112,96},{1... | collective-permute-start | bytes 786440 | tf_op jit(solution)/shard_map/ppermute | solution.py:427
  48.1 0.7 collective-permute-start.9
  48.8 0.6 plane_fix.4
  49.3 0.1 collective-permute-start.10
  49.4 5.3 %collective-permute-start.11 = (f32[4,16,8,128]{3,2,1,0:T(8,128)S(1)}, f32[4,16,8,128]{3,2,1,0:T(8,128)S(1)}, u32[]{:S(2)}, u32[]{:S(2)}) collective-permute-start(f32[4,16,8,128]{3,2,1,0:T(8,128)S(1)} %get-tuple-element.89.own_o), channel_id=1, source_target_pairs={{1,2},{2,1},{3,4},{4,3},{5,6},{6,5},{7,8},{8,7},{9,10},{10,9},{11,... | collective-permute-start | bytes 786440 | tf_op jit(solution)/shard_map/ppermute | solution.py:428
  54.8 4.7 %stencil.5 = (f32[4,16,16,1024]{3,2,1,0:T(8,128)S(1)}, f32[4,16,1024]{2,1,0:T(8,128)S(1)}, f32[4,16,1024]{2,1,0:T(8,128)S(1)}, f32[4,16,8,128]{3,2,1,0:T(8,128)S...) custom-call(f32[4,16,16,1024]{3,2,1,0:T(8,128)S(1)} %get-tuple-element.81.refs_0_, ...), custom_call_target="tpu_custom_call" | custom-call | tf_op jit(solution)/shard_map/stencil/pallas_call | solution.py:303
  59.5 0.1 far_fix.3
  59.7 0.5 row_fix.5
  60.2 0.5 plane_fix.5.field
  60.7 0.1 copy-done.3
  60.8 0.0 copy-done.5
  60.8 4.2 %finish.1 = (f32[4,16,16,1024]{3,2,1,0:T(8,128)}, f32[256,128]{1,0:T(8,128)S(1)}) custom-call(f32[4,16,16,1024]{3,2,1,0:T(8,128)S(1)} %plane_fix.5.field, f32[4,16,16,1024]{3,2,1,0:T(8,128)S(1)} %get-tuple-element.97.both, s32[256]{0:T(256)S(1)} %copy-done.4, f32[4,256]{1,0:T(4,128)S(1)} %copy-done.3, s32[1,256]{1,0:T(1,128)S(1)} %bitcast.5), custom_call_target="tpu_custom_call" | custom-call | tf_op jit(solution)/shard_map/finish/pallas_call | solution.py:419
  65.0 29.7 %all_to_all.5 = f32[128,2,128]{2,1,0:T(2,128)S(1)} all-to-all(f32[128,2,128]{2,1,0:T(2,128)S(1)} %bitcast.4), channel_id=1, replica_groups=mesh['span'=8,'cross'=16] {'span','cross'}, dimensions={0} | all-to-all | bytes 262144 | tf_op jit(solution)/shard_map/all_to_all | solution.py:459
  94.7 0.1 reduce_sum.9
  94.9 0.7 fusion
  (20 shorter events, 0.1 us)
Async XLA Ops:
  0.6 94.3 %copy-start = (f32[128,128]{1,0:T(8,128)S(1)}, f32[128,128]{1,0:T(8,128)}, u32[]{:S(2)}) copy-start(f32[128,128]{1,0:T(8,128)} %param.11) | copy-start | bytes 196612
  0.6 14.7 %copy-start.1 = (f32[3,16,16,1024]{3,2,1,0:T(8,128)S(1)}, f32[3,16,16,1024]{3,2,1,0:T(8,128)}, u32[]{:S(2)}) copy-start(f32[3,16,16,1024]{3,2,1,0:T(8,128)} %refs_1_.5) | copy-start | bytes 9437188
  4.3 18.7 %collective-permute-start = (f32[7,16,8,128]{3,2,1,0:T(8,128)S(1)}, f32[7,16,8,128]{3,2,1,0:T(8,128)S(1)}, u32[]{:S(2)}, u32[]{:S(2)}) collective-permute-start(f32[7,16,8,128]{3,2,1,0:T(8,128)S(1)} %get-tuple-element.57.own_e.base_e), channel_id=1, source_target_pairs={{0,1},{1,0},{2,3},{3,2},{4,5},{5,4},{6,7},{7,6},{8,9},{9,8},{10,11... | collective-permute-start | bytes 1376264 | tf_op jit(solution)/shard_map/ppermute | solution.py:427
  5.8 17.2 %collective-permute-start.1 = (f32[7,16,8,128]{3,2,1,0:T(8,128)S(1)}, f32[7,16,8,128]{3,2,1,0:T(8,128)S(1)}, u32[]{:S(2)}, u32[]{:S(2)}) collective-permute-start(f32[7,16,8,128]{3,2,1,0:T(8,128)S(1)} %get-tuple-element.58.own_o.base_o), channel_id=1, source_target_pairs={{1,2},{2,1},{3,4},{4,3},{5,6},{6,5},{7,8},{8,7},{9,10},{10,9},{11,... | collective-permute-start | bytes 1376264 | tf_op jit(solution)/shard_map/ppermute | solution.py:428
  9.3 15.0 %collective-permute-start.3 = (f32[7,16,1024]{2,1,0:T(8,128)S(1)}, f32[7,16,1024]{2,1,0:T(8,128)S(1)}, u32[]{:S(2)}, u32[]{:S(2)}) collective-permute-start(f32[7,16,1024]{2,1,0:T(8,128)S(1)} %get-tuple-element.63.own_o.base_o.old_o), channel_id=1, source_target_pairs={{16,32},{32,16},{48,64},{64,48},{80,96},{96,80},{17,33},{33,17},{4... | collective-permute-start | bytes 1376264 | tf_op jit(solution)/shard_map/ppermute | solution.py:428
  10.0 26.1 %collective-permute-start.2 = (f32[7,16,1024]{2,1,0:T(8,128)S(1)}, f32[7,16,1024]{2,1,0:T(8,128)S(1)}, u32[]{:S(2)}, u32[]{:S(2)}) collective-permute-start(f32[7,16,1024]{2,1,0:T(8,128)S(1)} %get-tuple-element.52.after.own_e.base_e.old_e), channel_id=1, source_target_pairs={{0,16},{16,0},{32,48},{48,32},{64,80},{80,64},{96,112},{112,96},{1... | collective-permute-start | bytes 1376264 | tf_op jit(solution)/shard_map/ppermute | solution.py:427
  15.3 2.2 %copy-start.2 = (f32[4,16,16,1024]{3,2,1,0:T(8,128)S(1)}, f32[4,16,16,1024]{3,2,1,0:T(8,128)}, u32[]{:S(2)}) copy-start(f32[4,16,16,1024]{3,2,1,0:T(8,128)} %field.1) | copy-start | bytes 12582916
  23.5 21.5 %collective-permute-start.4 = (f32[4,16,1024]{2,1,0:T(8,128)S(1)}, f32[4,16,1024]{2,1,0:T(8,128)S(1)}, u32[]{:S(2)}, u32[]{:S(2)}) collective-permute-start(f32[4,16,1024]{2,1,0:T(8,128)S(1)} %get-tuple-element.59.q_e), channel_id=1, source_target_pairs={{0,16},{16,0},{32,48},{48,32},{64,80},{80,64},{96,112},{112,96},{1... | collective-permute-start | bytes 786440 | tf_op jit(solution)/shard_map/ppermute | solution.py:427
  23.6 21.4 %collective-permute-start.5 = (f32[4,16,1024]{2,1,0:T(8,128)S(1)}, f32[4,16,1024]{2,1,0:T(8,128)S(1)}, u32[]{:S(2)}, u32[]{:S(2)}) collective-permute-start(f32[4,16,1024]{2,1,0:T(8,128)S(1)} %get-tuple-element.60.q_o), channel_id=1, source_target_pairs={{16,32},{32,16},{48,64},{64,48},{80,96},{96,80},{17,33},{33,17},{4... | collective-permute-start | bytes 786440 | tf_op jit(solution)/shard_map/ppermute | solution.py:428
  36.7 8.4 %collective-permute-start.6 = (f32[4,16,8,128]{3,2,1,0:T(8,128)S(1)}, f32[4,16,8,128]{3,2,1,0:T(8,128)S(1)}, u32[]{:S(2)}, u32[]{:S(2)}) collective-permute-start(f32[4,16,8,128]{3,2,1,0:T(8,128)S(1)} %get-tuple-element.72.own_e), channel_id=1, source_target_pairs={{0,1},{1,0},{2,3},{3,2},{4,5},{5,4},{6,7},{7,6},{8,9},{9,8},{10,11... | collective-permute-start | bytes 786440 | tf_op jit(solution)/shard_map/ppermute | solution.py:427
  36.8 8.3 %collective-permute-start.7 = (f32[4,16,8,128]{3,2,1,0:T(8,128)S(1)}, f32[4,16,8,128]{3,2,1,0:T(8,128)S(1)}, u32[]{:S(2)}, u32[]{:S(2)}) collective-permute-start(f32[4,16,8,128]{3,2,1,0:T(8,128)S(1)} %get-tuple-element.73.own_o), channel_id=1, source_target_pairs={{1,2},{2,1},{3,4},{4,3},{5,6},{6,5},{7,8},{8,7},{9,10},{10,9},{11,... | collective-permute-start | bytes 786440 | tf_op jit(solution)/shard_map/ppermute | solution.py:428
  45.6 13.9 %collective-permute-start.8 = (f32[4,16,1024]{2,1,0:T(8,128)S(1)}, f32[4,16,1024]{2,1,0:T(8,128)S(1)}, u32[]{:S(2)}, u32[]{:S(2)}) collective-permute-start(f32[4,16,1024]{2,1,0:T(8,128)S(1)} %get-tuple-element.74.q_e), channel_id=1, source_target_pairs={{0,16},{16,0},{32,48},{48,32},{64,80},{80,64},{96,112},{112,96},{1... | collective-permute-start | bytes 786440 | tf_op jit(solution)/shard_map/ppermute | solution.py:427
  48.1 11.4 %collective-permute-start.9 = (f32[4,16,1024]{2,1,0:T(8,128)S(1)}, f32[4,16,1024]{2,1,0:T(8,128)S(1)}, u32[]{:S(2)}, u32[]{:S(2)}) collective-permute-start(f32[4,16,1024]{2,1,0:T(8,128)S(1)} %get-tuple-element.75.q_o), channel_id=1, source_target_pairs={{16,32},{32,16},{48,64},{64,48},{80,96},{96,80},{17,33},{33,17},{4... | collective-permute-start | bytes 786440 | tf_op jit(solution)/shard_map/ppermute | solution.py:428
  49.3 10.3 %collective-permute-start.10 = (f32[4,16,8,128]{3,2,1,0:T(8,128)S(1)}, f32[4,16,8,128]{3,2,1,0:T(8,128)S(1)}, u32[]{:S(2)}, u32[]{:S(2)}) collective-permute-start(f32[4,16,8,128]{3,2,1,0:T(8,128)S(1)} %get-tuple-element.88.own_e), channel_id=1, source_target_pairs={{0,1},{1,0},{2,3},{3,2},{4,5},{5,4},{6,7},{7,6},{8,9},{9,8},{10,11... | collective-permute-start | bytes 786440 | tf_op jit(solution)/shard_map/ppermute | solution.py:427
  49.4 10.2 %collective-permute-start.11 = (f32[4,16,8,128]{3,2,1,0:T(8,128)S(1)}, f32[4,16,8,128]{3,2,1,0:T(8,128)S(1)}, u32[]{:S(2)}, u32[]{:S(2)}) collective-permute-start(f32[4,16,8,128]{3,2,1,0:T(8,128)S(1)} %get-tuple-element.89.own_o), channel_id=1, source_target_pairs={{1,2},{2,1},{3,4},{4,3},{5,6},{6,5},{7,8},{8,7},{9,10},{10,9},{11,... | collective-permute-start | bytes 786440 | tf_op jit(solution)/shard_map/ppermute | solution.py:428
  60.1 0.7 copy-start.3
  60.1 0.7 copy-start.4
  60.2 0.7 copy-start.5

commit v4 on v3

--- a/solution.py
+++ b/solution.py
@@ -191,7 +191,7 @@
     return call(sides_kernel, "outer_sides", outs, [ANYWHERE] * 2, [IN_VMEM] * 4, scratch, mib=52)(field, base)
 
 
-def gather_tiles(cells, blocks, normals, rows):
+def gather_tiles(cells, blocks, weights, rows):
     ny, nx = cells[0].shape[2:]
     per_row = nx // LANES
     row_bits, y_bits = per_row.bit_length() - 1, ny.bit_length() - 1
@@ -211,7 +211,7 @@
                 run = cells[0][c, z, near, col]
                 for more in cells[1:]:
                     run = run + more[c, z, near, col]
-                total = total + normals[c, t] * run
+                total = total + weights[c, group, pl.ds(j, 1), :] * run
             total = pltpu.roll(total, (j + ROWS - (y & (ROWS - 1))) & (ROWS - 1), 0)
             kept = jnp.where(sub == j, total, kept)
         rows[pl.ds(pl.multiple_of(group * ROWS, ROWS), ROWS), :] = TIME_STEP * kept
@@ -404,21 +404,43 @@
                 cost=FREE, aliases={0: 0})(*args)
 
 
-def finish_kernel(field, both, blocks, normals, sections, new, table, rows, sem):
-    out = pltpu.make_async_copy(field, new, sem)
-    out.start()
-    gather_tiles((both, field), blocks, normals, rows)
+def spread_kernel(normals, weights):
+    count = normals.shape[1]
+    across = jnp.concatenate([normals[...], jnp.zeros((ROWS - 4, count), jnp.float32)]).T
+    for c in range(4):
+        weights[c] = jnp.broadcast_to(across[:, c:c + 1], (count, LANES)).reshape(count // ROWS, ROWS, LANES)
+
+
+def spread(normals):
+    return call(spread_kernel, "spread", f32(4, normals.shape[1] // ROWS, ROWS, LANES), [IN_VMEM], IN_VMEM, cost=FREE)(normals)
+
+
+def finish_kernel(field, both, blocks, weights, sections, new, table, rows, sems):
+    nz = field.shape[1]
+
+    def out(z):
+        return pltpu.make_async_copy(field.at[:, z], new.at[:, z], sems.at[z])
+
+    for z in range(nz):
+        out(z).start()
+    gather_tiles((both, field), blocks, weights, rows)
     labels = lax.broadcasted_iota(jnp.int32, (table.shape[0], rows.shape[0]), 0)
-    onehot = (labels == sections[...]).astype(jnp.float32)
-    table[...] = jnp.dot(onehot, rows[...], precision=lax.Precision.HIGHEST, preferred_element_type=jnp.float32)
-    out.wait()
-
-
-def finish(field, both, blocks, normals, sections, total):
-    scratch = [VMEM((blocks.shape[0], LANES), jnp.float32), pltpu.SemaphoreType.DMA]
+    onehot = (labels == sections[...]).astype(jnp.float32).astype(jnp.bfloat16)
+    left, parts = rows[...], []
+    for _ in range(3):
+        parts.append(left.astype(jnp.bfloat16))
+        left = left - parts[-1].astype(jnp.float32)
+    sums = jnp.dot(onehot, jnp.concatenate(parts, axis=1), preferred_element_type=jnp.float32)
+    table[...] = sums[:, :LANES] + sums[:, LANES:2 * LANES] + sums[:, 2 * LANES:]
+    for z in range(nz):
+        out(z).wait()
+
+
+def finish(field, both, blocks, weights, sections, total):
+    scratch = [VMEM((blocks.shape[0], LANES), jnp.float32), pltpu.SemaphoreType.DMA((field.shape[1],))]
     return call(finish_kernel, "finish", [f32(*field.shape), f32(total, LANES)],
-                [IN_VMEM] * 2 + [IN_SMEM] * 2 + [IN_VMEM], [ANYWHERE, IN_VMEM], scratch)(
-        field, both, blocks, normals, sections)
+                [IN_VMEM] * 2 + [IN_SMEM] + [IN_VMEM] * 2, [ANYWHERE, IN_VMEM], scratch)(
+        field, both, blocks, weights, sections)
 
 
 def swap(sides, axis):
@@ -455,7 +477,7 @@
             far_rows = swap(own_rows, "cross")
     sections = tile_sections.reshape(1, -1)
     devices = lax.axis_size("cross") * lax.axis_size("span")
-    field, table = finish(field, both, wall_blocks, tile_normals, sections, devices * SEC_DEV)
+    field, table = finish(field, both, wall_blocks, spread(tile_normals), sections, devices * SEC_DEV)
     parts = lax.all_to_all(table.reshape(devices, SEC_DEV, LANES), ("span", "cross"), 0, 0, tiled=True)
     section_sum = jnp.sum(parts, axis=0)
     modal_load = jnp.dot(section_sum, modes, precision=lax.Precision.HIGHEST, preferred_element_type=jnp.float32)

time: 95.9 us -> 93.9 us (0.979)
  waiting for transfers between devices: 11.9 us -> 2.78 us
  starting transfers between devices: 24.2 us -> 31.7 us
  Pallas kernels: 25.6 us -> 24.5 us
    ppermute x6, waiting for transfers between devices: 11.9 us -> 2.77 us  [swap(): lax.ppermute(even, axis, [(i, i ^ 1) for i in range(count)])]
    ppermute x6, starting transfers between devices: 9.53 us -> 16.9 us  [swap(): lax.ppermute(even, axis, [(i, i ^ 1) for i in range(count)])]
    pallas_call x1, Pallas kernels: 4.19 us -> 2.71 us  [finish(): call(finish_kernel, 'finish', [f32(*field.shape), f32(total, LANES)], [IN...]
  transfers between devices with their start and end apart: 12 -> 12, of which waited for: 1 -> 1; matrix products, arithmetic and copies ran while one was open for 0% -> 0% of each run, Pallas kernels for 17% -> 18%
where the time goes in v4:
time: 93.9 us; the launch traced here: 93.6 us
  starting transfers between devices  31.7 us (34%)
  blocking collectives  30.4 us (32%)
  Pallas kernels  24.5 us (26%)
  waiting for transfers between devices  2.78 us (3%)
  local copies, waits for them, and re-layouts  2.37 us (3%)
  between operations  0.94 us (1%)
    all_to_all x1, blocking collectives, local(): lax.all_to_all(table.reshape(devices, SEC_DEV, LANES), ('span', 'cross'),...  30.4 us
    ppermute x6, starting transfers between devices, swap(): lax.ppermute(even, axis, [(i, i ^ 1) for i in range(count)])  16.9 us
    ppermute x6, starting transfers between devices, swap(): lax.ppermute(odd, axis, [(i, (i + 1 ^ 1) - 1) for i in range(1, count - 1)])  14.8 us
    pallas_call x3, Pallas kernels, stencil(): call(functools.partial(stencil_kernel, step), 'stencil', outs, ins, [IN_V...  14.5 us
    pallas_call x1, Pallas kernels, outer_sides(): call(sides_kernel, 'outer_sides', outs, [ANYWHERE] * 2, [IN_VMEM] * 4, sc...  3.63 us
    ppermute x6, waiting for transfers between devices, swap(): lax.ppermute(even, axis, [(i, i ^ 1) for i in range(count)])  2.77 us
    pallas_call x1, Pallas kernels, finish(): call(finish_kernel, 'finish', [f32(*field.shape), f32(total, LANES)], [IN...  2.71 us
    unnamed x12, local copies, waits for them, and re-layouts  2.37 us
  transfers between devices with their start and end apart: 12, of which 1 were waited for; matrix products, arithmetic and copies ran while one was open for 0% of the time, Pallas kernels for 18%

profile of v4, /device:TPU:1, one launch (start us, length us, event | category | flops | bytes accessed | tf_op | source)
XLA Modules:
  0.0 93.6 jit_solution(14261718515471707986)
XLA Ops:
  0.7 3.6 %outer_sides.1 = (f32[7,16,1024]{2,1,0:T(8,128)S(1)}, f32[7,16,1024]{2,1,0:T(8,128)S(1)}, f32[7,16,8,128]{3,2,1,0:T(8,128)S(1)}, f32[7,16,8,128]{3,2,1,0:T(8,128)S(1)}) custom-call(f32[4,16,16,1024]{3,2,1,0:T(8,128)} %field.1, f32[3,16,16,1024]{3,2,1,0:T(8,128)} %refs_1_.5), custom_call_target="tpu_custom_call" | custom-call | tf_op jit(solution)/shard_map/outer_sides/pallas_call | solution.py:191
  4.3 1.5 %collective-permute-start = (f32[7,16,8,128]{3,2,1,0:T(8,128)S(1)}, f32[7,16,8,128]{3,2,1,0:T(8,128)S(1)}, u32[]{:S(2)}, u32[]{:S(2)}) collective-permute-start(f32[7,16,8,128]{3,2,1,0:T(8,128)S(1)} %get-tuple-element.57.own_e.base_e), channel_id=1, source_target_pairs={{0,1},{1,0},{2,3},{3,2},{4,5},{5,4},{6,7},{7,6},{8,9},{9,8},{10,11... | collective-permute-start | bytes 1376264 | tf_op jit(solution)/shard_map/ppermute | solution.py:449
  5.8 3.5 %collective-permute-start.1 = (f32[7,16,8,128]{3,2,1,0:T(8,128)S(1)}, f32[7,16,8,128]{3,2,1,0:T(8,128)S(1)}, u32[]{:S(2)}, u32[]{:S(2)}) collective-permute-start(f32[7,16,8,128]{3,2,1,0:T(8,128)S(1)} %get-tuple-element.58.own_o.base_o), channel_id=1, source_target_pairs={{1,2},{2,1},{3,4},{4,3},{5,6},{6,5},{7,8},{8,7},{9,10},{10,9},{11,... | collective-permute-start | bytes 1376264 | tf_op jit(solution)/shard_map/ppermute | solution.py:450
  9.3 2.8 %collective-permute-start.2 = (f32[7,16,1024]{2,1,0:T(8,128)S(1)}, f32[7,16,1024]{2,1,0:T(8,128)S(1)}, u32[]{:S(2)}, u32[]{:S(2)}) collective-permute-start(f32[7,16,1024]{2,1,0:T(8,128)S(1)} %get-tuple-element.52.after.own_e.base_e.old_e), channel_id=1, source_target_pairs={{0,16},{16,0},{32,48},{48,32},{64,80},{80,64},{96,112},{112,96},{1... | collective-permute-start | bytes 1376264 | tf_op jit(solution)/shard_map/ppermute | solution.py:449
  12.2 0.7 collective-permute-start.3
  12.9 2.2 %copy-done.2 = f32[4,16,16,1024]{3,2,1,0:T(8,128)S(1)} copy-done((f32[4,16,16,1024]{3,2,1,0:T(8,128)S(1)}, f32[4,16,16,1024]{3,2,1,0:T(8,128)}, u32[]{:S(2)}) %copy-start.2) | copy-done | bytes 4194328
  15.0 5.5 %stencil.3 = (f32[4,16,16,1024]{3,2,1,0:T(8,128)S(1)}, f32[4,16,1024]{2,1,0:T(8,128)S(1)}, f32[4,16,1024]{2,1,0:T(8,128)S(1)}, f32[4,16,8,128]{3,2,1,0:T(8,128)S...) custom-call(f32[4,16,16,1024]{3,2,1,0:T(8,128)S(1)} %copy-done.2, f32[3,16,16,1024]{3,2,1,0:T(8,128)S(1)} %copy-done.1), custom_call_target="tpu_custom_call" | custom-call | tf_op jit(solution)/shard_map/stencil/pallas_call | solution.py:303
  20.6 0.5 row_fix.3
  21.0 5.3 %collective-permute-start.4 = (f32[4,16,1024]{2,1,0:T(8,128)S(1)}, f32[4,16,1024]{2,1,0:T(8,128)S(1)}, u32[]{:S(2)}, u32[]{:S(2)}) collective-permute-start(f32[4,16,1024]{2,1,0:T(8,128)S(1)} %get-tuple-element.59.q_e), channel_id=1, source_target_pairs={{0,16},{16,0},{32,48},{48,32},{64,80},{80,64},{96,112},{112,96},{1... | collective-permute-start | bytes 786440 | tf_op jit(solution)/shard_map/ppermute | solution.py:449
  26.3 0.7 collective-permute-start.5
  27.0 0.6 plane_fix.3
  27.6 0.1 collective-permute-start.6
  27.7 3.9 %collective-permute-start.7 = (f32[4,16,8,128]{3,2,1,0:T(8,128)S(1)}, f32[4,16,8,128]{3,2,1,0:T(8,128)S(1)}, u32[]{:S(2)}, u32[]{:S(2)}) collective-permute-start(f32[4,16,8,128]{3,2,1,0:T(8,128)S(1)} %get-tuple-element.73.own_o), channel_id=1, source_target_pairs={{1,2},{2,1},{3,4},{4,3},{5,6},{6,5},{7,8},{8,7},{9,10},{10,9},{11,... | collective-permute-start | bytes 786440 | tf_op jit(solution)/shard_map/ppermute | solution.py:450
  31.6 4.3 %stencil.4 = (f32[4,16,16,1024]{3,2,1,0:T(8,128)S(1)}, f32[4,16,1024]{2,1,0:T(8,128)S(1)}, f32[4,16,1024]{2,1,0:T(8,128)S(1)}, f32[4,16,8,128]{3,2,1,0:T(8,128)S(1)}, f32[4,16,8,128]{3,2,1,0:T(8,128)S(1)}) custom-call(f32[4,16,16,1024]{3,2,1,0:T(8,128)S(1)} %get-tuple-element.64.refs_0_.refs_3_, f32[3,16,16,1024]{3,2,1,0:T(8,128)S(1)} %copy-done.1, ...), custom_call_target="tpu_custom_call" | custom-call | tf_op jit(solution)/shard_map/stencil/pallas_call | solution.py:303
  35.9 2.8 %collective-permute-done.4.got_e = f32[4,16,1024]{2,1,0:T(8,128)S(1)} collective-permute-done((f32[4,16,1024]{2,1,0:T(8,128)S(1)}, f32[4,16,1024]{2,1,0:T(8,128)S(1)}, u32[]{:S(2)}, u32[]{:S(2)}) %collective-permute-start.4) | collective-permute-done | bytes 262176 | tf_op jit(solution)/shard_map/ppermute | solution.py:449
  38.7 0.1 far_fix.2
  38.8 0.5 row_fix.4
  39.3 7.1 %collective-permute-start.8 = (f32[4,16,1024]{2,1,0:T(8,128)S(1)}, f32[4,16,1024]{2,1,0:T(8,128)S(1)}, u32[]{:S(2)}, u32[]{:S(2)}) collective-permute-start(f32[4,16,1024]{2,1,0:T(8,128)S(1)} %get-tuple-element.74.q_e), channel_id=1, source_target_pairs={{0,16},{16,0},{32,48},{48,32},{64,80},{80,64},{96,112},{112,96},{1... | collective-permute-start | bytes 786440 | tf_op jit(solution)/shard_map/ppermute | solution.py:449
  46.4 0.7 collective-permute-start.9
  47.1 0.6 plane_fix.4
  47.7 0.1 collective-permute-start.10
  47.8 5.3 %collective-permute-start.11 = (f32[4,16,8,128]{3,2,1,0:T(8,128)S(1)}, f32[4,16,8,128]{3,2,1,0:T(8,128)S(1)}, u32[]{:S(2)}, u32[]{:S(2)}) collective-permute-start(f32[4,16,8,128]{3,2,1,0:T(8,128)S(1)} %get-tuple-element.89.own_o), channel_id=1, source_target_pairs={{1,2},{2,1},{3,4},{4,3},{5,6},{6,5},{7,8},{8,7},{9,10},{10,9},{11,... | collective-permute-start | bytes 786440 | tf_op jit(solution)/shard_map/ppermute | solution.py:450
  53.1 0.4 spread.1.weights
  53.5 4.7 %stencil.5 = (f32[4,16,16,1024]{3,2,1,0:T(8,128)S(1)}, f32[4,16,1024]{2,1,0:T(8,128)S(1)}, f32[4,16,1024]{2,1,0:T(8,128)S(1)}, f32[4,16,8,128]{3,2,1,0:T(8,128)S...) custom-call(f32[4,16,16,1024]{3,2,1,0:T(8,128)S(1)} %get-tuple-element.81.refs_0_, ...), custom_call_target="tpu_custom_call" | custom-call | tf_op jit(solution)/shard_map/stencil/pallas_call | solution.py:303
  58.2 0.1 far_fix.3
  58.4 0.5 row_fix.5
  58.9 0.5 plane_fix.5.field
  59.4 0.1 copy-done.4
  59.5 2.7 %finish.1 = (f32[4,16,16,1024]{3,2,1,0:T(8,128)}, f32[256,128]{1,0:T(8,128)S(1)}) custom-call(f32[4,16,16,1024]{3,2,1,0:T(8,128)S(1)} %plane_fix.5.field, f32[4,16,16,1024]{3,2,1,0:T(8,128)S(1)} %get-tuple-element.97.both, s32[256]{0:T(256)S(1)} %copy-done.4, f32[4,32,8,128]{3,2,1,0:T(8,128)S(1)} %spread.1.weights, s32[1,256]{1,0:T(1,128)S(1)} %bitcast.5), custom_call_target="tpu_custom_call" | custom-call | tf_op jit(solution)/shard_map/finish/pallas_call | solution.py:441
  62.3 30.4 %all_to_all.5 = f32[128,2,128]{2,1,0:T(2,128)S(1)} all-to-all(f32[128,2,128]{2,1,0:T(2,128)S(1)} %bitcast.4), channel_id=1, replica_groups=mesh['span'=8,'cross'=16] {'span','cross'}, dimensions={0} | all-to-all | bytes 262144 | tf_op jit(solution)/shard_map/all_to_all | solution.py:481
  92.7 0.1 reduce_sum.9
  92.8 0.7 fusion
  (21 shorter events, 0.1 us)
Async XLA Ops:
  0.6 92.2 %copy-start = (f32[128,128]{1,0:T(8,128)S(1)}, f32[128,128]{1,0:T(8,128)}, u32[]{:S(2)}) copy-start(f32[128,128]{1,0:T(8,128)} %param.11) | copy-start | bytes 196612
  0.6 12.2 %copy-start.1 = (f32[3,16,16,1024]{3,2,1,0:T(8,128)S(1)}, f32[3,16,16,1024]{3,2,1,0:T(8,128)}, u32[]{:S(2)}) copy-start(f32[3,16,16,1024]{3,2,1,0:T(8,128)} %refs_1_.5) | copy-start | bytes 9437188
  4.3 16.3 %collective-permute-start = (f32[7,16,8,128]{3,2,1,0:T(8,128)S(1)}, f32[7,16,8,128]{3,2,1,0:T(8,128)S(1)}, u32[]{:S(2)}, u32[]{:S(2)}) collective-permute-start(f32[7,16,8,128]{3,2,1,0:T(8,128)S(1)} %get-tuple-element.57.own_e.base_e), channel_id=1, source_target_pairs={{0,1},{1,0},{2,3},{3,2},{4,5},{5,4},{6,7},{7,6},{8,9},{9,8},{10,11... | collective-permute-start | bytes 1376264 | tf_op jit(solution)/shard_map/ppermute | solution.py:449
  5.8 14.8 %collective-permute-start.1 = (f32[7,16,8,128]{3,2,1,0:T(8,128)S(1)}, f32[7,16,8,128]{3,2,1,0:T(8,128)S(1)}, u32[]{:S(2)}, u32[]{:S(2)}) collective-permute-start(f32[7,16,8,128]{3,2,1,0:T(8,128)S(1)} %get-tuple-element.58.own_o.base_o), channel_id=1, source_target_pairs={{1,2},{2,1},{3,4},{4,3},{5,6},{6,5},{7,8},{8,7},{9,10},{10,9},{11,... | collective-permute-start | bytes 1376264 | tf_op jit(solution)/shard_map/ppermute | solution.py:450
  9.3 17.7 %collective-permute-start.2 = (f32[7,16,1024]{2,1,0:T(8,128)S(1)}, f32[7,16,1024]{2,1,0:T(8,128)S(1)}, u32[]{:S(2)}, u32[]{:S(2)}) collective-permute-start(f32[7,16,1024]{2,1,0:T(8,128)S(1)} %get-tuple-element.52.after.own_e.base_e.old_e), channel_id=1, source_target_pairs={{0,16},{16,0},{32,48},{48,32},{64,80},{80,64},{96,112},{112,96},{1... | collective-permute-start | bytes 1376264 | tf_op jit(solution)/shard_map/ppermute | solution.py:449
  12.2 14.9 %collective-permute-start.3 = (f32[7,16,1024]{2,1,0:T(8,128)S(1)}, f32[7,16,1024]{2,1,0:T(8,128)S(1)}, u32[]{:S(2)}, u32[]{:S(2)}) collective-permute-start(f32[7,16,1024]{2,1,0:T(8,128)S(1)} %get-tuple-element.63.own_o.base_o.old_o), channel_id=1, source_target_pairs={{16,32},{32,16},{48,64},{64,48},{80,96},{96,80},{17,33},{33,17},{4... | collective-permute-start | bytes 1376264 | tf_op jit(solution)/shard_map/ppermute | solution.py:450
  12.9 2.2 %copy-start.2 = (f32[4,16,16,1024]{3,2,1,0:T(8,128)S(1)}, f32[4,16,16,1024]{3,2,1,0:T(8,128)}, u32[]{:S(2)}) copy-start(f32[4,16,16,1024]{3,2,1,0:T(8,128)} %field.1) | copy-start | bytes 12582916
  21.0 17.6 %collective-permute-start.4 = (f32[4,16,1024]{2,1,0:T(8,128)S(1)}, f32[4,16,1024]{2,1,0:T(8,128)S(1)}, u32[]{:S(2)}, u32[]{:S(2)}) collective-permute-start(f32[4,16,1024]{2,1,0:T(8,128)S(1)} %get-tuple-element.59.q_e), channel_id=1, source_target_pairs={{0,16},{16,0},{32,48},{48,32},{64,80},{80,64},{96,112},{112,96},{1... | collective-permute-start | bytes 786440 | tf_op jit(solution)/shard_map/ppermute | solution.py:449
  26.3 12.3 %collective-permute-start.5 = (f32[4,16,1024]{2,1,0:T(8,128)S(1)}, f32[4,16,1024]{2,1,0:T(8,128)S(1)}, u32[]{:S(2)}, u32[]{:S(2)}) collective-permute-start(f32[4,16,1024]{2,1,0:T(8,128)S(1)} %get-tuple-element.60.q_o), channel_id=1, source_target_pairs={{16,32},{32,16},{48,64},{64,48},{80,96},{96,80},{17,33},{33,17},{4... | collective-permute-start | bytes 786440 | tf_op jit(solution)/shard_map/ppermute | solution.py:450
  27.6 11.2 %collective-permute-start.6 = (f32[4,16,8,128]{3,2,1,0:T(8,128)S(1)}, f32[4,16,8,128]{3,2,1,0:T(8,128)S(1)}, u32[]{:S(2)}, u32[]{:S(2)}) collective-permute-start(f32[4,16,8,128]{3,2,1,0:T(8,128)S(1)} %get-tuple-element.72.own_e), channel_id=1, source_target_pairs={{0,1},{1,0},{2,3},{3,2},{4,5},{5,4},{6,7},{7,6},{8,9},{9,8},{10,11... | collective-permute-start | bytes 786440 | tf_op jit(solution)/shard_map/ppermute | solution.py:449
  27.7 11.1 %collective-permute-start.7 = (f32[4,16,8,128]{3,2,1,0:T(8,128)S(1)}, f32[4,16,8,128]{3,2,1,0:T(8,128)S(1)}, u32[]{:S(2)}, u32[]{:S(2)}) collective-permute-start(f32[4,16,8,128]{3,2,1,0:T(8,128)S(1)} %get-tuple-element.73.own_o), channel_id=1, source_target_pairs={{1,2},{2,1},{3,4},{4,3},{5,6},{6,5},{7,8},{8,7},{9,10},{10,9},{11,... | collective-permute-start | bytes 786440 | tf_op jit(solution)/shard_map/ppermute | solution.py:450
  39.3 13.8 %copy-start.3 = (f32[4,256]{1,0:T(4,128)S(1)}, f32[4,256]{1,0:T(4,128)}, u32[]{:S(2)}) copy-start(f32[4,256]{1,0:T(4,128)} %normals.1) | copy-start | bytes 12292
  39.3 18.9 %collective-permute-start.8 = (f32[4,16,1024]{2,1,0:T(8,128)S(1)}, f32[4,16,1024]{2,1,0:T(8,128)S(1)}, u32[]{:S(2)}, u32[]{:S(2)}) collective-permute-start(f32[4,16,1024]{2,1,0:T(8,128)S(1)} %get-tuple-element.74.q_e), channel_id=1, source_target_pairs={{0,16},{16,0},{32,48},{48,32},{64,80},{80,64},{96,112},{112,96},{1... | collective-permute-start | bytes 786440 | tf_op jit(solution)/shard_map/ppermute | solution.py:449
  46.4 11.8 %collective-permute-start.9 = (f32[4,16,1024]{2,1,0:T(8,128)S(1)}, f32[4,16,1024]{2,1,0:T(8,128)S(1)}, u32[]{:S(2)}, u32[]{:S(2)}) collective-permute-start(f32[4,16,1024]{2,1,0:T(8,128)S(1)} %get-tuple-element.75.q_o), channel_id=1, source_target_pairs={{16,32},{32,16},{48,64},{64,48},{80,96},{96,80},{17,33},{33,17},{4... | collective-permute-start | bytes 786440 | tf_op jit(solution)/shard_map/ppermute | solution.py:450
  47.7 10.7 %collective-permute-start.10 = (f32[4,16,8,128]{3,2,1,0:T(8,128)S(1)}, f32[4,16,8,128]{3,2,1,0:T(8,128)S(1)}, u32[]{:S(2)}, u32[]{:S(2)}) collective-permute-start(f32[4,16,8,128]{3,2,1,0:T(8,128)S(1)} %get-tuple-element.88.own_e), channel_id=1, source_target_pairs={{0,1},{1,0},{2,3},{3,2},{4,5},{5,4},{6,7},{7,6},{8,9},{9,8},{10,11... | collective-permute-start | bytes 786440 | tf_op jit(solution)/shard_map/ppermute | solution.py:449
  47.8 10.6 %collective-permute-start.11 = (f32[4,16,8,128]{3,2,1,0:T(8,128)S(1)}, f32[4,16,8,128]{3,2,1,0:T(8,128)S(1)}, u32[]{:S(2)}, u32[]{:S(2)}) collective-permute-start(f32[4,16,8,128]{3,2,1,0:T(8,128)S(1)} %get-tuple-element.89.own_o), channel_id=1, source_target_pairs={{1,2},{2,1},{3,4},{4,3},{5,6},{6,5},{7,8},{8,7},{9,10},{10,9},{11,... | collective-permute-start | bytes 786440 | tf_op jit(solution)/shard_map/ppermute | solution.py:450
  58.8 0.7 copy-start.4
  58.8 0.7 copy-start.5

commit v5 on v4

--- a/solution.py
+++ b/solution.py
@@ -404,6 +404,44 @@
                 cost=FREE, aliases={0: 0})(*args)
 
 
+def last_planes_kernel(big, own_e, own_o, base_e, base_o, fbase_e, fbase_o, far_e, far_o, whole):
+    nz, ny, nx = big.shape[1:]
+    uppers = upper_sides("span")
+    for upper, own, base, fbase, far in ((uppers[0], own_e, base_e, fbase_e, far_e), (uppers[1], own_o, base_o, fbase_o, far_o)):
+        z = jnp.where(upper, nz - 1, 0)
+        for yt in range(ny // ROWS):
+            for k in range(nx // LANES):
+                tile = (pl.ds(yt * ROWS, ROWS), pl.ds(k * LANES, LANES))
+                add = fix(sign_of(upper), 2, [own[(c, *tile)] for c in range(3)], [base[(4 + c, *tile)] for c in range(3)],
+                          [far[(c, *tile)] for c in range(4)], [fbase[(4 + c, *tile)] for c in range(3)])
+                for c in range(4):
+                    whole[(c, z, *tile)] = big[(c, z, *tile)] + add[c]
+
+
+def last_rows_kernel(big, own_e, own_o, base_e, base_o, far_e, far_o, fbase_e, fbase_o, whole):
+    nz, ny, nx = big.shape[1:]
+    uppers = upper_sides("cross")
+
+    def body(z, carry):
+        adds = []
+        for upper, own, base, far, fbase in ((uppers[0], own_e, base_e, far_e, fbase_e), (uppers[1], own_o, base_o, far_o, fbase_o)):
+            adds.append(fix(sign_of(upper), 1, [own[c, z] for c in range(3)], [base[4 + c, z] for c in range(3)],
+                            [far[c, z] for c in range(4)], [fbase[4 + c, z] for c in range(3)]))
+        for c in range(4):
+            lo, hi = jnp.where(uppers[0], adds[1][c], adds[0][c]), jnp.where(uppers[0], adds[0][c], adds[1][c])
+            for k in range(nx // LANES):
+                col = pl.ds(k * LANES, LANES)
+                whole[c, z, pl.ds(0, 1), col] = big[c, z, pl.ds(0, 1), col] + lo[k:k + 1]
+                whole[c, z, pl.ds(ny - 1, 1), col] = big[c, z, pl.ds(ny - 1, 1), col] + hi[k:k + 1]
+        return carry
+
+    lax.fori_loop(0, nz, body, 0)
+
+
+def in_place(kernel, name, *args):
+    return call(kernel, name, f32(*args[0].shape), [IN_VMEM] * len(args), IN_VMEM, cost=FREE, aliases={0: 0})(*args)
+
+
 def spread_kernel(normals, weights):
     count = normals.shape[1]
     across = jnp.concatenate([normals[...], jnp.zeros((ROWS - 4, count), jnp.float32)]).T
@@ -467,6 +505,9 @@
             after = far[0]
             if step == STEPS - 1:
                 both = edge.pop()
+                field = in_place(last_planes_kernel, "last_planes", fresh, *own, *base_planes, *far_base, *far)
+                field = in_place(last_rows_kernel, "last_rows", field, *own_rows, *base_rows, *far_rows, *far_base_rows)
+                break
         *planes, row_lo, row_hi = row_fix(after, edge[:2], edge[2:], own_rows, base_rows, far_rows, far_base_rows)
         if step < STEPS - 1:
             got = swap(planes, "span")

time: 93.9 us -> 96.3 us (1.026)
  Pallas kernels: 24.5 us -> 27.9 us
    pallas_call x0 -> x2, Pallas kernels: none -> 3.54 us  [in_place(): call(kernel, name, f32(*args[0].shape), [IN_VMEM] * len(args), IN_VMEM, c...]
  transfers between devices with their start and end apart: 12 -> 12, of which waited for: 1 -> 1; matrix products, arithmetic and copies ran while one was open for 0% -> 0% of each run, Pallas kernels for 18% -> 19%
where the time goes in v5:
time: 96.3 us; the launch traced here: 96 us
  starting transfers between devices  31.7 us (33%)
  blocking collectives  29.6 us (31%)
  Pallas kernels  27.9 us (29%)
  waiting for transfers between devices  2.78 us (3%)
  local copies, waits for them, and re-layouts  2.22 us (2%)
    all_to_all x1, blocking collectives, local(): lax.all_to_all(table.reshape(devices, SEC_DEV, LANES), ('span', 'cross'),...  29.6 us
    ppermute x6, starting transfers between devices, swap(): lax.ppermute(even, axis, [(i, i ^ 1) for i in range(count)])  16.9 us
    pallas_call x3, Pallas kernels, stencil(): call(functools.partial(stencil_kernel, step), 'stencil', outs, ins, [IN_V...  15.4 us
    ppermute x6, starting transfers between devices, swap(): lax.ppermute(odd, axis, [(i, (i + 1 ^ 1) - 1) for i in range(1, count - 1)])  14.8 us
    pallas_call x1, Pallas kernels, outer_sides(): call(sides_kernel, 'outer_sides', outs, [ANYWHERE] * 2, [IN_VMEM] * 4, sc...  3.63 us
    pallas_call x2, Pallas kernels, in_place(): call(kernel, name, f32(*args[0].shape), [IN_VMEM] * len(args), IN_VMEM, c...  3.54 us
    ppermute x6, waiting for transfers between devices, swap(): lax.ppermute(even, axis, [(i, i ^ 1) for i in range(count)])  2.77 us
    pallas_call x1, Pallas kernels, finish(): call(finish_kernel, 'finish', [f32(*field.shape), f32(total, LANES)], [IN...  2.71 us
  transfers between devices with their start and end apart: 12, of which 1 were waited for; matrix products, arithmetic and copies ran while one was open for 0% of the time, Pallas kernels for 19%

profile of v5, /device:TPU:1, one launch (start us, length us, event | category | flops | bytes accessed | tf_op | source)
XLA Modules:
  0.0 96.0 jit_solution(2393867437991289272)
XLA Ops:
  0.6 0.0 copy-start
  0.7 3.6 %outer_sides.1 = (f32[7,16,1024]{2,1,0:T(8,128)S(1)}, f32[7,16,1024]{2,1,0:T(8,128)S(1)}, f32[7,16,8,128]{3,2,1,0:T(8,128)S(1)}, f32[7,16,8,128]{3,2,1,0:T(8,128)S(1)}) custom-call(f32[4,16,16,1024]{3,2,1,0:T(8,128)} %field.1, f32[3,16,16,1024]{3,2,1,0:T(8,128)} %refs_1_.5), custom_call_target="tpu_custom_call" | custom-call | tf_op jit(solution)/shard_map/outer_sides/pallas_call | solution.py:191
  4.3 1.5 %collective-permute-start = (f32[7,16,8,128]{3,2,1,0:T(8,128)S(1)}, f32[7,16,8,128]{3,2,1,0:T(8,128)S(1)}, u32[]{:S(2)}, u32[]{:S(2)}) collective-permute-start(f32[7,16,8,128]{3,2,1,0:T(8,128)S(1)} %get-tuple-element.49.own_e.base_e), channel_id=1, source_target_pairs={{0,1},{1,0},{2,3},{3,2},{4,5},{5,4},{6,7},{7,6},{8,9},{9,8},{10,11... | collective-permute-start | bytes 1376264 | tf_op jit(solution)/shard_map/ppermute | solution.py:487
  5.8 3.5 %collective-permute-start.1 = (f32[7,16,8,128]{3,2,1,0:T(8,128)S(1)}, f32[7,16,8,128]{3,2,1,0:T(8,128)S(1)}, u32[]{:S(2)}, u32[]{:S(2)}) collective-permute-start(f32[7,16,8,128]{3,2,1,0:T(8,128)S(1)} %get-tuple-element.50.own_o.base_o), channel_id=1, source_target_pairs={{1,2},{2,1},{3,4},{4,3},{5,6},{6,5},{7,8},{8,7},{9,10},{10,9},{11,... | collective-permute-start | bytes 1376264 | tf_op jit(solution)/shard_map/ppermute | solution.py:488
  9.3 2.8 %collective-permute-start.2 = (f32[7,16,1024]{2,1,0:T(8,128)S(1)}, f32[7,16,1024]{2,1,0:T(8,128)S(1)}, u32[]{:S(2)}, u32[]{:S(2)}) collective-permute-start(f32[7,16,1024]{2,1,0:T(8,128)S(1)} %get-tuple-element.44.after.own_e.base_e.old_e), channel_id=1, source_target_pairs={{0,16},{16,0},{32,48},{48,32},{64,80},{80,64},{96,112},{112,96},{1... | collective-permute-start | bytes 1376264 | tf_op jit(solution)/shard_map/ppermute | solution.py:487
  12.2 0.7 collective-permute-start.3
  12.9 2.2 %copy-done.2 = f32[4,16,16,1024]{3,2,1,0:T(8,128)S(1)} copy-done((f32[4,16,16,1024]{3,2,1,0:T(8,128)S(1)}, f32[4,16,16,1024]{3,2,1,0:T(8,128)}, u32[]{:S(2)}) %copy-start.2) | copy-done | bytes 4194328
  15.0 5.5 %stencil.3 = (f32[4,16,16,1024]{3,2,1,0:T(8,128)S(1)}, f32[4,16,1024]{2,1,0:T(8,128)S(1)}, f32[4,16,1024]{2,1,0:T(8,128)S(1)}, f32[4,16,8,128]{3,2,1,0:T(8,128)S...) custom-call(f32[4,16,16,1024]{3,2,1,0:T(8,128)S(1)} %copy-done.2, f32[3,16,16,1024]{3,2,1,0:T(8,128)S(1)} %copy-done.1), custom_call_target="tpu_custom_call" | custom-call | tf_op jit(solution)/shard_map/stencil/pallas_call | solution.py:303
  20.6 0.5 row_fix.2
  21.0 5.3 %collective-permute-start.4 = (f32[4,16,1024]{2,1,0:T(8,128)S(1)}, f32[4,16,1024]{2,1,0:T(8,128)S(1)}, u32[]{:S(2)}, u32[]{:S(2)}) collective-permute-start(f32[4,16,1024]{2,1,0:T(8,128)S(1)} %get-tuple-element.51.q_e), channel_id=1, source_target_pairs={{0,16},{16,0},{32,48},{48,32},{64,80},{80,64},{96,112},{112,96},{1... | collective-permute-start | bytes 786440 | tf_op jit(solution)/shard_map/ppermute | solution.py:487
  26.3 0.7 collective-permute-start.5
  27.0 0.6 plane_fix.2
  27.6 0.1 collective-permute-start.6
  27.7 3.9 %collective-permute-start.7 = (f32[4,16,8,128]{3,2,1,0:T(8,128)S(1)}, f32[4,16,8,128]{3,2,1,0:T(8,128)S(1)}, u32[]{:S(2)}, u32[]{:S(2)}) collective-permute-start(f32[4,16,8,128]{3,2,1,0:T(8,128)S(1)} %get-tuple-element.65.own_o), channel_id=1, source_target_pairs={{1,2},{2,1},{3,4},{4,3},{5,6},{6,5},{7,8},{8,7},{9,10},{10,9},{11,... | collective-permute-start | bytes 786440 | tf_op jit(solution)/shard_map/ppermute | solution.py:488
  31.6 4.3 %stencil.4 = (f32[4,16,16,1024]{3,2,1,0:T(8,128)S(1)}, f32[4,16,1024]{2,1,0:T(8,128)S(1)}, f32[4,16,1024]{2,1,0:T(8,128)S(1)}, f32[4,16,8,128]{3,2,1,0:T(8,128)S(1)}, f32[4,16,8,128]{3,2,1,0:T(8,128)S(1)}) custom-call(f32[4,16,16,1024]{3,2,1,0:T(8,128)S(1)} %get-tuple-element.56.refs_0_.refs_3_, f32[3,16,16,1024]{3,2,1,0:T(8,128)S(1)} %copy-done.1, ...), custom_call_target="tpu_custom_call" | custom-call | tf_op jit(solution)/shard_map/stencil/pallas_call | solution.py:303
  35.9 2.8 %collective-permute-done.4.got_e = f32[4,16,1024]{2,1,0:T(8,128)S(1)} collective-permute-done((f32[4,16,1024]{2,1,0:T(8,128)S(1)}, f32[4,16,1024]{2,1,0:T(8,128)S(1)}, u32[]{:S(2)}, u32[]{:S(2)}) %collective-permute-start.4) | collective-permute-done | bytes 262176 | tf_op jit(solution)/shard_map/ppermute | solution.py:487
  38.7 0.1 far_fix.2
  38.8 0.5 row_fix.3
  39.3 7.1 %collective-permute-start.8 = (f32[4,16,1024]{2,1,0:T(8,128)S(1)}, f32[4,16,1024]{2,1,0:T(8,128)S(1)}, u32[]{:S(2)}, u32[]{:S(2)}) collective-permute-start(f32[4,16,1024]{2,1,0:T(8,128)S(1)} %get-tuple-element.66.q_e), channel_id=1, source_target_pairs={{0,16},{16,0},{32,48},{48,32},{64,80},{80,64},{96,112},{112,96},{1... | collective-permute-start | bytes 786440 | tf_op jit(solution)/shard_map/ppermute | solution.py:487
  46.4 0.7 collective-permute-start.9
  47.1 0.6 plane_fix.3
  47.7 0.1 collective-permute-start.10
  47.8 5.3 %collective-permute-start.11 = (f32[4,16,8,128]{3,2,1,0:T(8,128)S(1)}, f32[4,16,8,128]{3,2,1,0:T(8,128)S(1)}, u32[]{:S(2)}, u32[]{:S(2)}) collective-permute-start(f32[4,16,8,128]{3,2,1,0:T(8,128)S(1)} %get-tuple-element.80.own_o), channel_id=1, source_target_pairs={{1,2},{2,1},{3,4},{4,3},{5,6},{6,5},{7,8},{8,7},{9,10},{10,9},{11,... | collective-permute-start | bytes 786440 | tf_op jit(solution)/shard_map/ppermute | solution.py:488
  53.1 0.4 spread.1.weights
  53.5 5.6 %stencil.5 = (f32[4,16,16,1024]{3,2,1,0:T(8,128)S(1)}, f32[4,16,1024]{2,1,0:T(8,128)}, f32[4,16,1024]{2,1,0:T(8,128)}, f32[4,16,8,128]{3,2,1,0:T(8,128)}, f32[4,...) custom-call(f32[4,16,16,1024]{3,2,1,0:T(8,128)S(1)} %get-tuple-element.73.refs_0_, ...), custom_call_target="tpu_custom_call" | custom-call | tf_op jit(solution)/shard_map/stencil/pallas_call | solution.py:303
  59.1 0.1 far_fix.3
  59.2 0.2 last_planes.1.big
  59.4 3.3 %last_rows.1.field = f32[4,16,16,1024]{3,2,1,0:T(8,128)S(1)} custom-call(f32[4,16,16,1024]{3,2,1,0:T(8,128)S(1)} %last_planes.1.big, f32[4,16,8,128]{3,2,1,0:T(8,128)S(1)} %get-tuple-element.79.own_e, f32[4,16,8,128]{3,2,1,0:T(8,128)S(1)} %get-tuple-element.80.own_o, ...), custom_call_target="tpu_custom_call", output_to_operand_aliasing={{}: (0, {})} | custom-call | tf_op jit(solution)/shard_map/last_rows/pallas_call | solution.py:442
  62.8 2.7 %finish.1 = (f32[4,16,16,1024]{3,2,1,0:T(8,128)}, f32[256,128]{1,0:T(8,128)S(1)}) custom-call(f32[4,16,16,1024]{3,2,1,0:T(8,128)S(1)} %last_rows.1.field, f32[4,16,16,1024]{3,2,1,0:T(8,128)S(1)} %get-tuple-element.81.both, s32[256]{0:T(256)S(1)} %copy-done.4, f32[4,32,8,128]{3,2,1,0:T(8,128)S(1)} %spread.1.weights, s32[1,256]{1,0:T(1,128)S(1)} %bitcast.5), custom_call_target="tpu_custom_call" | custom-call | tf_op jit(solution)/shard_map/finish/pallas_call | solution.py:479
  65.5 29.6 %all_to_all.5 = f32[128,2,128]{2,1,0:T(2,128)S(1)} all-to-all(f32[128,2,128]{2,1,0:T(2,128)S(1)} %bitcast.4), channel_id=1, replica_groups=mesh['span'=8,'cross'=16] {'span','cross'}, dimensions={0} | all-to-all | bytes 262144 | tf_op jit(solution)/shard_map/all_to_all | solution.py:522
  95.1 0.1 reduce_sum.9
  95.2 0.7 fusion
  (21 shorter events, 0.1 us)
Async XLA Ops:
  0.6 94.6 %copy-start = (f32[128,128]{1,0:T(8,128)S(1)}, f32[128,128]{1,0:T(8,128)}, u32[]{:S(2)}) copy-start(f32[128,128]{1,0:T(8,128)} %param.11) | copy-start | bytes 196612
  0.6 12.2 %copy-start.1 = (f32[3,16,16,1024]{3,2,1,0:T(8,128)S(1)}, f32[3,16,16,1024]{3,2,1,0:T(8,128)}, u32[]{:S(2)}) copy-start(f32[3,16,16,1024]{3,2,1,0:T(8,128)} %refs_1_.5) | copy-start | bytes 9437188
  4.3 16.3 %collective-permute-start = (f32[7,16,8,128]{3,2,1,0:T(8,128)S(1)}, f32[7,16,8,128]{3,2,1,0:T(8,128)S(1)}, u32[]{:S(2)}, u32[]{:S(2)}) collective-permute-start(f32[7,16,8,128]{3,2,1,0:T(8,128)S(1)} %get-tuple-element.49.own_e.base_e), channel_id=1, source_target_pairs={{0,1},{1,0},{2,3},{3,2},{4,5},{5,4},{6,7},{7,6},{8,9},{9,8},{10,11... | collective-permute-start | bytes 1376264 | tf_op jit(solution)/shard_map/ppermute | solution.py:487
  5.8 14.8 %collective-permute-start.1 = (f32[7,16,8,128]{3,2,1,0:T(8,128)S(1)}, f32[7,16,8,128]{3,2,1,0:T(8,128)S(1)}, u32[]{:S(2)}, u32[]{:S(2)}) collective-permute-start(f32[7,16,8,128]{3,2,1,0:T(8,128)S(1)} %get-tuple-element.50.own_o.base_o), channel_id=1, source_target_pairs={{1,2},{2,1},{3,4},{4,3},{5,6},{6,5},{7,8},{8,7},{9,10},{10,9},{11,... | collective-permute-start | bytes 1376264 | tf_op jit(solution)/shard_map/ppermute | solution.py:488
  9.3 17.7 %collective-permute-start.2 = (f32[7,16,1024]{2,1,0:T(8,128)S(1)}, f32[7,16,1024]{2,1,0:T(8,128)S(1)}, u32[]{:S(2)}, u32[]{:S(2)}) collective-permute-start(f32[7,16,1024]{2,1,0:T(8,128)S(1)} %get-tuple-element.44.after.own_e.base_e.old_e), channel_id=1, source_target_pairs={{0,16},{16,0},{32,48},{48,32},{64,80},{80,64},{96,112},{112,96},{1... | collective-permute-start | bytes 1376264 | tf_op jit(solution)/shard_map/ppermute | solution.py:487
  12.2 14.9 %collective-permute-start.3 = (f32[7,16,1024]{2,1,0:T(8,128)S(1)}, f32[7,16,1024]{2,1,0:T(8,128)S(1)}, u32[]{:S(2)}, u32[]{:S(2)}) collective-permute-start(f32[7,16,1024]{2,1,0:T(8,128)S(1)} %get-tuple-element.55.own_o.base_o.old_o), channel_id=1, source_target_pairs={{16,32},{32,16},{48,64},{64,48},{80,96},{96,80},{17,33},{33,17},{4... | collective-permute-start | bytes 1376264 | tf_op jit(solution)/shard_map/ppermute | solution.py:488
  12.9 2.2 %copy-start.2 = (f32[4,16,16,1024]{3,2,1,0:T(8,128)S(1)}, f32[4,16,16,1024]{3,2,1,0:T(8,128)}, u32[]{:S(2)}) copy-start(f32[4,16,16,1024]{3,2,1,0:T(8,128)} %field.1) | copy-start | bytes 12582916
  21.0 17.6 %collective-permute-start.4 = (f32[4,16,1024]{2,1,0:T(8,128)S(1)}, f32[4,16,1024]{2,1,0:T(8,128)S(1)}, u32[]{:S(2)}, u32[]{:S(2)}) collective-permute-start(f32[4,16,1024]{2,1,0:T(8,128)S(1)} %get-tuple-element.51.q_e), channel_id=1, source_target_pairs={{0,16},{16,0},{32,48},{48,32},{64,80},{80,64},{96,112},{112,96},{1... | collective-permute-start | bytes 786440 | tf_op jit(solution)/shard_map/ppermute | solution.py:487
  26.3 12.3 %collective-permute-start.5 = (f32[4,16,1024]{2,1,0:T(8,128)S(1)}, f32[4,16,1024]{2,1,0:T(8,128)S(1)}, u32[]{:S(2)}, u32[]{:S(2)}) collective-permute-start(f32[4,16,1024]{2,1,0:T(8,128)S(1)} %get-tuple-element.52.q_o), channel_id=1, source_target_pairs={{16,32},{32,16},{48,64},{64,48},{80,96},{96,80},{17,33},{33,17},{4... | collective-permute-start | bytes 786440 | tf_op jit(solution)/shard_map/ppermute | solution.py:488
  27.6 11.2 %collective-permute-start.6 = (f32[4,16,8,128]{3,2,1,0:T(8,128)S(1)}, f32[4,16,8,128]{3,2,1,0:T(8,128)S(1)}, u32[]{:S(2)}, u32[]{:S(2)}) collective-permute-start(f32[4,16,8,128]{3,2,1,0:T(8,128)S(1)} %get-tuple-element.64.own_e), channel_id=1, source_target_pairs={{0,1},{1,0},{2,3},{3,2},{4,5},{5,4},{6,7},{7,6},{8,9},{9,8},{10,11... | collective-permute-start | bytes 786440 | tf_op jit(solution)/shard_map/ppermute | solution.py:487
  27.7 11.1 %collective-permute-start.7 = (f32[4,16,8,128]{3,2,1,0:T(8,128)S(1)}, f32[4,16,8,128]{3,2,1,0:T(8,128)S(1)}, u32[]{:S(2)}, u32[]{:S(2)}) collective-permute-start(f32[4,16,8,128]{3,2,1,0:T(8,128)S(1)} %get-tuple-element.65.own_o), channel_id=1, source_target_pairs={{1,2},{2,1},{3,4},{4,3},{5,6},{6,5},{7,8},{8,7},{9,10},{10,9},{11,... | collective-permute-start | bytes 786440 | tf_op jit(solution)/shard_map/ppermute | solution.py:488
  39.3 13.8 %copy-start.3 = (f32[4,256]{1,0:T(4,128)S(1)}, f32[4,256]{1,0:T(4,128)}, u32[]{:S(2)}) copy-start(f32[4,256]{1,0:T(4,128)} %normals.1) | copy-start | bytes 12292
  39.3 19.8 %collective-permute-start.8 = (f32[4,16,1024]{2,1,0:T(8,128)S(1)}, f32[4,16,1024]{2,1,0:T(8,128)S(1)}, u32[]{:S(2)}, u32[]{:S(2)}) collective-permute-start(f32[4,16,1024]{2,1,0:T(8,128)S(1)} %get-tuple-element.66.q_e), channel_id=1, source_target_pairs={{0,16},{16,0},{32,48},{48,32},{64,80},{80,64},{96,112},{112,96},{1... | collective-permute-start | bytes 786440 | tf_op jit(solution)/shard_map/ppermute | solution.py:487
  46.4 12.6 %collective-permute-start.9 = (f32[4,16,1024]{2,1,0:T(8,128)S(1)}, f32[4,16,1024]{2,1,0:T(8,128)S(1)}, u32[]{:S(2)}, u32[]{:S(2)}) collective-permute-start(f32[4,16,1024]{2,1,0:T(8,128)S(1)} %get-tuple-element.67.q_o), channel_id=1, source_target_pairs={{16,32},{32,16},{48,64},{64,48},{80,96},{96,80},{17,33},{33,17},{4... | collective-permute-start | bytes 786440 | tf_op jit(solution)/shard_map/ppermute | solution.py:488
  47.7 11.8 %collective-permute-start.10 = (f32[4,16,8,128]{3,2,1,0:T(8,128)S(1)}, f32[4,16,8,128]{3,2,1,0:T(8,128)S(1)}, u32[]{:S(2)}, u32[]{:S(2)}) collective-permute-start(f32[4,16,8,128]{3,2,1,0:T(8,128)S(1)} %get-tuple-element.79.own_e), channel_id=1, source_target_pairs={{0,1},{1,0},{2,3},{3,2},{4,5},{5,4},{6,7},{7,6},{8,9},{9,8},{10,11... | collective-permute-start | bytes 786440 | tf_op jit(solution)/shard_map/ppermute | solution.py:487
  47.8 11.7 %collective-permute-start.11 = (f32[4,16,8,128]{3,2,1,0:T(8,128)S(1)}, f32[4,16,8,128]{3,2,1,0:T(8,128)S(1)}, u32[]{:S(2)}, u32[]{:S(2)}) collective-permute-start(f32[4,16,8,128]{3,2,1,0:T(8,128)S(1)} %get-tuple-element.80.own_o), channel_id=1, source_target_pairs={{1,2},{2,1},{3,4},{4,3},{5,6},{6,5},{7,8},{8,7},{9,10},{10,9},{11,... | collective-permute-start | bytes 786440 | tf_op jit(solution)/shard_map/ppermute | solution.py:488
  59.4 3.4 %copy-start.4 = (s32[256]{0:T(256)S(1)}, s32[256]{0:T(256)}, u32[]{:S(2)}) copy-start(s32[256]{0:T(256)} %blocks.1) | copy-start | bytes 3076
  59.4 3.4 %copy-start.5 = (s32[256,1]{0,1:T(1,128)S(1)}, s32[256,1]{0,1:T(1,128)}, u32[]{:S(2)}) copy-start(s32[256,1]{0,1:T(1,128)} %param.9) | copy-start | bytes 3076
